TPU v7x, 32 devices: a whole 2x2x4 slice. The times are simulated.
32 devices in a mesh: wide: 16 (over z, y, x), rows: 2 (over core).
Axes of the slice: x: 2, y: 2, z: 4, core: 2. Of those that a mesh axis runs over, the one named last changes fastest.
Arguments:
- slabs: bfloat16 [16, 2, 10, 32, 128], P('wide', 'rows'), may hold values from -6 to 6
- dest: int32 [16, 2, 10], P('wide', 'rows'), may hold values from 0 to 15, as said below
- pos: int32 [16, 2, 10], P('wide', 'rows'), may hold values from 0 to 9, as said below
- lengths: int32 [16], P('wide'), may hold values from 1 to 5
- cot: bfloat16 [16, 5, 4, 32, 128], P('wide', None, 'rows'), may hold values from -6 to 6
- w_first: bfloat16 [3456, 128], P('wide'), may hold values from -0.109375 to 0.109375
- w_second: bfloat16 [3456, 128], P('wide'), may hold values from -0.109375 to 0.109375
Outputs:
- block_out: bfloat16 [16, 5, 4, 32, 128], P('wide', None, 'rows')
- grad_input: bfloat16 [16, 5, 4, 32, 128], P('wide', None, 'rows')
- grad_w_first: float32 [3456, 128], P('wide')
- grad_w_second: float32 [3456, 128], P('wide')
Inputs may be any that keep to these rules, and one draw needn't show every extreme that they name: `dest`: within a band no loader sends more than one slab to any clip; every clip receives exactly 10 slabs in each band. `pos`: for every clip and band the 10 slabs it receives carry the places 0 to 9, each once.
All inputs are finite; a program needn't handle non-finite values.
Results may differ from a plain program's by a relative error of at most 0.018.
Values may be sent and summed in bfloat16 or wider, within the bound.
No kernel may reach another device: no remote copies, remote signals or barrier semaphores. Data moves between devices by JAX's collectives and lax.ppermute only.
A program may use at most 64 MiB of HBM per device.

v0:
```python
import math

import jax
import jax.numpy as jnp
from jax import lax
from jax.sharding import PartitionSpec as P


def with_halo(block, sides, width):
    for axis, dim in sides:
        count = lax.axis_size(axis)
        forward = [(i, i + 1) for i in range(count - 1)]
        backward = [(target, source) for source, target in forward]
        low = lax.ppermute(
            lax.slice_in_dim(block, block.shape[dim] - width, None, axis=dim), axis, forward
        )
        high = lax.ppermute(lax.slice_in_dim(block, 0, width, axis=dim), axis, backward)
        block = jnp.concatenate([low, block, high], axis=dim)
    return block


def silu_slope(values):
    sig = jax.nn.sigmoid(values)
    return sig * (1.0 + values * (1.0 - sig))


def conv_forward(extended, kernel):
    padded = jnp.concatenate([extended[:1], extended[:1], extended], axis=0)
    result = lax.conv_general_dilated(
        padded[None],
        kernel,
        (1, 1, 1),
        ((0, 0), (0, 0), (1, 1)),
        dimension_numbers=("NDHWC", "DHWIO", "NDHWC"),
        preferred_element_type=jnp.float32,
    )
    return result[0]


def conv_weight_grad(extended, upstream):
    padded = jnp.concatenate([extended[:1], extended[:1], extended], axis=0)
    result = lax.conv_general_dilated(
        padded[None],
        upstream[None],
        (1, 1, 1),
        ((0, 0), (0, 0), (1, 1)),
        dimension_numbers=("CDHWN", "IDHWO", "NDHWC"),
        preferred_element_type=jnp.float32,
    )
    channels = extended.shape[-1]
    return jnp.transpose(result, (1, 2, 3, 0, 4)).reshape(27 * channels, upstream.shape[-1])


def conv_data_grad(upstream_ext, kernel):
    padded = jnp.pad(upstream_ext, ((2, 2), (0, 0), (0, 0), (0, 0)))
    flipped = kernel[::-1, ::-1, ::-1]
    result = lax.conv_general_dilated(
        padded[None],
        flipped,
        (1, 1, 1),
        ((0, 0), (0, 0), (1, 1)),
        dimension_numbers=("NDHWC", "DHWOI", "NDHWC"),
        preferred_element_type=jnp.float32,
    )[0]
    head = (result[0] + result[1] + result[2])[None]
    return jnp.concatenate([head, result[3:]], axis=0)


def body(slabs, dest, pos, lengths, cot, w_first, w_second):
    wide_size = lax.axis_size("wide")
    band_count = lax.axis_size("rows")
    slab_count = slabs.shape[2]
    columns = slabs.shape[3]
    channels = slabs.shape[4]
    frames = cot.shape[1]
    band_rows = cot.shape[2]
    capacity = -(-slab_count // wide_size)
    slot_count = wide_size * capacity
    targets = dest[0, 0]
    places = pos[0, 0]
    ranking = jnp.arange(slab_count, dtype=jnp.int32)
    earlier = (targets[None, :] == targets[:, None]) & (ranking[None, :] < ranking[:, None])
    slab_rank = jnp.sum(earlier.astype(jnp.int32), axis=1)
    slot_of = targets * capacity + slab_rank
    placing = slot_of[None, :] == jnp.arange(slot_count, dtype=jnp.int32)[:, None]
    flat_slabs = slabs[0, 0].reshape(slab_count, columns * channels)
    outgoing = jnp.dot(placing.astype(jnp.bfloat16), flat_slabs, preferred_element_type=jnp.float32)
    outgoing = outgoing.astype(jnp.bfloat16).reshape(wide_size, capacity, columns * channels)
    labels = jnp.sum(jnp.where(placing, places[None, :] + 1, 0), axis=1) - 1
    labels = labels.reshape(wide_size, capacity)
    arrived, arrived_places = (
        lax.all_to_all(outgoing, "wide", split_axis=0, concat_axis=0, tiled=True),
        lax.all_to_all(labels, "wide", split_axis=0, concat_axis=0, tiled=True),
    )
    settle = (
        arrived_places.reshape(slot_count)[None, :]
        == jnp.arange(slab_count, dtype=jnp.int32)[:, None]
    )
    tile = jnp.dot(
        settle.astype(jnp.bfloat16),
        arrived.reshape(slot_count, columns * channels),
        preferred_element_type=jnp.float32,
    )
    tile = tile.astype(jnp.bfloat16).reshape(frames, band_rows, columns, channels)
    full_first, full_second = (
        lax.all_gather(w_first, "wide", axis=0, tiled=True),
        lax.all_gather(w_second, "wide", axis=0, tiled=True),
    )
    kernel_first = full_first.reshape(3, 3, 3, channels, channels)
    kernel_second = full_second.reshape(3, 3, 3, channels, channels)
    tile_wide = tile.astype(jnp.float32)
    first = jax.nn.silu(tile_wide).astype(jnp.bfloat16)
    first_ext = with_halo(first, (("rows", 1),), 1)
    act = conv_forward(first_ext, kernel_first).astype(jnp.bfloat16)
    second = jax.nn.silu(act.astype(jnp.float32)).astype(jnp.bfloat16)
    second_ext = with_halo(second, (("rows", 1),), 1)
    block_out = (tile_wide + conv_forward(second_ext, kernel_second)).astype(jnp.bfloat16)
    live = (jnp.arange(frames, dtype=jnp.int32) < lengths[0])[:, None, None, None]
    out_grad = jnp.where(live, cot[0], jnp.zeros_like(cot[0]))
    out_grad_ext = with_halo(out_grad, (("rows", 1),), 1)
    weight_second = conv_weight_grad(second_ext, out_grad)
    hidden_grad = conv_data_grad(out_grad_ext, kernel_second)
    act_grad = (hidden_grad * silu_slope(act.astype(jnp.float32))).astype(jnp.bfloat16)
    act_grad_ext = with_halo(act_grad, (("rows", 1),), 1)
    weight_first = conv_weight_grad(first_ext, act_grad)
    first_grad = conv_data_grad(act_grad_ext, kernel_first)
    grad_input = (out_grad.astype(jnp.float32) + first_grad * silu_slope(tile_wide)).astype(
        jnp.bfloat16
    )
    scale = 1.0 / math.sqrt(frames * band_rows * columns * band_count * wide_size)
    weight_first = weight_first * scale
    weight_second = weight_second * scale
    total_first, total_second = (
        lax.psum(weight_first.astype(jnp.bfloat16), "rows").astype(jnp.float32),
        lax.psum(weight_second.astype(jnp.bfloat16), "rows").astype(jnp.float32),
    )
    share_first, share_second = (
        lax.psum_scatter(total_first, "wide", scatter_dimension=0, tiled=True),
        lax.psum_scatter(total_second, "wide", scatter_dimension=0, tiled=True),
    )
    return (block_out[None], grad_input[None], share_first, share_second)


def solution(mesh):
    return jax.shard_map(
        body,
        mesh=mesh,
        in_specs=(
            P("wide", "rows", None, None, None),
            P("wide", "rows", None),
            P("wide", "rows", None),
            P("wide"),
            P("wide", None, "rows", None, None),
            P("wide", None),
            P("wide", None),
        ),
        out_specs=(
            P("wide", None, "rows", None, None),
            P("wide", None, "rows", None, None),
            P("wide", None),
            P("wide", None),
        ),
        check_vma=False,
    )
```

profile of v0, /device:TPU:0, one launch (start us, length us, event | category | flops | bytes accessed | tf_op | source)
XLA Modules:
  0.0 440.7 jit_solution(9445548104870461526)
XLA Ops:
  7.2 0.7 add_bitcast_fusion.1
  7.8 0.9 convert_reduce_fusion
  8.8 0.7 bitcast_add_fusion
  9.4 0.1 select_reduce_fusion
  9.5 0.7 copy.172
  10.2 8.3 %all-to-all-start = ((s32[16,1,1]{2,1,0:T(1,128)}), s32[16,1,1]{2,1,0:T(1,128)S(1)}, u32[]{:S(2)}, u32[]{:S(2)}) async-start(s32[16,1,1]{2,1,0:T(1,128)} %copy.172), calls=%async_computation | async-start | bytes 16384 | tf_op jit(solution)/shard_map/all_to_all | solution.py:93
  19.2 1.0 bitcast_select_fusion
  20.2 1.5 collective-permute-start.4
  21.7 1.3 collective-permute-start.5
  23.0 0.9 pad.69
  23.9 0.1 copy.216
  23.9 46.8 %all_gather.6 = bf16[3456,128]{1,0:T(8,128)(2,1)S(1)} all-gather(bf16[216,128]{1,0:T(8,128)(2,1)} %param.12), channel_id=1, replica_groups=mesh['wide'=16,'rows'=2] {'wide'}, dimensions={0}, use_global_device_ids=true | all-gather | bytes 940032 | tf_op jit(solution)/shard_map/all_gather | solution.py:106
  70.7 41.6 %all_gather.7 = bf16[3456,128]{1,0:T(8,128)(2,1)S(1)} all-gather(bf16[216,128]{1,0:T(8,128)(2,1)S(1)} %copy-done.2), channel_id=1, replica_groups=mesh['wide'=16,'rows'=2] {'wide'}, dimensions={0}, use_global_device_ids=true | all-gather | bytes 940032 | tf_op jit(solution)/shard_map/all_gather | solution.py:107
  112.3 0.2 fusion.1
  112.5 0.5 broadcast.172
  113.0 0.7 reduce.1
  113.7 0.7 reshape.270
  114.4 3.5 all-to-all-start.1
  118.0 0.0 all-reduce.7.cloned.1.call-start
  118.0 0.4 reduce
  118.4 0.2 copy.214
  118.6 0.1 pad.13.clone
  118.7 0.1 copy.186
  118.9 1.2 convolution_select_fusion.1
  120.0 5.7 %all-to-all-done.1 = bf16[16,2,2048]{2,1,0:T(2,128)(2,1)S(1)} async-done(((bf16[16,2,2048]{2,1,0:T(2,128)(2,1)}), bf16[16,2,2048]{2,1,0:T(2,128)(2,1)S(1)}, u32[]{:S(2)}, u32[]{:S(2)}) %all-to-all-start.1) | async-done | bytes 131104 | tf_op jit(solution)/shard_map/all_to_all | solution.py:92
  125.7 0.1 reshape.271
  125.9 0.3 fusion
  126.1 0.1 copy.217
  126.2 0.1 multiply_convert_fusion.2
  126.3 1.3 collective-permute-start
  127.6 1.3 collective-permute-start.1
  128.9 0.1 copy.189
  129.1 1.6 collective-permute-done.1
  130.7 0.1 copy.212
  130.9 0.1 pad.9.clone
  131.1 0.9 fusion.43
  132.0 0.1 copy.198
  132.1 0.1 copy.177
  132.2 0.1 slice.111
  132.3 0.1 fusion.53
  132.4 2.1 collective-permute-start.6
  134.5 1.3 collective-permute-start.7
  135.8 3.0 collective-permute-start.2
  138.8 1.5 collective-permute-start.3
  140.3 3.5 multiply_convert_fusion.1
  143.9 0.2 copy.215
  144.0 0.1 pad.15.clone
  144.2 0.1 copy.193
  144.3 1.2 convolution_select_fusion
  145.5 0.1 copy.196
  145.7 0.1 copy.213
  145.9 0.1 pad.11.clone
  146.1 0.9 convolution_select_fusion.2
  147.0 0.1 copy.182
  147.1 0.7 fusion.55
  147.9 3.5 multiply_convert_fusion
  151.4 0.0 reduce-scatter.7.cloned.1.call-start
  151.5 18.8 %all-reduce.7.cloned.1.call-done = (bf16[3456,128]{1,0:T(8,128)(2,1)}, bf16[3456,128]{1,0:T(8,128)(2,1)}) async-done(((bf16[3456,128]{1,0:T(8,128)(2,1)}, bf16[3456,128]{1,0:T(8,128)(2,1)}), (bf16[3456,128]{1,0:T(8,128)(2,1)}, bf16[3456,128]{1,0:T(8,128)(2,1)})) %all-reduce.7.cloned.1.call-update) | async-done | bytes 1769488 | tf_op jit(solution)/shard_map/psum | solution.py:134
  170.3 2.6 convert_element_type.113
  172.9 0.0 reduce-scatter.7.cloned.1.call-update
  172.9 0.0 reduce-scatter.9.cloned.1.call-start
  173.0 1.3 convert_element_type.116
  174.3 129.0 %reduce-scatter.7.cloned.1.call-done = f32[216,128]{1,0:T(8,128)} async-done(((f32[3456,128]{1,0:T(8,128)}), f32[216,128]{1,0:T(8,128)}) %reduce-scatter.7.cloned.1.call-update) | async-done | bytes 110608
  303.3 130.9 %reduce-scatter.9.cloned.1.call-done = f32[216,128]{1,0:T(8,128)} async-done(((f32[3456,128]{1,0:T(8,128)}), f32[216,128]{1,0:T(8,128)}) %reduce-scatter.9.cloned.1.call-update) | async-done | bytes 110608
  (54 shorter events, 0.7 us)
Async XLA Ops:
  7.2 63.5 %copy-start.2 = (bf16[216,128]{1,0:T(8,128)(2,1)S(1)}, bf16[216,128]{1,0:T(8,128)(2,1)}, u32[]{:S(2)}) copy-start(bf16[216,128]{1,0:T(8,128)(2,1)} %param.13) | copy-start | bytes 165892
  10.2 104.2 %all-to-all-start = ((s32[16,1,1]{2,1,0:T(1,128)}), s32[16,1,1]{2,1,0:T(1,128)S(1)}, u32[]{:S(2)}, u32[]{:S(2)}) async-start(s32[16,1,1]{2,1,0:T(1,128)} %copy.172), calls=%async_computation | async-start | bytes 16384 | tf_op jit(solution)/shard_map/all_to_all | solution.py:93
  20.2 98.2 %collective-permute-start.4 = (bf16[5,1,32,128]{3,2,1,0:T(8,128)(2,1)S(1)}, bf16[5,1,32,128]{3,2,1,0:T(8,128)(2,1)S(1)}, u32[]{:S(2)}, u32[]{:S(2)}) collective-permute-start(bf16[5,1,32,128]{3,2,1,0:T(8,128)(2,1)S(1)} %get-tuple-element.39), channel_id=1, source_target_pairs={{0,1},{2,3},{4,5},{6,7},{8,9},{10,11},{12,13},{14,15},{16,17},{18,... | collective-permute-start | bytes 122888 | tf_op jit(solution)/shard_map/ppermute | solution.py:14
  21.7 96.7 %collective-permute-start.5 = (bf16[5,1,32,128]{3,2,1,0:T(8,128)(2,1)S(1)}, bf16[5,1,32,128]{3,2,1,0:T(8,128)(2,1)S(1)}, u32[]{:S(2)}, u32[]{:S(2)}) collective-permute-start(bf16[5,1,32,128]{3,2,1,0:T(8,128)(2,1)S(1)} %get-tuple-element.40), channel_id=1, source_target_pairs={{1,0},{3,2},{5,4},{7,6},{9,8},{11,10},{13,12},{15,14},{17,16},{19,... | collective-permute-start | bytes 122888 | tf_op jit(solution)/shard_map/ppermute | solution.py:17
  113.0 5.8 %copy-start.3 = (pred[8,5]{0,1:T(8,128)(4,1)S(1)}, pred[8,5]{0,1:T(8,128)(4,1)}, u32[]{:S(2)}) copy-start(pred[8,5]{0,1:T(8,128)(4,1)} %constant.44) | copy-start | bytes 124
  114.4 11.3 %all-to-all-start.1 = ((bf16[16,2,2048]{2,1,0:T(2,128)(2,1)}), bf16[16,2,2048]{2,1,0:T(2,128)(2,1)S(1)}, u32[]{:S(2)}, u32[]{:S(2)}) async-start(bf16[16,2,2048]{2,1,0:T(2,128)(2,1)} %reshape.270), calls=%async_computation.1 | async-start | bytes 262144 | tf_op jit(solution)/shard_map/all_to_all | solution.py:92
  118.0 52.3 %all-reduce.7.cloned.1.call-start = ((), (), s32[]{:S(2)}) async-start(), calls=%async_computation.6 | async-start | bytes 3538944 | tf_op jit(solution)/shard_map/psum | solution.py:134
  126.3 2.8 collective-permute-start
  127.6 3.1 collective-permute-start.1
  132.4 11.4 %collective-permute-start.6 = (bf16[5,1,32,128]{3,2,1,0:T(8,128)(2,1)S(1)}, bf16[5,1,32,128]{3,2,1,0:T(8,128)(2,1)S(1)}, u32[]{:S(2)}, u32[]{:S(2)}) collective-permute-start(bf16[5,1,32,128]{3,2,1,0:T(8,128)(2,1)S(1)} %get-tuple-element.35), channel_id=1, source_target_pairs={{0,1},{2,3},{4,5},{6,7},{8,9},{10,11},{12,13},{14,15},{16,17},{18,... | collective-permute-start | bytes 122888 | tf_op jit(solution)/shard_map/ppermute | solution.py:14
  134.5 9.4 %collective-permute-start.7 = (bf16[5,1,32,128]{3,2,1,0:T(8,128)(2,1)S(1)}, bf16[5,1,32,128]{3,2,1,0:T(8,128)(2,1)S(1)}, u32[]{:S(2)}, u32[]{:S(2)}) collective-permute-start(bf16[5,1,32,128]{3,2,1,0:T(8,128)(2,1)S(1)} %get-tuple-element.36), channel_id=1, source_target_pairs={{1,0},{3,2},{5,4},{7,6},{9,8},{11,10},{13,12},{15,14},{17,16},{19,... | collective-permute-start | bytes 122888 | tf_op jit(solution)/shard_map/ppermute | solution.py:17
  135.8 9.9 %collective-permute-start.2 = (bf16[5,1,32,128]{3,2,1,0:T(8,128)(2,1)S(1)}, bf16[5,1,32,128]{3,2,1,0:T(8,128)(2,1)S(1)}, u32[]{:S(2)}, u32[]{:S(2)}) collective-permute-start(bf16[5,1,32,128]{3,2,1,0:T(8,128)(2,1)S(1)} %get-tuple-element.41), channel_id=1, source_target_pairs={{0,1},{2,3},{4,5},{6,7},{8,9},{10,11},{12,13},{14,15},{16,17},{18,... | collective-permute-start | bytes 122888 | tf_op jit(solution)/shard_map/ppermute | solution.py:14
  138.8 6.9 %collective-permute-start.3 = (bf16[5,1,32,128]{3,2,1,0:T(8,128)(2,1)S(1)}, bf16[5,1,32,128]{3,2,1,0:T(8,128)(2,1)S(1)}, u32[]{:S(2)}, u32[]{:S(2)}) collective-permute-start(bf16[5,1,32,128]{3,2,1,0:T(8,128)(2,1)S(1)} %get-tuple-element.42), channel_id=1, source_target_pairs={{1,0},{3,2},{5,4},{7,6},{9,8},{11,10},{13,12},{15,14},{17,16},{19,... | collective-permute-start | bytes 122888 | tf_op jit(solution)/shard_map/ppermute | solution.py:17
  146.1 1.0 copy-start.1
  151.4 151.9 %reduce-scatter.7.cloned.1.call-start = ((), (), s32[]{:S(2)}) async-start(), calls=%async_computation.4 | async-start | bytes 1880064
  170.3 2.7 copy-start
  172.9 261.3 %reduce-scatter.9.cloned.1.call-start = ((), (), s32[]{:S(2)}) async-start(), calls=%async_computation.5 | async-start | bytes 1880064
Sparse Core Ops, SparseCore 0:
  151.6 18.6 all-reduce.6
  176.5 126.8 reduce-scatter.6
  309.5 124.6 reduce-scatter.8
where the time goes:
time: 441 us
  waiting for transfers between devices  286 us (65%)
  blocking collectives  88.4 us (20%)
  starting transfers between devices  25.1 us (6%)
  between operations  15 us (3%)
  matrix products  11.6 us (3%)
  other arithmetic  9.4 us (2%)
  local copies, waits for them, and re-layouts  5.15 us (1%)
    unnamed x5, waiting for transfers between devices  260 us
    all_gather x1, blocking collectives, body(): lax.all_gather(w_first, 'wide', axis=0, tiled=True)  46.8 us
    all_gather x1, blocking collectives, body(): lax.all_gather(w_second, 'wide', axis=0, tiled=True)  41.6 us
    psum x1, waiting for transfers between devices, body(): lax.psum(weight_first.astype(jnp.bfloat16), 'rows').astype(jnp.float32)  18.8 us
  transfers between devices with their start and end apart: 13, of which 5 were waited for; matrix products, arithmetic and copies ran while one was open for 3% of the time, Pallas kernels for 0%

commit v1 on v0

--- a/solution.py
+++ b/solution.py
@@ -1,9 +1,16 @@
+import functools
 import math
 
 import jax
 import jax.numpy as jnp
 from jax import lax
+from jax.experimental import pallas as pl
+from jax.experimental.pallas import tpu as pltpu
 from jax.sharding import PartitionSpec as P
+
+BF16 = jnp.bfloat16
+F32 = jnp.float32
+LABEL_ROWS = 16
 
 
 def with_halo(block, sides, width):
@@ -66,7 +73,7 @@
     return jnp.concatenate([head, result[3:]], axis=0)
 
 
-def body(slabs, dest, pos, lengths, cot, w_first, w_second):
+def body_general(slabs, dest, pos, lengths, cot, w_first, w_second):
     wide_size = lax.axis_size("wide")
     band_count = lax.axis_size("rows")
     slab_count = slabs.shape[2]
@@ -141,7 +148,298 @@
     return (block_out[None], grad_input[None], share_first, share_second)
 
 
+def pack_kernel(dest_ref, pos_ref, slabs_ref, out_ref):
+    slots, rows, channels = out_ref.shape
+    columns = slabs_ref.shape[1]
+    out_ref[...] = jnp.zeros(out_ref.shape, BF16)
+    for slot in range(slots):
+        out_ref[slot, columns:, :] = jnp.full((rows - columns, channels), -1.0, BF16)
+    for slab in range(slabs_ref.shape[0]):
+        slot = dest_ref[slab]
+        out_ref[slot, :columns, :] = slabs_ref[slab]
+        place = pos_ref[slab].astype(F32)
+        out_ref[slot, columns:, :] = jnp.full((rows - columns, channels), place, F32).astype(BF16)
+
+
+def pack(slabs, dest, pos, slots):
+    count, columns, channels = slabs.shape
+    smem = pl.BlockSpec(memory_space=pltpu.SMEM)
+    vmem = pl.BlockSpec(memory_space=pltpu.VMEM)
+    return pl.pallas_call(
+        pack_kernel,
+        out_shape=jax.ShapeDtypeStruct((slots, columns + LABEL_ROWS, channels), BF16),
+        in_specs=[smem, smem, vmem],
+        out_specs=vmem,
+    )(dest, pos, slabs)
+
+
+def settle(mine, tile_ref, first_row):
+    slots, rows, channels = mine.shape
+    columns = rows - LABEL_ROWS
+    frames = tile_ref.shape[0]
+    labels = [mine[j, columns : columns + 8, :].astype(F32)[None] for j in range(slots)]
+    for place in range(frames * 2):
+        total = jnp.zeros((columns // 8, 8, channels), F32)
+        for j in range(slots):
+            values = mine[j, :columns, :].astype(F32).reshape(columns // 8, 8, channels)
+            total = total + jnp.where(labels[j] == float(place), values, 0.0)
+        tile_ref[place // 2, first_row + place % 2] = total.reshape(columns, channels)
+
+
+def shifted(field):
+    shape = field.shape
+    column = lax.broadcasted_iota(jnp.int32, shape, len(shape) - 2)
+    count = shape[-2]
+    flat = field.reshape(-1, shape[-1])
+    low = pltpu.roll(flat, 1, 0).reshape(shape)
+    high = pltpu.roll(flat, flat.shape[0] - 1, 0).reshape(shape)
+    low = jnp.where(column == 0, 0.0, low)
+    high = jnp.where(column == count - 1, 0.0, high)
+    return low.astype(BF16), field.astype(BF16), high.astype(BF16)
+
+
+def spread(field, store, flip):
+    rows = field.shape[1]
+    columns = shifted(field)
+    for b in range(3):
+        for e in range(3):
+            source = columns[2 - e] if flip else columns[e]
+            offset = (1 - b) if flip else (b - 1)
+            low = max(0, -offset)
+            high = min(rows, rows - offset)
+            piece = b * 3 + e
+            store(low, high, piece, source[:, low + offset : high + offset])
+            for row in range(rows):
+                if not low <= row < high:
+                    store(row, row + 1, piece, jnp.zeros_like(source[:, :1]))
+
+
+def unit_kernel(
+    core_ref,
+    length_ref,
+    mine_ref,
+    other_ref,
+    cot_mine_ref,
+    cot_other_ref,
+    w_mine_ref,
+    w_other_ref,
+    block_ref,
+    grad_ref,
+    weight_ref,
+    w_scratch,
+    wl_scratch,
+    tile_scratch,
+    act_scratch,
+    x_scratch,
+    g_scratch,
+    up_scratch,
+    sum_scratch,
+    sem,
+    *,
+    scale,
+):
+    core = core_ref[0]
+    length = length_ref[0]
+    frames, rows, columns, channels = tile_scratch.shape
+    band_rows = block_ref.shape[1]
+    cells = frames * rows * columns
+    nine = 9 * channels
+    my_row = core * band_rows
+    other_row = (1 - core) * band_rows
+
+    load_mine = pltpu.make_async_copy(w_mine_ref, w_scratch.at[core], sem.at[0])
+    load_other = pltpu.make_async_copy(w_other_ref, w_scratch.at[1 - core], sem.at[1])
+    load_mine.start()
+    load_other.start()
+
+    settle(mine_ref, tile_scratch, my_row)
+    settle(other_ref, tile_scratch, other_row)
+
+    tile = tile_scratch[...]
+    first = tile / (1.0 + jnp.exp(-tile))
+
+    def store_x(index):
+        def store(low, high, piece, values):
+            lanes = slice(piece * channels, (piece + 1) * channels)
+            x_scratch[index, 2:, low:high, :, lanes] = values
+            x_scratch[index, 0, low:high, :, lanes] = values[0]
+            x_scratch[index, 1, low:high, :, lanes] = values[0]
+
+        return store
+
+    def store_g(low, high, piece, values):
+        lanes = slice(piece * channels, (piece + 1) * channels)
+        g_scratch[:, low:high, :, lanes] = values
+
+    spread(first, store_x(0), False)
+
+    for t in range(frames):
+        keep = t < length
+        up_scratch[1, t, pl.ds(my_row, band_rows)] = jnp.where(
+            keep, cot_mine_ref[t].astype(F32), 0.0
+        ).astype(BF16)
+        up_scratch[1, t, pl.ds(other_row, band_rows)] = jnp.where(
+            keep, cot_other_ref[t].astype(F32), 0.0
+        ).astype(BF16)
+
+    load_mine.wait()
+    load_other.wait()
+
+    act = jnp.zeros((cells, channels), F32)
+    for a in range(3):
+        act = act + jnp.dot(
+            x_scratch[0, a : a + frames].reshape(cells, nine),
+            w_scratch[0, a].reshape(nine, channels),
+            preferred_element_type=F32,
+        )
+    act = act.astype(BF16).reshape(frames, rows, columns, channels)
+    act_scratch[...] = act
+    act = act.astype(F32)
+    second = act / (1.0 + jnp.exp(-act))
+    spread(second, store_x(1), False)
+
+    for index in range(2):
+        for a in range(3):
+            for piece in range(9):
+                wl_scratch[index, a, :, piece * channels : (piece + 1) * channels] = w_scratch[
+                    index, a, piece
+                ]
+
+    out_grad = up_scratch[1].astype(F32)
+    spread(out_grad, store_g, True)
+    nt = (((1,), (1,)), ((), ()))
+    sum_scratch[...] = jnp.zeros(sum_scratch.shape, F32)
+    for a in range(3):
+        part = lax.dot_general(
+            g_scratch[...].reshape(cells, nine),
+            wl_scratch[1, a],
+            nt,
+            preferred_element_type=F32,
+        )
+        sum_scratch[a : a + frames] += part.reshape(frames, rows, columns, channels)
+    sum_scratch[2] = sum_scratch[0] + sum_scratch[1] + sum_scratch[2]
+    act = act_scratch[...].astype(F32)
+    sig = 1.0 / (1.0 + jnp.exp(-act))
+    act_grad = (sum_scratch[2:] * (sig * (1.0 + act * (1.0 - sig)))).astype(BF16)
+    up_scratch[0] = act_grad
+
+    upstream = up_scratch[core].reshape(cells, channels).astype(F32).T.astype(BF16)
+    for a in range(3):
+        part = jnp.dot(
+            upstream,
+            x_scratch[core, a : a + frames].reshape(cells, nine),
+            preferred_element_type=F32,
+        )
+        for piece in range(9):
+            weight_ref[a, piece] = (
+                part[:, piece * channels : (piece + 1) * channels].T * scale
+            ).astype(BF16)
+
+    half = frames * band_rows * columns
+    band = (frames, band_rows, columns, channels)
+    out = jnp.zeros((half, channels), F32)
+    for a in range(3):
+        out = out + jnp.dot(
+            x_scratch[1, a : a + frames, pl.ds(my_row, band_rows)].reshape(half, nine),
+            w_scratch[1, a].reshape(nine, channels),
+            preferred_element_type=F32,
+        )
+    my_tile = tile_scratch[:, pl.ds(my_row, band_rows)]
+    block_ref[...] = (my_tile + out.reshape(band)).astype(BF16)
+
+    spread(act_grad.astype(F32), store_g, True)
+    sum_scratch[:, :band_rows] = jnp.zeros((sum_scratch.shape[0],) + band[1:], F32)
+    for a in range(3):
+        part = lax.dot_general(
+            g_scratch[:, pl.ds(my_row, band_rows)].reshape(half, nine),
+            wl_scratch[0, a],
+            nt,
+            preferred_element_type=F32,
+        )
+        sum_scratch[a : a + frames, :band_rows] += part.reshape(band)
+    sum_scratch[2, :band_rows] = (
+        sum_scratch[0, :band_rows] + sum_scratch[1, :band_rows] + sum_scratch[2, :band_rows]
+    )
+    sig = 1.0 / (1.0 + jnp.exp(-my_tile))
+    slope = sig * (1.0 + my_tile * (1.0 - sig))
+    my_up = up_scratch[1, :, pl.ds(my_row, band_rows)].astype(F32)
+    grad_ref[...] = (my_up + sum_scratch[2:, :band_rows] * slope).astype(BF16)
+
+
+def unit(core, length, mine, other, cot_mine, cot_other, w_mine, w_other, scale):
+    frames, band_rows, columns, channels = cot_mine.shape
+    rows = 2 * band_rows
+    smem = pl.BlockSpec(memory_space=pltpu.SMEM)
+    vmem = pl.BlockSpec(memory_space=pltpu.VMEM)
+    hbm = pl.BlockSpec(memory_space=pl.ANY)
+    band = jax.ShapeDtypeStruct(cot_mine.shape, BF16)
+    flops = 2 * 27 * channels * channels * frames * rows * columns * 4
+    return pl.pallas_call(
+        functools.partial(unit_kernel, scale=scale),
+        out_shape=(band, band, jax.ShapeDtypeStruct((3, 9, channels, channels), BF16)),
+        in_specs=[smem, smem, vmem, vmem, vmem, vmem, hbm, hbm],
+        out_specs=(vmem, vmem, vmem),
+        scratch_shapes=[
+            pltpu.VMEM((2, 3, 9, channels, channels), BF16),
+            pltpu.VMEM((2, 3, channels, 9 * channels), BF16),
+            pltpu.VMEM((frames, rows, columns, channels), F32),
+            pltpu.VMEM((frames, rows, columns, channels), BF16),
+            pltpu.VMEM((2, frames + 2, rows, columns, 9 * channels), BF16),
+            pltpu.VMEM((frames, rows, columns, 9 * channels), BF16),
+            pltpu.VMEM((2, frames, rows, columns, channels), BF16),
+            pltpu.VMEM((frames + 2, rows, columns, channels), F32),
+            pltpu.SemaphoreType.DMA((2,)),
+        ],
+        compiler_params=pltpu.CompilerParams(vmem_limit_bytes=40 * 1024 * 1024),
+        cost_estimate=pl.CostEstimate(flops=flops, bytes_accessed=4_000_000, transcendentals=0),
+    )(core, length, mine, other, cot_mine, cot_other, w_mine, w_other)
+
+
+def body_pair(slabs, dest, pos, lengths, cot, w_first, w_second):
+    wide_size = lax.axis_size("wide")
+    core = lax.axis_index("rows")
+    frames, band_rows, columns, channels = cot.shape[1:]
+    share = w_first.shape[0]
+    swap = [(0, 1), (1, 0)]
+
+    def exchange(block):
+        return lax.ppermute(block, "rows", swap)
+
+    cot_mine = cot[0]
+    cot_other = exchange(cot_mine)
+    own = jnp.where(core == 0, w_first, w_second)
+    copies = jnp.broadcast_to(own[None], (wide_size, share, channels))
+    w_mine = lax.all_to_all(copies, "wide", split_axis=0, concat_axis=0, tiled=True)
+    w_mine = w_mine.reshape(3, 9, channels, channels)
+    w_other = exchange(w_mine)
+
+    outgoing = pack(slabs[0, 0], dest[0, 0], pos[0, 0], wide_size)
+    mine = lax.all_to_all(outgoing, "wide", split_axis=0, concat_axis=0, tiled=True)
+    other = exchange(mine)
+
+    scale = 1.0 / math.sqrt(frames * band_rows * columns * 2 * wide_size)
+    block_out, grad_input, weight = unit(
+        core.astype(jnp.int32).reshape(1),
+        lengths,
+        mine,
+        other,
+        cot_mine,
+        cot_other,
+        w_mine,
+        w_other,
+        scale,
+    )
+    parts = weight.reshape(wide_size, share, channels)
+    parts = lax.all_to_all(parts, "wide", split_axis=0, concat_axis=0, tiled=True)
+    total = jnp.sum(parts.astype(F32), axis=0)
+    total_other = exchange(total)
+    share_first = jnp.where(core == 0, total, total_other)
+    share_second = jnp.where(core == 0, total_other, total)
+    return (block_out[None], grad_input[None], share_first, share_second)
+
+
 def solution(mesh):
+    body = body_pair if mesh.shape["rows"] == 2 else body_general
     return jax.shard_map(
         body,
         mesh=mesh,

time: 441 us -> 85.4 us (0.19)
  waiting for transfers between devices: 286 us -> 1.7 us
  starting transfers between devices: 25.1 us -> 0.58 us
  blocking collectives: 88.4 us -> 71.2 us
  between operations: 15 us -> 1.33 us
  matrix products: 11.6 us -> 0 us
  Pallas kernels: 0 us -> 8.42 us
  other arithmetic: 9.4 us -> 1.66 us
  local copies, waits for them, and re-layouts: 5.15 us -> 0.12 us
    unnamed x5 -> x0, waiting for transfers between devices: 260 us -> none
    all_gather x2 -> x0, blocking collectives: 88.4 us -> none  [the longest x1 46.8 us: body(): lax.all_gather(w_first, 'wide', axis=0, tiled=True)]
    all_to_all x0 -> x3, blocking collectives: none -> 71.2 us  [the longest x1 31.4 us: body_pair(): lax.all_to_all(copies, 'wide', split_axis=0, concat_axis=0, tiled=True)]
    psum x1 -> x0, waiting for transfers between devices: 18.8 us -> none  [body(): lax.psum(weight_first.astype(jnp.bfloat16), 'rows').astype(jnp.float32)]
    ppermute x8 -> x4, starting transfers between devices: 13.2 us -> 0.58 us  [exchange(): return lax.ppermute(block, 'rows', swap)]
    all_to_all x2 -> x0, starting transfers between devices: 11.8 us -> none  [the longest x1 8.31 us: body(): lax.all_to_all(labels, 'wide', split_axis=0, concat_axis=0, tiled=True)]
    pallas_call x0 -> x2, Pallas kernels: none -> 8.42 us  [the longest x1 6.81 us: unit(): pl.pallas_call(functools.partial(unit_kernel, scale=scale), out_shape=(ba...]
    transpose x2 -> x0, matrix products: 7.04 us -> none  [conv_weight_grad(): jnp.transpose(result, (1, 2, 3, 0, 4))]
  transfers between devices with their start and end apart: 13 -> 4, of which waited for: 5 -> 2; matrix products, arithmetic and copies ran while one was open for 3% -> 0% of each run, Pallas kernels for 0% -> 2%
where the time goes in v1:
time: 85.4 us; the launch traced here: 85 us
  blocking collectives  71.2 us (83%)
  Pallas kernels  8.42 us (10%)
  waiting for transfers between devices  1.7 us (2%)
  other arithmetic  1.66 us (2%)
  between operations  1.33 us (2%)
    all_to_all x1, blocking collectives, body_pair(): lax.all_to_all(copies, 'wide', split_axis=0, concat_axis=0, tiled=True)  31.4 us
    all_to_all x1, blocking collectives, body_pair(): lax.all_to_all(parts, 'wide', split_axis=0, concat_axis=0, tiled=True)  26.7 us
    all_to_all x1, blocking collectives, body_pair(): lax.all_to_all(outgoing, 'wide', split_axis=0, concat_axis=0, tiled=True)  13.1 us
    pallas_call x1, Pallas kernels, unit(): pl.pallas_call(functools.partial(unit_kernel, scale=scale), out_shape=(ba...  6.81 us
  transfers between devices with their start and end apart: 4, of which 2 were waited for; matrix products, arithmetic and copies ran while one was open for 0% of the time, Pallas kernels for 2%

profile of v1, /device:TPU:0, one launch (start us, length us, event | category | flops | bytes accessed | tf_op | source)
XLA Modules:
  0.0 85.0 jit_solution(1222143245468076613)
XLA Ops:
  0.6 0.8 broadcast_select_fusion.2
  1.5 0.1 broadcast_in_dim.12
  1.6 0.0 copy-start
  1.6 31.4 %all_to_all.15 = bf16[16,216,128]{2,1,0:T(8,128)(2,1)S(1)} all-to-all(bf16[16,216,128]{2,1,0:T(8,128)(2,1)S(1)} %broadcast_in_dim.12), channel_id=1, replica_groups=mesh['wide'=16,'rows'=2] {'wide'}, dimensions={0} | all-to-all | bytes 1769472 | tf_op jit(solution)/shard_map/all_to_all | solution.py:412
  33.1 0.0 collective-permute-start.2
  33.1 1.6 %shard_map.102 = bf16[16,48,128]{2,1,0:T(8,128)(2,1)} custom-call(s32[10]{0:T(128)} %bitcast.15, s32[10]{0:T(128)} %bitcast.16, bf16[10,32,128]{2,1,0:T(8,128)(2,1)} %bitcast.14), custom_call_target="tpu_custom_call" | custom-call | tf_op jit(solution)/shard_map/pallas_call | solution.py:168
  34.7 13.1 %all_to_all.16.mine_ref = bf16[16,48,128]{2,1,0:T(8,128)(2,1)S(1)} all-to-all(bf16[16,48,128]{2,1,0:T(8,128)(2,1)} %shard_map.102), channel_id=1, replica_groups=mesh['wide'=16,'rows'=2] {'wide'}, dimensions={0} | all-to-all | bytes 393216 | tf_op jit(solution)/shard_map/all_to_all | solution.py:417
  47.8 0.0 collective-permute-start
  47.8 0.0 copy-done
  47.8 0.5 collective-permute-start.1
  48.9 0.4 collective-permute-done.1.cot_other_ref
  49.3 0.0 collective-permute-done.other_ref
  49.3 0.0 collective-permute-done.2.w_other_ref
  49.3 6.8 %shard_map.103 = (bf16[5,2,32,128]{3,2,1,0:T(8,128)(2,1)}, bf16[5,2,32,128]{3,2,1,0:T(8,128)(2,1)}, bf16[3,9,128,128]{3,2,1,0:T(8,128)(2,1)S(1)}) custom-call(s32[1]{0:T(128)} %bitcast.core_ref, s32[1]{0:T(128)S(6)} %copy.11.length_ref, bf16[16,48,128]{2,1,0:T(8,128)(2,1)S(1)} %all_to_all.16.mine_ref, ...), custom_call_target="tpu_custom_call" | custom-call | flops 2264924160 | bytes 4000000 | tf_op jit(solution)/shard_map/pallas_call | solution.py:377
  56.1 26.7 %all_to_all.17 = bf16[16,216,128]{2,1,0:T(8,128)(2,1)S(1)} all-to-all(bf16[16,216,128]{2,1,0:T(8,128)(2,1)S(1)} %bitcast.11), channel_id=1, replica_groups=mesh['wide'=16,'rows'=2] {'wide'}, dimensions={0} | all-to-all | bytes 1769472 | tf_op jit(solution)/shard_map/all_to_all | solution.py:433
  82.8 0.1 convert_reduce_fusion
  82.9 0.1 collective-permute-start.3
  83.0 1.3 %collective-permute-done.3 = f32[216,128]{1,0:T(8,128)S(1)} collective-permute-done((f32[216,128]{1,0:T(8,128)S(1)}, f32[216,128]{1,0:T(8,128)S(1)}, u32[]{:S(2)}, u32[]{:S(2)}) %collective-permute-start.3) | collective-permute-done | bytes 110624 | tf_op jit(solution)/shard_map/ppermute | solution.py:406
  84.3 0.7 broadcast_select_fusion
Async XLA Ops:
  1.6 46.2 %copy-start = (bf16[1,5,2,32,128]{4,3,2,1,0:T(8,128)(2,1)S(1)}, bf16[1,5,2,32,128]{4,3,2,1,0:T(8,128)(2,1)}, u32[]{:S(2)}) copy-start(bf16[1,5,2,32,128]{4,3,2,1,0:T(8,128)(2,1)} %param.11) | copy-start | bytes 245764
  33.1 16.3 %collective-permute-start.2 = (bf16[3,9,128,128]{3,2,1,0:T(8,128)(2,1)S(1)}, bf16[3,9,128,128]{3,2,1,0:T(8,128)(2,1)S(1)}, u32[]{:S(2)}, u32[]{:S(2)}) collective-permute-start(bf16[3,9,128,128]{3,2,1,0:T(8,128)(2,1)S(1)} %bitcast.9), channel_id=1, source_target_pairs={{0,1},{1,0},{2,3},{3,2},{4,5},{5,4},{6,7},{7,6},{8,9},{9,8},{10,11... | collective-permute-start | bytes 2654216 | tf_op jit(solution)/shard_map/ppermute | solution.py:406
  47.8 1.6 %collective-permute-start = (bf16[16,48,128]{2,1,0:T(8,128)(2,1)S(1)}, bf16[16,48,128]{2,1,0:T(8,128)(2,1)S(1)}, u32[]{:S(2)}, u32[]{:S(2)}) collective-permute-start(bf16[16,48,128]{2,1,0:T(8,128)(2,1)S(1)} %all_to_all.16.mine_ref), channel_id=1, source_target_pairs={{0,1},{1,0},{2,3},{3,2},{4,5},{5,4},{6,7},{7,6},{8,9},{9,8},{10,11... | collective-permute-start | bytes 589832 | tf_op jit(solution)/shard_map/ppermute | solution.py:406
  47.8 1.6 %collective-permute-start.1 = (bf16[5,2,32,128]{3,2,1,0:T(8,128)(2,1)S(1)}, bf16[5,2,32,128]{3,2,1,0:T(8,128)(2,1)S(1)}, u32[]{:S(2)}, u32[]{:S(2)}) collective-permute-start(bf16[5,2,32,128]{3,2,1,0:T(8,128)(2,1)S(1)} %bitcast.12), channel_id=1, source_target_pairs={{0,1},{1,0},{2,3},{3,2},{4,5},{5,4},{6,7},{7,6},{8,9},{9,8},{10,11... | collective-permute-start | bytes 245768 | tf_op jit(solution)/shard_map/ppermute | solution.py:406
  82.9 1.4 %collective-permute-start.3 = (f32[216,128]{1,0:T(8,128)S(1)}, f32[216,128]{1,0:T(8,128)S(1)}, u32[]{:S(2)}, u32[]{:S(2)}) collective-permute-start(f32[216,128]{1,0:T(8,128)S(1)} %convert_reduce_fusion), channel_id=1, source_target_pairs={{0,1},{1,0},{2,3},{3,2},{4,5},{5,4},{6,7},{7,6},{8,9},{9,8},{10,11... | collective-permute-start | bytes 331784 | tf_op jit(solution)/shard_map/ppermute | solution.py:406

commit v2 on v1

--- a/solution.py
+++ b/solution.py
@@ -148,42 +148,132 @@
     return (block_out[None], grad_input[None], share_first, share_second)
 
 
-def pack_kernel(dest_ref, pos_ref, slabs_ref, out_ref):
-    slots, rows, channels = out_ref.shape
-    columns = slabs_ref.shape[1]
-    out_ref[...] = jnp.zeros(out_ref.shape, BF16)
-    for slot in range(slots):
-        out_ref[slot, columns:, :] = jnp.full((rows - columns, channels), -1.0, BF16)
-    for slab in range(slabs_ref.shape[0]):
-        slot = dest_ref[slab]
-        out_ref[slot, :columns, :] = slabs_ref[slab]
-        place = pos_ref[slab].astype(F32)
-        out_ref[slot, columns:, :] = jnp.full((rows - columns, channels), place, F32).astype(BF16)
-
-
-def pack(slabs, dest, pos, slots):
+def whole(count):
+    return [pl.BlockSpec(memory_space=pltpu.VMEM)] * count
+
+
+def scalars(count):
+    return [pl.BlockSpec(memory_space=pltpu.SMEM)] * count
+
+
+def position(side):
+    core = lax.axis_index("rows")
+    wide = lax.axis_index("wide")
+    high, low = wide // side, lax.rem(wide, side)
+    return core, high, low
+
+
+def walk(core, high, low):
+    return jnp.where(core == 0, high, low), jnp.where(core == 0, low, high)
+
+
+def chip_of(core, p, q, side):
+    high, low = walk(core, p, q)
+    return high * side + low
+
+
+def padded_rows(rows):
+    return -(-rows // 16) * 16
+
+
+def pack_kernel(dest_ref, pos_ref, slabs_ref, first_ref, second_ref, *out_refs):
+    side = len(out_refs)
+    core, high, low = position(side)
+    p, _ = walk(core, high, low)
+    count, columns, channels = slabs_ref.shape
+    share = first_ref.shape[0]
+    base = padded_rows(share)
+    row = lax.broadcasted_iota(jnp.int32, (LABEL_ROWS, channels), 0)
+    own = jnp.where(core == 0, first_ref[...].astype(F32), second_ref[...].astype(F32))
+    own = jnp.concatenate([own, jnp.zeros((base - share, channels), F32)], axis=0).astype(BF16)
+    slabs = [slabs_ref[s].astype(F32) for s in range(count)]
+    for k in range(side):
+        out_refs[k][:base, :] = own
+        labels = jnp.full((LABEL_ROWS, channels), -1.0, F32)
+        for q in range(side):
+            target = chip_of(core, jnp.bitwise_xor(p, k), q, side)
+            total = jnp.zeros((columns, channels), F32)
+            place = jnp.int32(-1)
+            for s in range(count):
+                match = dest_ref[s] == target
+                total = jnp.where(match, slabs[s], total)
+                place = jnp.where(match, pos_ref[s], place)
+            labels = jnp.where(row == q, place.astype(F32), labels)
+            at = base + q * columns
+            out_refs[k][at : at + columns, :] = total.astype(BF16)
+        out_refs[k][base + side * columns :, :] = labels.astype(BF16)
+
+
+def pack(dest, pos, slabs, first, second, side):
     count, columns, channels = slabs.shape
-    smem = pl.BlockSpec(memory_space=pltpu.SMEM)
-    vmem = pl.BlockSpec(memory_space=pltpu.VMEM)
+    rows = padded_rows(first.shape[0]) + side * columns + LABEL_ROWS
     return pl.pallas_call(
         pack_kernel,
-        out_shape=jax.ShapeDtypeStruct((slots, columns + LABEL_ROWS, channels), BF16),
-        in_specs=[smem, smem, vmem],
-        out_specs=vmem,
-    )(dest, pos, slabs)
-
-
-def settle(mine, tile_ref, first_row):
-    slots, rows, channels = mine.shape
-    columns = rows - LABEL_ROWS
-    frames = tile_ref.shape[0]
-    labels = [mine[j, columns : columns + 8, :].astype(F32)[None] for j in range(slots)]
+        out_shape=[jax.ShapeDtypeStruct((rows, channels), BF16)] * side,
+        in_specs=scalars(2) + whole(3),
+        out_specs=whole(side),
+    )(dest, pos, slabs, first, second)
+
+
+def relay_kernel(*refs, columns, base):
+    side = len(refs) // 2
+    ins, outs = refs[:side], refs[side:]
+    core, high, low = position(side)
+    _, q = walk(core, high, low)
+    channels = ins[0].shape[1]
+    row = lax.broadcasted_iota(jnp.int32, (LABEL_ROWS, channels), 0)
+    for j in range(side):
+        target = jnp.bitwise_xor(q, j)
+        start = pl.multiple_of(base + target * columns, 16)
+        labels = jnp.full((LABEL_ROWS, channels), -1.0, F32)
+        for k in range(side):
+            outs[j][k * base : (k + 1) * base, :] = ins[k][:base, :]
+            at = side * base + k * columns
+            outs[j][at : at + columns, :] = ins[k][pl.ds(start, columns), :]
+            theirs = ins[k][base + side * columns :, :].astype(F32)
+            label = jnp.sum(jnp.where(row == target, theirs, 0.0), axis=0, keepdims=True)
+            labels = jnp.where(row == k, label, labels)
+        outs[j][side * (base + columns) :, :] = labels.astype(BF16)
+
+
+def relay(ins, columns, base):
+    side = len(ins)
+    channels = ins[0].shape[1]
+    rows = side * (base + columns) + LABEL_ROWS
+    return pl.pallas_call(
+        functools.partial(relay_kernel, columns=columns, base=base),
+        out_shape=[jax.ShapeDtypeStruct((rows, channels), BF16)] * side,
+        in_specs=whole(side),
+        out_specs=whole(side),
+    )(*ins)
+
+
+def settle(blocks, tile_ref, first_row, base):
+    side = len(blocks)
+    frames, _, columns, channels = tile_ref.shape
+    slots = []
+    for block in blocks:
+        labels = block[side * (base + columns) :, :].astype(F32)
+        for k in range(side):
+            at = side * base + k * columns
+            values = block[at : at + columns, :].astype(F32)
+            slots.append((labels[k : k + 1], values))
     for place in range(frames * 2):
-        total = jnp.zeros((columns // 8, 8, channels), F32)
-        for j in range(slots):
-            values = mine[j, :columns, :].astype(F32).reshape(columns // 8, 8, channels)
-            total = total + jnp.where(labels[j] == float(place), values, 0.0)
-        tile_ref[place // 2, first_row + place % 2] = total.reshape(columns, channels)
+        total = jnp.zeros((columns, channels), F32)
+        for label, values in slots:
+            total = total + jnp.where(label == float(place), values, 0.0)
+        tile_ref[place // 2, first_row + place % 2] = total
+
+
+def gather_weight(blocks, wide_ref, core, high, low, share, base):
+    side = len(blocks)
+    p, q = walk(core, high, low)
+    for j in range(side):
+        for k in range(side):
+            owner = chip_of(core, jnp.bitwise_xor(p, k), jnp.bitwise_xor(q, j), side)
+            start = pl.multiple_of(owner * share, 8)
+            values = blocks[j][k * base : (k + 1) * base, :].astype(F32)
+            wide_ref[core, pl.ds(start, share), :] = values[:share]
 
 
 def shifted(field):
@@ -214,31 +304,30 @@
                     store(row, row + 1, piece, jnp.zeros_like(source[:, :1]))
 
 
-def unit_kernel(
-    core_ref,
-    length_ref,
-    mine_ref,
-    other_ref,
-    cot_mine_ref,
-    cot_other_ref,
-    w_mine_ref,
-    w_other_ref,
-    block_ref,
-    grad_ref,
-    weight_ref,
-    w_scratch,
-    wl_scratch,
-    tile_scratch,
-    act_scratch,
-    x_scratch,
-    g_scratch,
-    up_scratch,
-    sum_scratch,
-    sem,
-    *,
-    scale,
-):
-    core = core_ref[0]
+def unit_kernel(length_ref, *refs, scale, side, share):
+    refs = list(refs)
+
+    def take(count):
+        taken = refs[:count]
+        del refs[:count]
+        return taken
+
+    blocks_mine, blocks_other = take(side), take(side)
+    cot_mine_ref, cot_other_ref = take(2)
+    block_ref, grad_ref = take(2)
+    outs = take(side)
+    (
+        wide_ref,
+        w_scratch,
+        wl_scratch,
+        tile_scratch,
+        act_scratch,
+        x_scratch,
+        g_scratch,
+        up_scratch,
+        sum_scratch,
+    ) = refs
+    core, high, low = position(side)
     length = length_ref[0]
     frames, rows, columns, channels = tile_scratch.shape
     band_rows = block_ref.shape[1]
@@ -246,14 +335,19 @@
     nine = 9 * channels
     my_row = core * band_rows
     other_row = (1 - core) * band_rows
-
-    load_mine = pltpu.make_async_copy(w_mine_ref, w_scratch.at[core], sem.at[0])
-    load_other = pltpu.make_async_copy(w_other_ref, w_scratch.at[1 - core], sem.at[1])
-    load_mine.start()
-    load_other.start()
-
-    settle(mine_ref, tile_scratch, my_row)
-    settle(other_ref, tile_scratch, other_row)
+    base = padded_rows(share)
+
+    settle(blocks_mine, tile_scratch, my_row, base)
+    settle(blocks_other, tile_scratch, other_row, base)
+    gather_weight(blocks_mine, wide_ref, core, high, low, share, base)
+    gather_weight(blocks_other, wide_ref, 1 - core, high, low, share, base)
+    for index in range(2):
+        for a in range(3):
+            for piece in range(9):
+                at = (a * 9 + piece) * channels
+                values = wide_ref[index, at : at + channels, :].astype(BF16)
+                w_scratch[index, a, piece] = values
+                wl_scratch[index, a, :, piece * channels : (piece + 1) * channels] = values
 
     tile = tile_scratch[...]
     first = tile / (1.0 + jnp.exp(-tile))
@@ -281,9 +375,6 @@
         up_scratch[1, t, pl.ds(other_row, band_rows)] = jnp.where(
             keep, cot_other_ref[t].astype(F32), 0.0
         ).astype(BF16)
-
-    load_mine.wait()
-    load_other.wait()
 
     act = jnp.zeros((cells, channels), F32)
     for a in range(3):
@@ -297,13 +388,6 @@
     act = act.astype(F32)
     second = act / (1.0 + jnp.exp(-act))
     spread(second, store_x(1), False)
-
-    for index in range(2):
-        for a in range(3):
-            for piece in range(9):
-                wl_scratch[index, a, :, piece * channels : (piece + 1) * channels] = w_scratch[
-                    index, a, piece
-                ]
 
     out_grad = up_scratch[1].astype(F32)
     spread(out_grad, store_g, True)
@@ -331,9 +415,16 @@
             preferred_element_type=F32,
         )
         for piece in range(9):
-            weight_ref[a, piece] = (
+            at = (a * 9 + piece) * channels
+            wide_ref[0, at : at + channels, :] = (
                 part[:, piece * channels : (piece + 1) * channels].T * scale
-            ).astype(BF16)
+            )
+    p, q = walk(core, high, low)
+    for k in range(side):
+        for j in range(side):
+            owner = chip_of(core, j, jnp.bitwise_xor(q, k), side)
+            start = pl.multiple_of(owner * share, 8)
+            outs[k][j] = wide_ref[0, pl.ds(start, share), :].astype(BF16)
 
     half = frames * band_rows * columns
     band = (frames, band_rows, columns, channels)
@@ -366,20 +457,20 @@
     grad_ref[...] = (my_up + sum_scratch[2:, :band_rows] * slope).astype(BF16)
 
 
-def unit(core, length, mine, other, cot_mine, cot_other, w_mine, w_other, scale):
-    frames, band_rows, columns, channels = cot_mine.shape
+def unit(length, blocks_mine, blocks_other, cots, scale, share):
+    frames, band_rows, columns, channels = cots[0].shape
     rows = 2 * band_rows
-    smem = pl.BlockSpec(memory_space=pltpu.SMEM)
-    vmem = pl.BlockSpec(memory_space=pltpu.VMEM)
-    hbm = pl.BlockSpec(memory_space=pl.ANY)
-    band = jax.ShapeDtypeStruct(cot_mine.shape, BF16)
+    side = len(blocks_mine)
+    band = jax.ShapeDtypeStruct(cots[0].shape, BF16)
+    part = jax.ShapeDtypeStruct((side, share, channels), BF16)
     flops = 2 * 27 * channels * channels * frames * rows * columns * 4
-    return pl.pallas_call(
-        functools.partial(unit_kernel, scale=scale),
-        out_shape=(band, band, jax.ShapeDtypeStruct((3, 9, channels, channels), BF16)),
-        in_specs=[smem, smem, vmem, vmem, vmem, vmem, hbm, hbm],
-        out_specs=(vmem, vmem, vmem),
+    outs = pl.pallas_call(
+        functools.partial(unit_kernel, scale=scale, side=side, share=share),
+        out_shape=[band, band] + [part] * side,
+        in_specs=scalars(1) + whole(2 * side + 2),
+        out_specs=whole(2 + side),
         scratch_shapes=[
+            pltpu.VMEM((2, 27 * channels, channels), F32),
             pltpu.VMEM((2, 3, 9, channels, channels), BF16),
             pltpu.VMEM((2, 3, channels, 9 * channels), BF16),
             pltpu.VMEM((frames, rows, columns, channels), F32),
@@ -388,50 +479,85 @@
             pltpu.VMEM((frames, rows, columns, 9 * channels), BF16),
             pltpu.VMEM((2, frames, rows, columns, channels), BF16),
             pltpu.VMEM((frames + 2, rows, columns, channels), F32),
-            pltpu.SemaphoreType.DMA((2,)),
         ],
-        compiler_params=pltpu.CompilerParams(vmem_limit_bytes=40 * 1024 * 1024),
+        compiler_params=pltpu.CompilerParams(vmem_limit_bytes=48 * 1024 * 1024),
         cost_estimate=pl.CostEstimate(flops=flops, bytes_accessed=4_000_000, transcendentals=0),
-    )(core, length, mine, other, cot_mine, cot_other, w_mine, w_other)
+    )(length, *blocks_mine, *blocks_other, *cots)
+    return outs[0], outs[1], outs[2:]
+
+
+def total_of(refs, at):
+    total = refs[0][at].astype(F32)
+    for ref in refs[1:]:
+        total = total + ref[at].astype(F32)
+    return total
+
+
+def middle_kernel(*refs):
+    side = len(refs) // 2
+    core, high, low = position(side)
+    p, _ = walk(core, high, low)
+    for k in range(side):
+        refs[side + k][...] = total_of(refs[:side], jnp.bitwise_xor(p, k)).astype(BF16)
+
+
+def middle(parts):
+    side = len(parts)
+    return pl.pallas_call(
+        middle_kernel,
+        out_shape=[jax.ShapeDtypeStruct(parts[0].shape[1:], BF16)] * side,
+        in_specs=whole(side),
+        out_specs=whole(side),
+    )(*parts)
+
+
+def last_kernel(*refs):
+    refs[-1][...] = total_of(refs[:-1], ...)
+
+
+def last(parts):
+    return pl.pallas_call(
+        last_kernel,
+        out_shape=jax.ShapeDtypeStruct(parts[0].shape, F32),
+        in_specs=whole(len(parts)),
+        out_specs=whole(1)[0],
+    )(*parts)
 
 
 def body_pair(slabs, dest, pos, lengths, cot, w_first, w_second):
     wide_size = lax.axis_size("wide")
+    side = math.isqrt(wide_size)
     core = lax.axis_index("rows")
     frames, band_rows, columns, channels = cot.shape[1:]
     share = w_first.shape[0]
-    swap = [(0, 1), (1, 0)]
+    base = padded_rows(share)
 
     def exchange(block):
-        return lax.ppermute(block, "rows", swap)
-
-    cot_mine = cot[0]
-    cot_other = exchange(cot_mine)
-    own = jnp.where(core == 0, w_first, w_second)
-    copies = jnp.broadcast_to(own[None], (wide_size, share, channels))
-    w_mine = lax.all_to_all(copies, "wide", split_axis=0, concat_axis=0, tiled=True)
-    w_mine = w_mine.reshape(3, 9, channels, channels)
-    w_other = exchange(w_mine)
-
-    outgoing = pack(slabs[0, 0], dest[0, 0], pos[0, 0], wide_size)
-    mine = lax.all_to_all(outgoing, "wide", split_axis=0, concat_axis=0, tiled=True)
-    other = exchange(mine)
+        return lax.ppermute(block, "rows", [(0, 1), (1, 0)])
+
+    def pairs(step, k):
+        both = []
+        for chip in range(wide_size):
+            high, low = chip // side, chip % side
+            to_high, to_low = (high ^ k) * side + low, high * side + (low ^ k)
+            targets = (to_high, to_low) if step == 0 else (to_low, to_high)
+            both += [(chip * 2 + c, targets[c] * 2 + c) for c in range(2)]
+        return both
+
+    def send(blocks, step):
+        sent = [lax.ppermute(blocks[k], ("wide", "rows"), pairs(step, k)) for k in range(1, side)]
+        return [blocks[0]] + sent
+
+    packed = pack(dest[0, 0], pos[0, 0], slabs[0, 0], w_first, w_second, side)
+    relayed = relay(send(packed, 0), columns, base)
+    blocks_mine = send(relayed, 1)
+    blocks_other = [exchange(block) for block in blocks_mine]
+    cots = (cot[0], exchange(cot[0]))
 
     scale = 1.0 / math.sqrt(frames * band_rows * columns * 2 * wide_size)
-    block_out, grad_input, weight = unit(
-        core.astype(jnp.int32).reshape(1),
-        lengths,
-        mine,
-        other,
-        cot_mine,
-        cot_other,
-        w_mine,
-        w_other,
-        scale,
-    )
-    parts = weight.reshape(wide_size, share, channels)
-    parts = lax.all_to_all(parts, "wide", split_axis=0, concat_axis=0, tiled=True)
-    total = jnp.sum(parts.astype(F32), axis=0)
+    block_out, grad_input, parts = unit(lengths, blocks_mine, blocks_other, cots, scale, share)
+
+    total = last(send(middle(send(parts, 1)), 0))
     total_other = exchange(total)
     share_first = jnp.where(core == 0, total, total_other)
     share_second = jnp.where(core == 0, total_other, total)
@@ -439,7 +565,9 @@
 
 
 def solution(mesh):
-    body = body_pair if mesh.shape["rows"] == 2 else body_general
+    side = math.isqrt(mesh.shape["wide"])
+    square = side * side == mesh.shape["wide"] and side & (side - 1) == 0
+    body = body_pair if mesh.shape["rows"] == 2 and square else body_general
     return jax.shard_map(
         body,
         mesh=mesh,

time: 85.4 us -> 65.1 us (0.76)
  blocking collectives: 71.2 us -> 0 us
  waiting for transfers between devices: 1.7 us -> 26 us
  starting transfers between devices: 0.58 us -> 17.6 us
  Pallas kernels: 8.42 us -> 14.7 us
  local copies, waits for them, and re-layouts: 0.12 us -> 3.59 us
    all_to_all x3 -> x0, blocking collectives: 71.2 us -> none  [the longest x1 31.4 us: body_pair(): lax.all_to_all(copies, 'wide', split_axis=0, concat_axis=0, tiled=True)]
    ppermute x4 -> x18, waiting for transfers between devices: 1.7 us -> 26 us  [the longest x12 23.7 us: send(): lax.ppermute(blocks[k], ('wide', 'rows'), pairs(step, k))]
    ppermute x4 -> x18, starting transfers between devices: 0.58 us -> 17.6 us  [the longest x12 17 us: send(): lax.ppermute(blocks[k], ('wide', 'rows'), pairs(step, k))]
    pallas_call x2 -> x5, Pallas kernels: 8.42 us -> 14.7 us  [the longest x1 6.97 us: unit(): pl.pallas_call(functools.partial(unit_kernel, scale=scale, side=side, sha...]
    unnamed x2 -> x24, local copies, waits for them, and re-layouts: 0.01 us -> 3.59 us
    select_n x1, other arithmetic: 0.7 us -> 1.59 us  [body_pair(): share_second = jnp.where(core == 0, total_other, total)]
  transfers between devices with their start and end apart: 4 -> 18, of which waited for: 2 -> 12; matrix products, arithmetic and copies ran while one was open for 0% -> 0% of each run, Pallas kernels for 2% -> 0%
where the time goes in v2:
time: 65.1 us; the launch traced here: 64.8 us
  waiting for transfers between devices  26 us (40%)
  starting transfers between devices  17.6 us (27%)
  Pallas kernels  14.7 us (23%)
  local copies, waits for them, and re-layouts  3.59 us (6%)
  other arithmetic  1.59 us (2%)
  between operations  1.34 us (2%)
    ppermute x12, waiting for transfers between devices, send(): lax.ppermute(blocks[k], ('wide', 'rows'), pairs(step, k))  23.7 us
    ppermute x12, starting transfers between devices, send(): lax.ppermute(blocks[k], ('wide', 'rows'), pairs(step, k))  17 us
    pallas_call x1, Pallas kernels, unit(): pl.pallas_call(functools.partial(unit_kernel, scale=scale, side=side, sha...  6.97 us
    unnamed x24, local copies, waits for them, and re-layouts  3.59 us
    ppermute x6, waiting for transfers between devices, exchange(): return lax.ppermute(block, 'rows', [(0, 1), (1, 0)])  2.34 us
    pallas_call x1, Pallas kernels, relay(): pl.pallas_call(functools.partial(relay_kernel, columns=columns, base=base...  2.18 us
    pallas_call x1, Pallas kernels, middle(): pl.pallas_call(middle_kernel, out_shape=[jax.ShapeDtypeStruct(parts[0].sh...  2.01 us
    pallas_call x1, Pallas kernels, pack(): pl.pallas_call(pack_kernel, out_shape=[jax.ShapeDtypeStruct((rows, channe...  1.94 us
  transfers between devices with their start and end apart: 18, of which 12 were waited for; matrix products, arithmetic and copies ran while one was open for 0% of the time, Pallas kernels for 0%

profile of v2, /device:TPU:0, one launch (start us, length us, event | category | flops | bytes accessed | tf_op | source)
XLA Modules:
  0.0 64.8 jit_solution(6705457791125408119)
XLA Ops:
  0.6 1.9 %shard_map.102 = (bf16[368,128]{1,0:T(8,128)(2,1)}, bf16[368,128]{1,0:T(8,128)(2,1)}, bf16[368,128]{1,0:T(8,128)(2,1)}, bf16[368,128]{1,0:T(8,128)(2,1)}) custom-call(s32[10]{0:T(128)} %bitcast.9, s32[10]{0:T(128)} %bitcast.10, bf16[10,32,128]{2,1,0:T(8,128)(2,1)} %bitcast.8, bf16[216,128]{1,0:T(8,128)(2,1)} %first_ref.1, bf16[216,128]{1,0:T(8,128)(2,1)} %second_ref.1), custom_call_target="tpu_custom_call" | custom-call | tf_op jit(solution)/shard_map/pallas_call | solution.py:210
  2.6 3.0 %collective-permute-start = (bf16[368,128]{1,0:T(8,128)(2,1)}, bf16[368,128]{1,0:T(8,128)(2,1)S(1)}, u32[]{:S(2)}, u32[]{:S(2)}) collective-permute-start(bf16[368,128]{1,0:T(8,128)(2,1)} %get-tuple-element.23), channel_id=1, source_target_pairs={{0,8},{1,3},{2,10},{3,1},{4,12},{5,7},{6,14},{7,5},{8,0},{9,11},{1... | collective-permute-start | bytes 282632 | tf_op jit(solution)/shard_map/ppermute | solution.py:548
  5.6 2.6 %collective-permute-start.1 = (bf16[368,128]{1,0:T(8,128)(2,1)}, bf16[368,128]{1,0:T(8,128)(2,1)S(1)}, u32[]{:S(2)}, u32[]{:S(2)}) collective-permute-start(bf16[368,128]{1,0:T(8,128)(2,1)} %get-tuple-element.24), channel_id=1, source_target_pairs={{0,16},{1,5},{2,18},{3,7},{4,20},{5,1},{6,22},{7,3},{8,24},{9,13},... | collective-permute-start | bytes 282632 | tf_op jit(solution)/shard_map/ppermute | solution.py:548
  8.2 0.0 collective-permute-start.2
  8.2 0.2 collective-permute-done.refs_1_
  8.4 0.0 copy-start.6
  8.4 3.9 %collective-permute-done.1.refs_2_ = bf16[368,128]{1,0:T(8,128)(2,1)S(1)} collective-permute-done((bf16[368,128]{1,0:T(8,128)(2,1)}, bf16[368,128]{1,0:T(8,128)(2,1)S(1)}, u32[]{:S(2)}, u32[]{:S(2)}) %collective-permute-start.1) | collective-permute-done | bytes 94240 | tf_op jit(solution)/shard_map/ppermute | solution.py:548
  12.3 0.0 copy-start.7
  12.3 2.5 %collective-permute-done.2.refs_3_ = bf16[368,128]{1,0:T(8,128)(2,1)S(1)} collective-permute-done((bf16[368,128]{1,0:T(8,128)(2,1)}, bf16[368,128]{1,0:T(8,128)(2,1)S(1)}, u32[]{:S(2)}, u32[]{:S(2)}) %collective-permute-start.2) | collective-permute-done | bytes 94240 | tf_op jit(solution)/shard_map/ppermute | solution.py:548
  14.8 0.0 copy-start.8
  14.8 0.0 copy-done.6
  14.8 0.0 copy-done.7
  14.8 0.6 copy-done.8
  15.4 0.0 copy-start.2
  15.4 2.2 %shard_map.103 = (bf16[1040,128]{1,0:T(8,128)(2,1)}, bf16[1040,128]{1,0:T(8,128)(2,1)}, bf16[1040,128]{1,0:T(8,128)(2,1)}, bf16[1040,128]{1,0:T(8,128)(2,1)}) custom-call(bf16[368,128]{1,0:T(8,128)(2,1)} %get-tuple-element.22.refs_0_, bf16[368,128]{1,0:T(8,128)(2,1)} %copy-done.6, bf16[368,128]{1,0:T(8,128)(2,1)} %copy-done.7, bf16[368,128]{1,0:T(8,128)(2,1)} %copy-done.8), custom_call_target="tpu_custom_call" | custom-call | tf_op jit(solution)/shard_map/pallas_call | solution.py:243
  17.6 1.5 %collective-permute-start.3 = (bf16[1040,128]{1,0:T(8,128)(2,1)}, bf16[1040,128]{1,0:T(8,128)(2,1)S(1)}, u32[]{:S(2)}, u32[]{:S(2)}) collective-permute-start(bf16[1040,128]{1,0:T(8,128)(2,1)} %get-tuple-element.27), channel_id=1, source_target_pairs={{0,2},{1,9},{2,0},{3,11},{4,6},{5,13},{6,4},{7,15},{8,10},{9,1},{1... | collective-permute-start | bytes 798728 | tf_op jit(solution)/shard_map/ppermute | solution.py:548
  19.1 1.6 %collective-permute-start.4 = (bf16[1040,128]{1,0:T(8,128)(2,1)}, bf16[1040,128]{1,0:T(8,128)(2,1)S(1)}, u32[]{:S(2)}, u32[]{:S(2)}) collective-permute-start(bf16[1040,128]{1,0:T(8,128)(2,1)} %get-tuple-element.28), channel_id=1, source_target_pairs={{0,4},{1,17},{2,6},{3,19},{4,0},{5,21},{6,2},{7,23},{8,12},{9,25},... | collective-permute-start | bytes 798728 | tf_op jit(solution)/shard_map/ppermute | solution.py:548
  20.6 0.4 collective-permute-start.5
  21.1 0.0 collective-permute-start.6
  21.1 3.1 %collective-permute-done.3.refs_1_ = bf16[1040,128]{1,0:T(8,128)(2,1)S(1)} collective-permute-done((bf16[1040,128]{1,0:T(8,128)(2,1)}, bf16[1040,128]{1,0:T(8,128)(2,1)S(1)}, u32[]{:S(2)}, u32[]{:S(2)}) %collective-permute-start.3) | collective-permute-done | bytes 266272 | tf_op jit(solution)/shard_map/ppermute | solution.py:548
  24.2 0.0 collective-permute-start.7
  24.2 4.3 %collective-permute-done.4.refs_2_ = bf16[1040,128]{1,0:T(8,128)(2,1)S(1)} collective-permute-done((bf16[1040,128]{1,0:T(8,128)(2,1)}, bf16[1040,128]{1,0:T(8,128)(2,1)S(1)}, u32[]{:S(2)}, u32[]{:S(2)}) %collective-permute-start.4) | collective-permute-done | bytes 266272 | tf_op jit(solution)/shard_map/ppermute | solution.py:548
  28.6 0.0 collective-permute-start.8
  28.6 0.0 collective-permute-done.5.refs_3_
  28.6 0.5 collective-permute-start.9
  29.1 0.0 copy-done.2
  29.1 0.1 collective-permute-start.10
  29.8 0.8 %collective-permute-done.10.refs_9_ = bf16[5,2,32,128]{3,2,1,0:T(8,128)(2,1)S(1)} collective-permute-done((bf16[5,2,32,128]{3,2,1,0:T(8,128)(2,1)S(1)}, bf16[5,2,32,128]{3,2,1,0:T(8,128)(2,1)S(1)}, u32[]{:S(2)}, u32[]{:S(2)}) %collective-permute-start.10) | collective-permute-done | bytes 81952 | tf_op jit(solution)/shard_map/ppermute | solution.py:536
  30.6 0.0 collective-permute-done.6.refs_4_
  30.6 0.0 collective-permute-done.7.refs_5_
  30.6 0.0 collective-permute-done.8.refs_6_
  30.6 0.0 collective-permute-done.9.refs_7_
  30.6 0.0 copy-start.1
  30.6 0.9 %copy-done.1 = bf16[1040,128]{1,0:T(8,128)(2,1)S(1)} copy-done((bf16[1040,128]{1,0:T(8,128)(2,1)S(1)}, bf16[1040,128]{1,0:T(8,128)(2,1)}, u32[]{:S(2)}) %copy-start.1) | copy-done | bytes 266264
  31.6 7.0 %shard_map.104 = (bf16[5,2,32,128]{3,2,1,0:T(8,128)(2,1)}, bf16[5,2,32,128]{3,2,1,0:T(8,128)(2,1)}, bf16[4,216,128]{2,1,0:T(8,128)(2,1)S(1)}, bf16[4,216,128]{2,...) custom-call(s32[1]{0:T(128)S(6)} %copy.11.length_ref, ...), custom_call_target="tpu_custom_call" | custom-call | flops 2264924160 | bytes 4000000 | tf_op jit(solution)/shard_map/pallas_call | solution.py:467
  38.6 0.0 copy-start
  38.6 0.7 %copy-done = bf16[4,216,128]{2,1,0:T(8,128)(2,1)} copy-done((bf16[4,216,128]{2,1,0:T(8,128)(2,1)}, bf16[4,216,128]{2,1,0:T(8,128)(2,1)S(1)}, u32[]{:S(2)}) %copy-start) | copy-done | bytes 221208
  39.2 0.6 collective-permute-start.11
  39.8 1.4 %collective-permute-start.12 = (bf16[4,216,128]{2,1,0:T(8,128)(2,1)S(1)}, bf16[4,216,128]{2,1,0:T(8,128)(2,1)S(1)}, u32[]{:S(2)}, u32[]{:S(2)}) collective-permute-start(bf16[4,216,128]{2,1,0:T(8,128)(2,1)S(1)} %get-tuple-element.34), channel_id=1, source_target_pairs={{0,4},{1,17},{2,6},{3,19},{4,0},{5,21},{6,2},{7,23},{8,12},{9,25},... | collective-permute-start | bytes 663560 | tf_op jit(solution)/shard_map/ppermute | solution.py:548
  41.3 1.4 %collective-permute-start.13 = (bf16[4,216,128]{2,1,0:T(8,128)(2,1)S(1)}, bf16[4,216,128]{2,1,0:T(8,128)(2,1)S(1)}, u32[]{:S(2)}, u32[]{:S(2)}) collective-permute-start(bf16[4,216,128]{2,1,0:T(8,128)(2,1)S(1)} %get-tuple-element.35), channel_id=1, source_target_pairs={{0,6},{1,25},{2,4},{3,27},{4,2},{5,29},{6,0},{7,31},{8,14},{9,17},... | collective-permute-start | bytes 663560 | tf_op jit(solution)/shard_map/ppermute | solution.py:548
  42.7 2.4 %collective-permute-done.11.refs_1_ = bf16[4,216,128]{2,1,0:T(8,128)(2,1)S(1)} collective-permute-done((bf16[4,216,128]{2,1,0:T(8,128)(2,1)S(1)}, bf16[4,216,128]{2,1,0:T(8,128)(2,1)S(1)}, u32[]{:S(2)}, u32[]{:S(2)}) %collective-permute-start.11) | collective-permute-done | bytes 221216 | tf_op jit(solution)/shard_map/ppermute | solution.py:548
  45.2 0.0 copy-start.3
  45.2 2.0 %collective-permute-done.12.refs_2_ = bf16[4,216,128]{2,1,0:T(8,128)(2,1)S(1)} collective-permute-done((bf16[4,216,128]{2,1,0:T(8,128)(2,1)S(1)}, bf16[4,216,128]{2,1,0:T(8,128)(2,1)S(1)}, u32[]{:S(2)}, u32[]{:S(2)}) %collective-permute-start.12) | collective-permute-done | bytes 221216 | tf_op jit(solution)/shard_map/ppermute | solution.py:548
  47.2 0.0 copy-start.4
  47.2 1.4 %collective-permute-done.13.refs_3_ = bf16[4,216,128]{2,1,0:T(8,128)(2,1)S(1)} collective-permute-done((bf16[4,216,128]{2,1,0:T(8,128)(2,1)S(1)}, bf16[4,216,128]{2,1,0:T(8,128)(2,1)S(1)}, u32[]{:S(2)}, u32[]{:S(2)}) %collective-permute-start.13) | collective-permute-done | bytes 221216 | tf_op jit(solution)/shard_map/ppermute | solution.py:548
  48.5 0.0 copy-start.5
  48.5 0.0 copy-done.3
  48.5 0.0 copy-done.4
  48.5 0.7 %copy-done.5 = bf16[4,216,128]{2,1,0:T(8,128)(2,1)} copy-done((bf16[4,216,128]{2,1,0:T(8,128)(2,1)}, bf16[4,216,128]{2,1,0:T(8,128)(2,1)S(1)}, u32[]{:S(2)}) %copy-start.5) | copy-done | bytes 221208
  49.2 2.0 %shard_map.105 = (bf16[216,128]{1,0:T(8,128)(2,1)}, bf16[216,128]{1,0:T(8,128)(2,1)}, bf16[216,128]{1,0:T(8,128)(2,1)}, bf16[216,128]{1,0:T(8,128)(2,1)}) custom-call(bf16[4,216,128]{2,1,0:T(8,128)(2,1)} %copy-done, bf16[4,216,128]{2,1,0:T(8,128)(2,1)} %copy-done.3, bf16[4,216,128]{2,1,0:T(8,128)(2,1)} %copy-done.4, bf16[4,216,128]{2,1,0:T(8,128)(2,1)} %copy-done.5), custom_call_target="tpu_custom_call" | custom-call | tf_op jit(solution)/shard_map/pallas_call | solution.py:506
  51.2 1.1 %collective-permute-start.14 = (bf16[216,128]{1,0:T(8,128)(2,1)}, bf16[216,128]{1,0:T(8,128)(2,1)S(1)}, u32[]{:S(2)}, u32[]{:S(2)}) collective-permute-start(bf16[216,128]{1,0:T(8,128)(2,1)} %get-tuple-element.37), channel_id=1, source_target_pairs={{0,8},{1,3},{2,10},{3,1},{4,12},{5,7},{6,14},{7,5},{8,0},{9,11},{1... | collective-permute-start | bytes 165896 | tf_op jit(solution)/shard_map/ppermute | solution.py:548
  52.3 0.9 %collective-permute-start.15 = (bf16[216,128]{1,0:T(8,128)(2,1)}, bf16[216,128]{1,0:T(8,128)(2,1)S(1)}, u32[]{:S(2)}, u32[]{:S(2)}) collective-permute-start(bf16[216,128]{1,0:T(8,128)(2,1)} %get-tuple-element.38), channel_id=1, source_target_pairs={{0,16},{1,5},{2,18},{3,7},{4,20},{5,1},{6,22},{7,3},{8,24},{9,13},... | collective-permute-start | bytes 165896 | tf_op jit(solution)/shard_map/ppermute | solution.py:548
  53.2 2.4 %collective-permute-start.16 = (bf16[216,128]{1,0:T(8,128)(2,1)}, bf16[216,128]{1,0:T(8,128)(2,1)S(1)}, u32[]{:S(2)}, u32[]{:S(2)}) collective-permute-start(bf16[216,128]{1,0:T(8,128)(2,1)} %get-tuple-element.39), channel_id=1, source_target_pairs={{0,24},{1,7},{2,26},{3,5},{4,28},{5,3},{6,30},{7,1},{8,16},{9,15},... | collective-permute-start | bytes 165896 | tf_op jit(solution)/shard_map/ppermute | solution.py:548
  55.6 0.0 collective-permute-done.14.refs_1_
  55.6 0.0 copy-start.9
  55.6 2.6 %collective-permute-done.15.refs_2_ = bf16[216,128]{1,0:T(8,128)(2,1)S(1)} collective-permute-done((bf16[216,128]{1,0:T(8,128)(2,1)}, bf16[216,128]{1,0:T(8,128)(2,1)S(1)}, u32[]{:S(2)}, u32[]{:S(2)}) %collective-permute-start.15) | collective-permute-done | bytes 55328 | tf_op jit(solution)/shard_map/ppermute | solution.py:548
  58.2 1.3 %collective-permute-done.16.refs_3_ = bf16[216,128]{1,0:T(8,128)(2,1)S(1)} collective-permute-done((bf16[216,128]{1,0:T(8,128)(2,1)}, bf16[216,128]{1,0:T(8,128)(2,1)S(1)}, u32[]{:S(2)}, u32[]{:S(2)}) %collective-permute-start.16) | collective-permute-done | bytes 55328 | tf_op jit(solution)/shard_map/ppermute | solution.py:548
  59.5 0.0 copy-done.9
  59.5 0.0 copy-done.10
  59.5 0.6 copy-done.11
  60.1 1.6 %shard_map.106 = f32[216,128]{1,0:T(8,128)} custom-call(bf16[216,128]{1,0:T(8,128)(2,1)} %get-tuple-element.36.refs_0_, bf16[216,128]{1,0:T(8,128)(2,1)} %copy-done.9, bf16[216,128]{1,0:T(8,128)(2,1)} %copy-done.10, bf16[216,128]{1,0:T(8,128)(2,1)} %copy-done.11), custom_call_target="tpu_custom_call" | custom-call | tf_op jit(solution)/shard_map/pallas_call | solution.py:519
  61.7 0.0 collective-permute-start.17
  61.7 1.5 %collective-permute-done.17 = f32[216,128]{1,0:T(8,128)S(1)} collective-permute-done((f32[216,128]{1,0:T(8,128)}, f32[216,128]{1,0:T(8,128)S(1)}, u32[]{:S(2)}, u32[]{:S(2)}) %collective-permute-start.17) | collective-permute-done | bytes 110624 | tf_op jit(solution)/shard_map/ppermute | solution.py:536
  63.2 1.6 %broadcast_select_fusion = (f32[216,128]{1,0:T(8,128)}, f32[216,128]{1,0:T(8,128)}) fusion(f32[216,128]{1,0:T(8,128)S(1)} %collective-permute-done.17, f32[216,128]{1,0:T(8,128)} %shard_map.106, pred[]{:T(512)S(6)} %eq.4), kind=kLoop, calls=%fused_computation | loop fusion | flops 55296 | bytes 442369 | tf_op jit(solution)/shard_map/jit(_where)/select_n | solution.py:563
  (2 shorter events, 0.0 us)
Async XLA Ops:
  2.6 5.8 %collective-permute-start = (bf16[368,128]{1,0:T(8,128)(2,1)}, bf16[368,128]{1,0:T(8,128)(2,1)S(1)}, u32[]{:S(2)}, u32[]{:S(2)}) collective-permute-start(bf16[368,128]{1,0:T(8,128)(2,1)} %get-tuple-element.23), channel_id=1, source_target_pairs={{0,8},{1,3},{2,10},{3,1},{4,12},{5,7},{6,14},{7,5},{8,0},{9,11},{1... | collective-permute-start | bytes 282632 | tf_op jit(solution)/shard_map/ppermute | solution.py:548
  5.6 6.7 %collective-permute-start.1 = (bf16[368,128]{1,0:T(8,128)(2,1)}, bf16[368,128]{1,0:T(8,128)(2,1)S(1)}, u32[]{:S(2)}, u32[]{:S(2)}) collective-permute-start(bf16[368,128]{1,0:T(8,128)(2,1)} %get-tuple-element.24), channel_id=1, source_target_pairs={{0,16},{1,5},{2,18},{3,7},{4,20},{5,1},{6,22},{7,3},{8,24},{9,13},... | collective-permute-start | bytes 282632 | tf_op jit(solution)/shard_map/ppermute | solution.py:548
  8.2 6.6 %collective-permute-start.2 = (bf16[368,128]{1,0:T(8,128)(2,1)}, bf16[368,128]{1,0:T(8,128)(2,1)S(1)}, u32[]{:S(2)}, u32[]{:S(2)}) collective-permute-start(bf16[368,128]{1,0:T(8,128)(2,1)} %get-tuple-element.25), channel_id=1, source_target_pairs={{0,24},{1,7},{2,26},{3,5},{4,28},{5,3},{6,30},{7,1},{8,16},{9,15},... | collective-permute-start | bytes 282632 | tf_op jit(solution)/shard_map/ppermute | solution.py:548
  8.4 6.4 %copy-start.6 = (bf16[368,128]{1,0:T(8,128)(2,1)}, bf16[368,128]{1,0:T(8,128)(2,1)S(1)}, u32[]{:S(2)}) copy-start(bf16[368,128]{1,0:T(8,128)(2,1)S(1)} %collective-permute-done.refs_1_) | copy-start | bytes 282628
  12.3 2.5 %copy-start.7 = (bf16[368,128]{1,0:T(8,128)(2,1)}, bf16[368,128]{1,0:T(8,128)(2,1)S(1)}, u32[]{:S(2)}) copy-start(bf16[368,128]{1,0:T(8,128)(2,1)S(1)} %collective-permute-done.1.refs_2_) | copy-start | bytes 282628
  14.8 0.6 copy-start.8
  15.4 13.7 %copy-start.2 = (bf16[1,5,2,32,128]{4,3,2,1,0:T(8,128)(2,1)S(1)}, bf16[1,5,2,32,128]{4,3,2,1,0:T(8,128)(2,1)}, u32[]{:S(2)}) copy-start(bf16[1,5,2,32,128]{4,3,2,1,0:T(8,128)(2,1)} %param.11) | copy-start | bytes 245764
  17.6 6.6 %collective-permute-start.3 = (bf16[1040,128]{1,0:T(8,128)(2,1)}, bf16[1040,128]{1,0:T(8,128)(2,1)S(1)}, u32[]{:S(2)}, u32[]{:S(2)}) collective-permute-start(bf16[1040,128]{1,0:T(8,128)(2,1)} %get-tuple-element.27), channel_id=1, source_target_pairs={{0,2},{1,9},{2,0},{3,11},{4,6},{5,13},{6,4},{7,15},{8,10},{9,1},{1... | collective-permute-start | bytes 798728 | tf_op jit(solution)/shard_map/ppermute | solution.py:548
  19.1 9.5 %collective-permute-start.4 = (bf16[1040,128]{1,0:T(8,128)(2,1)}, bf16[1040,128]{1,0:T(8,128)(2,1)S(1)}, u32[]{:S(2)}, u32[]{:S(2)}) collective-permute-start(bf16[1040,128]{1,0:T(8,128)(2,1)} %get-tuple-element.28), channel_id=1, source_target_pairs={{0,4},{1,17},{2,6},{3,19},{4,0},{5,21},{6,2},{7,23},{8,12},{9,25},... | collective-permute-start | bytes 798728 | tf_op jit(solution)/shard_map/ppermute | solution.py:548
  20.6 7.9 %collective-permute-start.5 = (bf16[1040,128]{1,0:T(8,128)(2,1)}, bf16[1040,128]{1,0:T(8,128)(2,1)S(1)}, u32[]{:S(2)}, u32[]{:S(2)}) collective-permute-start(bf16[1040,128]{1,0:T(8,128)(2,1)} %get-tuple-element.29), channel_id=1, source_target_pairs={{0,6},{1,25},{2,4},{3,27},{4,2},{5,29},{6,0},{7,31},{8,14},{9,17},... | collective-permute-start | bytes 798728 | tf_op jit(solution)/shard_map/ppermute | solution.py:548
  21.1 9.5 %collective-permute-start.6 = (bf16[1040,128]{1,0:T(8,128)(2,1)}, bf16[1040,128]{1,0:T(8,128)(2,1)S(1)}, u32[]{:S(2)}, u32[]{:S(2)}) collective-permute-start(bf16[1040,128]{1,0:T(8,128)(2,1)} %get-tuple-element.26.refs_0_), channel_id=1, source_target_pairs={{0,1},{1,0},{2,3},{3,2},{4,5},{5,4},{6,7},{7,6},{8,9},{9,8},{10,11... | collective-permute-start | bytes 798728 | tf_op jit(solution)/shard_map/ppermute | solution.py:536
  24.2 6.4 %collective-permute-start.7 = (bf16[1040,128]{1,0:T(8,128)(2,1)S(1)}, bf16[1040,128]{1,0:T(8,128)(2,1)S(1)}, u32[]{:S(2)}, u32[]{:S(2)}) collective-permute-start(bf16[1040,128]{1,0:T(8,128)(2,1)S(1)} %collective-permute-done.3.refs_1_), channel_id=1, source_target_pairs={{0,1},{1,0},{2,3},{3,2},{4,5},{5,4},{6,7},{7,6},{8,9},{9,8},{10,11... | collective-permute-start | bytes 798728 | tf_op jit(solution)/shard_map/ppermute | solution.py:536
  28.6 2.0 %collective-permute-start.8 = (bf16[1040,128]{1,0:T(8,128)(2,1)S(1)}, bf16[1040,128]{1,0:T(8,128)(2,1)S(1)}, u32[]{:S(2)}, u32[]{:S(2)}) collective-permute-start(bf16[1040,128]{1,0:T(8,128)(2,1)S(1)} %collective-permute-done.4.refs_2_), channel_id=1, source_target_pairs={{0,1},{1,0},{2,3},{3,2},{4,5},{5,4},{6,7},{7,6},{8,9},{9,8},{10,11... | collective-permute-start | bytes 798728 | tf_op jit(solution)/shard_map/ppermute | solution.py:536
  28.6 2.0 %collective-permute-start.9 = (bf16[1040,128]{1,0:T(8,128)(2,1)S(1)}, bf16[1040,128]{1,0:T(8,128)(2,1)S(1)}, u32[]{:S(2)}, u32[]{:S(2)}) collective-permute-start(bf16[1040,128]{1,0:T(8,128)(2,1)S(1)} %collective-permute-done.5.refs_3_), channel_id=1, source_target_pairs={{0,1},{1,0},{2,3},{3,2},{4,5},{5,4},{6,7},{7,6},{8,9},{9,8},{10,11... | collective-permute-start | bytes 798728 | tf_op jit(solution)/shard_map/ppermute | solution.py:536
  29.1 1.5 %collective-permute-start.10 = (bf16[5,2,32,128]{3,2,1,0:T(8,128)(2,1)S(1)}, bf16[5,2,32,128]{3,2,1,0:T(8,128)(2,1)S(1)}, u32[]{:S(2)}, u32[]{:S(2)}) collective-permute-start(bf16[5,2,32,128]{3,2,1,0:T(8,128)(2,1)S(1)} %bitcast.6), channel_id=1, source_target_pairs={{0,1},{1,0},{2,3},{3,2},{4,5},{5,4},{6,7},{7,6},{8,9},{9,8},{10,11... | collective-permute-start | bytes 245768 | tf_op jit(solution)/shard_map/ppermute | solution.py:536
  30.6 1.0 %copy-start.1 = (bf16[1040,128]{1,0:T(8,128)(2,1)S(1)}, bf16[1040,128]{1,0:T(8,128)(2,1)}, u32[]{:S(2)}) copy-start(bf16[1040,128]{1,0:T(8,128)(2,1)} %get-tuple-element.26.refs_0_) | copy-start | bytes 798724
  38.6 0.7 %copy-start = (bf16[4,216,128]{2,1,0:T(8,128)(2,1)}, bf16[4,216,128]{2,1,0:T(8,128)(2,1)S(1)}, u32[]{:S(2)}) copy-start(bf16[4,216,128]{2,1,0:T(8,128)(2,1)S(1)} %get-tuple-element.32.refs_0_) | copy-start | bytes 663556
  39.2 5.9 %collective-permute-start.11 = (bf16[4,216,128]{2,1,0:T(8,128)(2,1)S(1)}, bf16[4,216,128]{2,1,0:T(8,128)(2,1)S(1)}, u32[]{:S(2)}, u32[]{:S(2)}) collective-permute-start(bf16[4,216,128]{2,1,0:T(8,128)(2,1)S(1)} %get-tuple-element.33), channel_id=1, source_target_pairs={{0,2},{1,9},{2,0},{3,11},{4,6},{5,13},{6,4},{7,15},{8,10},{9,1},{1... | collective-permute-start | bytes 663560 | tf_op jit(solution)/shard_map/ppermute | solution.py:548
  39.8 7.3 %collective-permute-start.12 = (bf16[4,216,128]{2,1,0:T(8,128)(2,1)S(1)}, bf16[4,216,128]{2,1,0:T(8,128)(2,1)S(1)}, u32[]{:S(2)}, u32[]{:S(2)}) collective-permute-start(bf16[4,216,128]{2,1,0:T(8,128)(2,1)S(1)} %get-tuple-element.34), channel_id=1, source_target_pairs={{0,4},{1,17},{2,6},{3,19},{4,0},{5,21},{6,2},{7,23},{8,12},{9,25},... | collective-permute-start | bytes 663560 | tf_op jit(solution)/shard_map/ppermute | solution.py:548
  41.3 7.2 %collective-permute-start.13 = (bf16[4,216,128]{2,1,0:T(8,128)(2,1)S(1)}, bf16[4,216,128]{2,1,0:T(8,128)(2,1)S(1)}, u32[]{:S(2)}, u32[]{:S(2)}) collective-permute-start(bf16[4,216,128]{2,1,0:T(8,128)(2,1)S(1)} %get-tuple-element.35), channel_id=1, source_target_pairs={{0,6},{1,25},{2,4},{3,27},{4,2},{5,29},{6,0},{7,31},{8,14},{9,17},... | collective-permute-start | bytes 663560 | tf_op jit(solution)/shard_map/ppermute | solution.py:548
  45.2 3.4 %copy-start.3 = (bf16[4,216,128]{2,1,0:T(8,128)(2,1)}, bf16[4,216,128]{2,1,0:T(8,128)(2,1)S(1)}, u32[]{:S(2)}) copy-start(bf16[4,216,128]{2,1,0:T(8,128)(2,1)S(1)} %collective-permute-done.11.refs_1_) | copy-start | bytes 663556
  47.2 1.4 %copy-start.4 = (bf16[4,216,128]{2,1,0:T(8,128)(2,1)}, bf16[4,216,128]{2,1,0:T(8,128)(2,1)S(1)}, u32[]{:S(2)}) copy-start(bf16[4,216,128]{2,1,0:T(8,128)(2,1)S(1)} %collective-permute-done.12.refs_2_) | copy-start | bytes 663556
  48.5 0.7 %copy-start.5 = (bf16[4,216,128]{2,1,0:T(8,128)(2,1)}, bf16[4,216,128]{2,1,0:T(8,128)(2,1)S(1)}, u32[]{:S(2)}) copy-start(bf16[4,216,128]{2,1,0:T(8,128)(2,1)S(1)} %collective-permute-done.13.refs_3_) | copy-start | bytes 663556
  51.2 4.4 %collective-permute-start.14 = (bf16[216,128]{1,0:T(8,128)(2,1)}, bf16[216,128]{1,0:T(8,128)(2,1)S(1)}, u32[]{:S(2)}, u32[]{:S(2)}) collective-permute-start(bf16[216,128]{1,0:T(8,128)(2,1)} %get-tuple-element.37), channel_id=1, source_target_pairs={{0,8},{1,3},{2,10},{3,1},{4,12},{5,7},{6,14},{7,5},{8,0},{9,11},{1... | collective-permute-start | bytes 165896 | tf_op jit(solution)/shard_map/ppermute | solution.py:548
  52.3 5.9 %collective-permute-start.15 = (bf16[216,128]{1,0:T(8,128)(2,1)}, bf16[216,128]{1,0:T(8,128)(2,1)S(1)}, u32[]{:S(2)}, u32[]{:S(2)}) collective-permute-start(bf16[216,128]{1,0:T(8,128)(2,1)} %get-tuple-element.38), channel_id=1, source_target_pairs={{0,16},{1,5},{2,18},{3,7},{4,20},{5,1},{6,22},{7,3},{8,24},{9,13},... | collective-permute-start | bytes 165896 | tf_op jit(solution)/shard_map/ppermute | solution.py:548
  53.2 6.3 %collective-permute-start.16 = (bf16[216,128]{1,0:T(8,128)(2,1)}, bf16[216,128]{1,0:T(8,128)(2,1)S(1)}, u32[]{:S(2)}, u32[]{:S(2)}) collective-permute-start(bf16[216,128]{1,0:T(8,128)(2,1)} %get-tuple-element.39), channel_id=1, source_target_pairs={{0,24},{1,7},{2,26},{3,5},{4,28},{5,3},{6,30},{7,1},{8,16},{9,15},... | collective-permute-start | bytes 165896 | tf_op jit(solution)/shard_map/ppermute | solution.py:548
  55.6 3.8 %copy-start.9 = (bf16[216,128]{1,0:T(8,128)(2,1)}, bf16[216,128]{1,0:T(8,128)(2,1)S(1)}, u32[]{:S(2)}) copy-start(bf16[216,128]{1,0:T(8,128)(2,1)S(1)} %collective-permute-done.14.refs_1_) | copy-start | bytes 165892
  58.2 1.3 %copy-start.10 = (bf16[216,128]{1,0:T(8,128)(2,1)}, bf16[216,128]{1,0:T(8,128)(2,1)S(1)}, u32[]{:S(2)}) copy-start(bf16[216,128]{1,0:T(8,128)(2,1)S(1)} %collective-permute-done.15.refs_2_) | copy-start | bytes 165892
  59.5 0.6 copy-start.11
  61.7 1.5 %collective-permute-start.17 = (f32[216,128]{1,0:T(8,128)}, f32[216,128]{1,0:T(8,128)S(1)}, u32[]{:S(2)}, u32[]{:S(2)}) collective-permute-start(f32[216,128]{1,0:T(8,128)} %shard_map.106), channel_id=1, source_target_pairs={{0,1},{1,0},{2,3},{3,2},{4,5},{5,4},{6,7},{7,6},{8,9},{9,8},{10,11... | collective-permute-start | bytes 331784 | tf_op jit(solution)/shard_map/ppermute | solution.py:536

commit v3 on v2

--- a/solution.py
+++ b/solution.py
@@ -11,6 +11,7 @@
 BF16 = jnp.bfloat16
 F32 = jnp.float32
 LABEL_ROWS = 16
+SMALL = pltpu.CompilerParams(vmem_limit_bytes=8 * 1024 * 1024)
 
 
 def with_halo(block, sides, width):
@@ -176,19 +177,32 @@
     return -(-rows // 16) * 16
 
 
-def pack_kernel(dest_ref, pos_ref, slabs_ref, first_ref, second_ref, *out_refs):
-    side = len(out_refs)
+def pack_kernel(dest_ref, pos_ref, slabs_hbm, first_hbm, second_hbm, *refs):
+    side = len(refs) - 3
+    out_refs = refs[:side]
+    slabs_ref, own_ref, sem = refs[side:]
     core, high, low = position(side)
     p, _ = walk(core, high, low)
     count, columns, channels = slabs_ref.shape
-    share = first_ref.shape[0]
+    share = own_ref.shape[0]
     base = padded_rows(share)
+    load_slabs = pltpu.make_async_copy(slabs_hbm, slabs_ref, sem.at[0])
+    load_first = pltpu.make_async_copy(first_hbm, own_ref, sem.at[1])
+    load_second = pltpu.make_async_copy(second_hbm, own_ref, sem.at[1])
+    load_slabs.start()
+
+    @pl.when(core == 0)
+    def _():
+        load_first.start()
+
+    @pl.when(core != 0)
+    def _():
+        load_second.start()
+
     row = lax.broadcasted_iota(jnp.int32, (LABEL_ROWS, channels), 0)
-    own = jnp.where(core == 0, first_ref[...].astype(F32), second_ref[...].astype(F32))
-    own = jnp.concatenate([own, jnp.zeros((base - share, channels), F32)], axis=0).astype(BF16)
+    load_slabs.wait()
     slabs = [slabs_ref[s].astype(F32) for s in range(count)]
     for k in range(side):
-        out_refs[k][:base, :] = own
         labels = jnp.full((LABEL_ROWS, channels), -1.0, F32)
         for q in range(side):
             target = chip_of(core, jnp.bitwise_xor(p, k), q, side)
@@ -202,6 +216,11 @@
             at = base + q * columns
             out_refs[k][at : at + columns, :] = total.astype(BF16)
         out_refs[k][base + side * columns :, :] = labels.astype(BF16)
+    load_first.wait()
+    own = own_ref[...].astype(F32)
+    own = jnp.concatenate([own, jnp.zeros((base - share, channels), F32)], axis=0).astype(BF16)
+    for k in range(side):
+        out_refs[k][:base, :] = own
 
 
 def pack(dest, pos, slabs, first, second, side):
@@ -210,17 +229,37 @@
     return pl.pallas_call(
         pack_kernel,
         out_shape=[jax.ShapeDtypeStruct((rows, channels), BF16)] * side,
-        in_specs=scalars(2) + whole(3),
+        in_specs=scalars(2) + [pl.BlockSpec(memory_space=pltpu.HBM)] * 3,
         out_specs=whole(side),
+        scratch_shapes=[
+            pltpu.VMEM(slabs.shape, BF16),
+            pltpu.VMEM(first.shape, BF16),
+            pltpu.SemaphoreType.DMA((2,)),
+        ],
     )(dest, pos, slabs, first, second)
 
 
-def relay_kernel(*refs, columns, base):
+def keep_kernel(in_ref, out_ref):
+    out_ref[...] = in_ref[...]
+
+
+def keep(block):
+    return pl.pallas_call(
+        keep_kernel,
+        out_shape=jax.ShapeDtypeStruct(block.shape, block.dtype),
+        in_specs=whole(1),
+        out_specs=whole(1)[0],
+        compiler_params=SMALL,
+    )(block)
+
+
+def relay_kernel(cot_ref, *refs, columns, base):
     side = len(refs) // 2
-    ins, outs = refs[:side], refs[side:]
+    ins, outs = refs[:side][::-1], refs[side:]
     core, high, low = position(side)
     _, q = walk(core, high, low)
     channels = ins[0].shape[1]
+    end = side * (base + columns) + LABEL_ROWS
     row = lax.broadcasted_iota(jnp.int32, (LABEL_ROWS, channels), 0)
     for j in range(side):
         target = jnp.bitwise_xor(q, j)
@@ -233,19 +272,23 @@
             theirs = ins[k][base + side * columns :, :].astype(F32)
             label = jnp.sum(jnp.where(row == target, theirs, 0.0), axis=0, keepdims=True)
             labels = jnp.where(row == k, label, labels)
-        outs[j][side * (base + columns) :, :] = labels.astype(BF16)
-
-
-def relay(ins, columns, base):
+        outs[j][end - LABEL_ROWS : end, :] = labels.astype(BF16)
+    outs[0][end:, :] = cot_ref[...].reshape(-1, channels)
+
+
+def relay(cot, ins, columns, base):
     side = len(ins)
     channels = ins[0].shape[1]
     rows = side * (base + columns) + LABEL_ROWS
+    extra = cot.size // channels
     return pl.pallas_call(
         functools.partial(relay_kernel, columns=columns, base=base),
-        out_shape=[jax.ShapeDtypeStruct((rows, channels), BF16)] * side,
-        in_specs=whole(side),
+        out_shape=[jax.ShapeDtypeStruct((rows + extra, channels), BF16)]
+        + [jax.ShapeDtypeStruct((rows, channels), BF16)] * (side - 1),
+        in_specs=whole(side + 1),
         out_specs=whole(side),
-    )(*ins)
+        compiler_params=SMALL,
+    )(cot, *ins[::-1])
 
 
 def settle(blocks, tile_ref, first_row, base):
@@ -253,7 +296,8 @@
     frames, _, columns, channels = tile_ref.shape
     slots = []
     for block in blocks:
-        labels = block[side * (base + columns) :, :].astype(F32)
+        end = side * (base + columns)
+        labels = block[end : end + LABEL_ROWS, :].astype(F32)
         for k in range(side):
             at = side * base + k * columns
             values = block[at : at + columns, :].astype(F32)
@@ -304,6 +348,43 @@
                     store(row, row + 1, piece, jnp.zeros_like(source[:, :1]))
 
 
+def store_columns(scratch, index, frames, channels):
+    def store(low, high, piece, values):
+        lanes = slice(piece * channels, (piece + 1) * channels)
+        scratch[index, 2:, low:high, :, lanes] = values
+        scratch[index, 0, low:high, :, lanes] = values[0]
+        scratch[index, 1, low:high, :, lanes] = values[0]
+
+    return store
+
+
+def store_plain(scratch, channels):
+    def store(low, high, piece, values):
+        scratch[:, low:high, :, piece * channels : (piece + 1) * channels] = values
+
+    return store
+
+
+def data_grad(columns, wl_ref, sum_ref):
+    frames, rows, count, nine = columns.shape
+    channels = wl_ref.shape[1]
+    nt = (((1,), (1,)), ((), ()))
+    flat = columns.reshape(frames * rows * count, nine)
+    sum_ref[...] = jnp.zeros(sum_ref.shape, F32)
+    for a in range(3):
+        part = lax.dot_general(flat, wl_ref[a], nt, preferred_element_type=F32)
+        sum_ref[a : a + frames] += part.reshape(frames, rows, count, channels)
+    sum_ref[2] = sum_ref[0] + sum_ref[1] + sum_ref[2]
+
+
+def act_gradient(out_grad, act, wl_ref, g_ref, sum_ref):
+    spread(out_grad.astype(F32), store_plain(g_ref, out_grad.shape[-1]), True)
+    data_grad(g_ref[...], wl_ref, sum_ref)
+    act = act.astype(F32)
+    sig = 1.0 / (1.0 + jnp.exp(-act))
+    return (sum_ref[2:] * (sig * (1.0 + act * (1.0 - sig)))).astype(BF16)
+
+
 def unit_kernel(length_ref, *refs, scale, side, share):
     refs = list(refs)
 
@@ -313,15 +394,12 @@
         return taken
 
     blocks_mine, blocks_other = take(side), take(side)
-    cot_mine_ref, cot_other_ref = take(2)
-    block_ref, grad_ref = take(2)
+    tile_ref, act_scratch, out_grad_ref, act_grad_ref = take(4)
+    w_second_ref, wl_first_ref, wl_second_ref = take(3)
     outs = take(side)
     (
         wide_ref,
-        w_scratch,
-        wl_scratch,
-        tile_scratch,
-        act_scratch,
+        w_first_ref,
         x_scratch,
         g_scratch,
         up_scratch,
@@ -329,83 +407,62 @@
     ) = refs
     core, high, low = position(side)
     length = length_ref[0]
-    frames, rows, columns, channels = tile_scratch.shape
-    band_rows = block_ref.shape[1]
+    frames, rows, columns, channels = tile_ref.shape
+    band_rows = rows // 2
     cells = frames * rows * columns
     nine = 9 * channels
     my_row = core * band_rows
     other_row = (1 - core) * band_rows
     base = padded_rows(share)
 
-    settle(blocks_mine, tile_scratch, my_row, base)
-    settle(blocks_other, tile_scratch, other_row, base)
+    settle(blocks_mine, tile_ref, my_row, base)
+    settle(blocks_other, tile_ref, other_row, base)
     gather_weight(blocks_mine, wide_ref, core, high, low, share, base)
     gather_weight(blocks_other, wide_ref, 1 - core, high, low, share, base)
-    for index in range(2):
-        for a in range(3):
-            for piece in range(9):
-                at = (a * 9 + piece) * channels
-                values = wide_ref[index, at : at + channels, :].astype(BF16)
-                w_scratch[index, a, piece] = values
-                wl_scratch[index, a, :, piece * channels : (piece + 1) * channels] = values
-
-    tile = tile_scratch[...]
+    for a in range(3):
+        for piece in range(9):
+            at = (a * 9 + piece) * channels
+            lanes = slice(piece * channels, (piece + 1) * channels)
+            values = wide_ref[0, at : at + channels, :].astype(BF16)
+            w_first_ref[a, piece] = values
+            wl_first_ref[a, :, lanes] = values
+            values = wide_ref[1, at : at + channels, :].astype(BF16)
+            w_second_ref[a, piece] = values
+            wl_second_ref[a, :, lanes] = values
+
+    tile = tile_ref[...]
     first = tile / (1.0 + jnp.exp(-tile))
-
-    def store_x(index):
-        def store(low, high, piece, values):
-            lanes = slice(piece * channels, (piece + 1) * channels)
-            x_scratch[index, 2:, low:high, :, lanes] = values
-            x_scratch[index, 0, low:high, :, lanes] = values[0]
-            x_scratch[index, 1, low:high, :, lanes] = values[0]
-
-        return store
-
-    def store_g(low, high, piece, values):
-        lanes = slice(piece * channels, (piece + 1) * channels)
-        g_scratch[:, low:high, :, lanes] = values
-
-    spread(first, store_x(0), False)
-
-    for t in range(frames):
-        keep = t < length
-        up_scratch[1, t, pl.ds(my_row, band_rows)] = jnp.where(
-            keep, cot_mine_ref[t].astype(F32), 0.0
-        ).astype(BF16)
-        up_scratch[1, t, pl.ds(other_row, band_rows)] = jnp.where(
-            keep, cot_other_ref[t].astype(F32), 0.0
-        ).astype(BF16)
+    spread(first, store_columns(x_scratch, 0, frames, channels), False)
+
+    end = side * (base + columns) + LABEL_ROWS
+    band = (frames, band_rows, columns, channels)
+    for block, row in ((blocks_mine[0], my_row), (blocks_other[0], other_row)):
+        cot = block[end:, :].reshape(band)
+        for t in range(frames):
+            up_scratch[1, t, pl.ds(row, band_rows)] = jnp.where(
+                t < length, cot[t].astype(F32), 0.0
+            ).astype(BF16)
+    out_grad_ref[...] = up_scratch[1]
 
     act = jnp.zeros((cells, channels), F32)
     for a in range(3):
         act = act + jnp.dot(
             x_scratch[0, a : a + frames].reshape(cells, nine),
-            w_scratch[0, a].reshape(nine, channels),
+            w_first_ref[a].reshape(nine, channels),
             preferred_element_type=F32,
         )
     act = act.astype(BF16).reshape(frames, rows, columns, channels)
     act_scratch[...] = act
     act = act.astype(F32)
     second = act / (1.0 + jnp.exp(-act))
-    spread(second, store_x(1), False)
-
-    out_grad = up_scratch[1].astype(F32)
-    spread(out_grad, store_g, True)
-    nt = (((1,), (1,)), ((), ()))
-    sum_scratch[...] = jnp.zeros(sum_scratch.shape, F32)
-    for a in range(3):
-        part = lax.dot_general(
-            g_scratch[...].reshape(cells, nine),
-            wl_scratch[1, a],
-            nt,
-            preferred_element_type=F32,
+    spread(second, store_columns(x_scratch, 1, frames, channels), False)
+
+    @pl.when(core == 0)
+    def _():
+        act_grad_ref[...] = act_gradient(
+            up_scratch[1], act_scratch[...], wl_second_ref, g_scratch, sum_scratch
         )
-        sum_scratch[a : a + frames] += part.reshape(frames, rows, columns, channels)
-    sum_scratch[2] = sum_scratch[0] + sum_scratch[1] + sum_scratch[2]
-    act = act_scratch[...].astype(F32)
-    sig = 1.0 / (1.0 + jnp.exp(-act))
-    act_grad = (sum_scratch[2:] * (sig * (1.0 + act * (1.0 - sig)))).astype(BF16)
-    up_scratch[0] = act_grad
+        up_scratch[0] = act_grad_ref[...]
 
     upstream = up_scratch[core].reshape(cells, channels).astype(F32).T.astype(BF16)
     for a in range(3):
@@ -426,64 +483,114 @@
             start = pl.multiple_of(owner * share, 8)
             outs[k][j] = wide_ref[0, pl.ds(start, share), :].astype(BF16)
 
-    half = frames * band_rows * columns
-    band = (frames, band_rows, columns, channels)
-    out = jnp.zeros((half, channels), F32)
+
+def unit(length, blocks_mine, blocks_other, band, scale, share):
+    frames, band_rows, columns, channels = band
+    rows = 2 * band_rows
+    side = len(blocks_mine)
+    field = (frames, rows, columns, channels)
+    part = jax.ShapeDtypeStruct((side, share, channels), BF16)
+    flops = 2 * 27 * channels * channels * frames * rows * columns * 3
+    outs = pl.pallas_call(
+        functools.partial(unit_kernel, scale=scale, side=side, share=share),
+        out_shape=[
+            jax.ShapeDtypeStruct(field, F32),
+            jax.ShapeDtypeStruct(field, BF16),
+            jax.ShapeDtypeStruct(field, BF16),
+            jax.ShapeDtypeStruct(field, BF16),
+            jax.ShapeDtypeStruct((3, 9, channels, channels), BF16),
+            jax.ShapeDtypeStruct((3, channels, 9 * channels), BF16),
+            jax.ShapeDtypeStruct((3, channels, 9 * channels), BF16),
+        ]
+        + [part] * side,
+        in_specs=scalars(1) + whole(2 * side),
+        out_specs=whole(7 + side),
+        scratch_shapes=[
+            pltpu.VMEM((2, 27 * channels, channels), F32),
+            pltpu.VMEM((3, 9, channels, channels), BF16),
+            pltpu.VMEM((2, frames + 2, rows, columns, 9 * channels), BF16),
+            pltpu.VMEM((frames, rows, columns, 9 * channels), BF16),
+            pltpu.VMEM((2,) + field, BF16),
+            pltpu.VMEM((frames + 2, rows, columns, channels), F32),
+        ],
+        compiler_params=pltpu.CompilerParams(vmem_limit_bytes=36 * 1024 * 1024),
+        cost_estimate=pl.CostEstimate(flops=flops, bytes_accessed=4_000_000, transcendentals=0),
+    )(length, *blocks_mine, *blocks_other)
+    return outs[:7], outs[7:]
+
+
+def finish_kernel(
+    tile_ref,
+    act_ref,
+    out_grad_ref,
+    act_grad_ref,
+    w_second_ref,
+    wl_first_ref,
+    wl_second_ref,
+    block_ref,
+    grad_ref,
+    x_scratch,
+    g_scratch,
+    up_scratch,
+    full_scratch,
+    sum_scratch,
+):
+    frames, band_rows, columns, channels = block_ref.shape
+    nine = 9 * channels
+    cells = frames * band_rows * columns
+    core = lax.axis_index("rows")
+    my_row = core * band_rows
+    tile = tile_ref[:, pl.ds(my_row, band_rows)]
+
+    act = act_ref[...].astype(F32)
+    second = act / (1.0 + jnp.exp(-act))
+    spread(second, store_columns(x_scratch, 0, frames, channels), False)
+    out = jnp.zeros((cells, channels), F32)
     for a in range(3):
         out = out + jnp.dot(
-            x_scratch[1, a : a + frames, pl.ds(my_row, band_rows)].reshape(half, nine),
-            w_scratch[1, a].reshape(nine, channels),
+            x_scratch[0, a : a + frames, pl.ds(my_row, band_rows)].reshape(cells, nine),
+            w_second_ref[a].reshape(nine, channels),
             preferred_element_type=F32,
         )
-    my_tile = tile_scratch[:, pl.ds(my_row, band_rows)]
-    block_ref[...] = (my_tile + out.reshape(band)).astype(BF16)
-
-    spread(act_grad.astype(F32), store_g, True)
-    sum_scratch[:, :band_rows] = jnp.zeros((sum_scratch.shape[0],) + band[1:], F32)
-    for a in range(3):
-        part = lax.dot_general(
-            g_scratch[:, pl.ds(my_row, band_rows)].reshape(half, nine),
-            wl_scratch[0, a],
-            nt,
-            preferred_element_type=F32,
+    block_ref[...] = (tile + out.reshape(block_ref.shape)).astype(BF16)
+
+    @pl.when(core == 0)
+    def _():
+        up_scratch[...] = act_grad_ref[...]
+
+    @pl.when(core != 0)
+    def _():
+        up_scratch[...] = act_gradient(
+            out_grad_ref[...], act_ref[...], wl_second_ref, g_scratch, full_scratch
         )
-        sum_scratch[a : a + frames, :band_rows] += part.reshape(band)
-    sum_scratch[2, :band_rows] = (
-        sum_scratch[0, :band_rows] + sum_scratch[1, :band_rows] + sum_scratch[2, :band_rows]
-    )
-    sig = 1.0 / (1.0 + jnp.exp(-my_tile))
-    slope = sig * (1.0 + my_tile * (1.0 - sig))
-    my_up = up_scratch[1, :, pl.ds(my_row, band_rows)].astype(F32)
-    grad_ref[...] = (my_up + sum_scratch[2:, :band_rows] * slope).astype(BF16)
-
-
-def unit(length, blocks_mine, blocks_other, cots, scale, share):
-    frames, band_rows, columns, channels = cots[0].shape
-    rows = 2 * band_rows
-    side = len(blocks_mine)
-    band = jax.ShapeDtypeStruct(cots[0].shape, BF16)
-    part = jax.ShapeDtypeStruct((side, share, channels), BF16)
-    flops = 2 * 27 * channels * channels * frames * rows * columns * 4
-    outs = pl.pallas_call(
-        functools.partial(unit_kernel, scale=scale, side=side, share=share),
-        out_shape=[band, band] + [part] * side,
-        in_specs=scalars(1) + whole(2 * side + 2),
-        out_specs=whole(2 + side),
+
+    spread(up_scratch[...].astype(F32), store_plain(g_scratch, channels), True)
+    data_grad(g_scratch[:, pl.ds(my_row, band_rows)], wl_first_ref, sum_scratch)
+    sig = 1.0 / (1.0 + jnp.exp(-tile))
+    slope = sig * (1.0 + tile * (1.0 - sig))
+    upstream = out_grad_ref[:, pl.ds(my_row, band_rows)].astype(F32)
+    grad_ref[...] = (upstream + sum_scratch[2:] * slope).astype(BF16)
+
+
+def finish(kept):
+    frames, rows, columns, channels = kept[0].shape
+    band = jax.ShapeDtypeStruct((frames, rows // 2, columns, channels), BF16)
+    flops = 2 * 27 * channels * channels * frames * rows * columns
+    return pl.pallas_call(
+        finish_kernel,
+        out_shape=[band] * 2,
+        in_specs=whole(len(kept)),
+        out_specs=whole(2),
         scratch_shapes=[
-            pltpu.VMEM((2, 27 * channels, channels), F32),
-            pltpu.VMEM((2, 3, 9, channels, channels), BF16),
-            pltpu.VMEM((2, 3, channels, 9 * channels), BF16),
-            pltpu.VMEM((frames, rows, columns, channels), F32),
+            pltpu.VMEM((1, frames + 2, rows, columns, 9 * channels), BF16),
+            pltpu.VMEM((frames, rows, columns, 9 * channels), BF16),
             pltpu.VMEM((frames, rows, columns, channels), BF16),
-            pltpu.VMEM((2, frames + 2, rows, columns, 9 * channels), BF16),
-            pltpu.VMEM((frames, rows, columns, 9 * channels), BF16),
-            pltpu.VMEM((2, frames, rows, columns, channels), BF16),
             pltpu.VMEM((frames + 2, rows, columns, channels), F32),
+            pltpu.VMEM((frames + 2, rows // 2, columns, channels), F32),
         ],
-        compiler_params=pltpu.CompilerParams(vmem_limit_bytes=48 * 1024 * 1024),
-        cost_estimate=pl.CostEstimate(flops=flops, bytes_accessed=4_000_000, transcendentals=0),
-    )(length, *blocks_mine, *blocks_other, *cots)
-    return outs[0], outs[1], outs[2:]
+        compiler_params=pltpu.CompilerParams(vmem_limit_bytes=20 * 1024 * 1024),
+        cost_estimate=pl.CostEstimate(flops=flops, bytes_accessed=2_000_000, transcendentals=0),
+    )(*kept)
 
 
 def total_of(refs, at):
@@ -498,7 +605,7 @@
     core, high, low = position(side)
     p, _ = walk(core, high, low)
     for k in range(side):
-        refs[side + k][...] = total_of(refs[:side], jnp.bitwise_xor(p, k)).astype(BF16)
+        refs[side + k][...] = total_of(refs[:side][::-1], jnp.bitwise_xor(p, k)).astype(BF16)
 
 
 def middle(parts):
@@ -508,11 +615,12 @@
         out_shape=[jax.ShapeDtypeStruct(parts[0].shape[1:], BF16)] * side,
         in_specs=whole(side),
         out_specs=whole(side),
-    )(*parts)
+        compiler_params=SMALL,
+    )(*parts[::-1])
 
 
 def last_kernel(*refs):
-    refs[-1][...] = total_of(refs[:-1], ...)
+    refs[-1][...] = total_of(refs[:-1][::-1], ...)
 
 
 def last(parts):
@@ -521,7 +629,8 @@
         out_shape=jax.ShapeDtypeStruct(parts[0].shape, F32),
         in_specs=whole(len(parts)),
         out_specs=whole(1)[0],
-    )(*parts)
+        compiler_params=SMALL,
+    )(*parts[::-1])
 
 
 def body_pair(slabs, dest, pos, lengths, cot, w_first, w_second):
@@ -535,29 +644,34 @@
     def exchange(block):
         return lax.ppermute(block, "rows", [(0, 1), (1, 0)])
 
-    def pairs(step, k):
+    def pairs(axes, k):
         both = []
         for chip in range(wide_size):
             high, low = chip // side, chip % side
-            to_high, to_low = (high ^ k) * side + low, high * side + (low ^ k)
-            targets = (to_high, to_low) if step == 0 else (to_low, to_high)
-            both += [(chip * 2 + c, targets[c] * 2 + c) for c in range(2)]
+            targets = ((high ^ k) * side + low, high * side + (low ^ k))
+            both += [(chip * 2 + c, targets[axes[c]] * 2 + c) for c in range(2)]
         return both
 
-    def send(blocks, step):
-        sent = [lax.ppermute(blocks[k], ("wide", "rows"), pairs(step, k)) for k in range(1, side)]
-        return [blocks[0]] + sent
+    def send(blocks, axes):
+        sent = [
+            lax.ppermute(blocks[k], ("wide", "rows"), pairs(axes, k))
+            for k in range(side - 1, 0, -1)
+        ]
+        return [blocks[0]] + sent[::-1]
 
     packed = pack(dest[0, 0], pos[0, 0], slabs[0, 0], w_first, w_second, side)
-    relayed = relay(send(packed, 0), columns, base)
-    blocks_mine = send(relayed, 1)
+    _, *arrived = send(packed, (0, 1))
+    relayed = relay(cot[0], [keep(packed[0]), *arrived], columns, base)
+    blocks_mine = send(relayed, (1, 0))
     blocks_other = [exchange(block) for block in blocks_mine]
-    cots = (cot[0], exchange(cot[0]))
 
     scale = 1.0 / math.sqrt(frames * band_rows * columns * 2 * wide_size)
-    block_out, grad_input, parts = unit(lengths, blocks_mine, blocks_other, cots, scale, share)
-
-    total = last(send(middle(send(parts, 1)), 0))
+    kept, parts = unit(lengths, blocks_mine, blocks_other, cot.shape[1:], scale, share)
+    block_out, grad_input = finish(kept)
+
+    arrived = send(parts, (1, 0))
+    *arrived, block_out, grad_input = lax.optimization_barrier((*arrived, block_out, grad_input))
+    total = last(send(middle(arrived), (0, 1)))
     total_other = exchange(total)
     share_first = jnp.where(core == 0, total, total_other)
     share_second = jnp.where(core == 0, total_other, total)

time: 65.1 us -> 52.2 us (0.80)
  waiting for transfers between devices: 26 us -> 20.2 us
  Pallas kernels: 14.7 us -> 11 us
  local copies, waits for them, and re-layouts: 3.59 us -> 0.89 us
  other arithmetic: 1.59 us -> 0.7 us
    ppermute x12, waiting for transfers between devices: 23.7 us -> 18.1 us  [send(): lax.ppermute(blocks[k], ('wide', 'rows'), pairs(axes, k))]
    unnamed x24 -> x4, local copies, waits for them, and re-layouts: 3.59 us -> 0.89 us
    pallas_call x0 -> x2, Pallas kernels: none -> 2.54 us  [the longest x1 2.53 us: finish(): pl.pallas_call(finish_kernel, out_shape=[band] * 2, in_specs=whole(len(ke...]
    pallas_call x1, Pallas kernels: 2.18 us -> 0.15 us  [relay(): pl.pallas_call(functools.partial(relay_kernel, columns=columns, base=base...]
    pallas_call x1, Pallas kernels: 2.01 us -> 0.11 us  [middle(): pl.pallas_call(middle_kernel, out_shape=[jax.ShapeDtypeStruct(parts[0].sh...]
    pallas_call x1, Pallas kernels: 1.57 us -> 0.03 us  [last(): pl.pallas_call(last_kernel, out_shape=jax.ShapeDtypeStruct(parts[0].shape...]
    pallas_call x1, Pallas kernels: 6.97 us -> 5.51 us  [unit(): pl.pallas_call(functools.partial(unit_kernel, scale=scale, side=side, sha...]
    select_n x1, other arithmetic: 1.59 us -> 0.7 us  [body_pair(): share_second = jnp.where(core == 0, total_other, total)]
  transfers between devices with their start and end apart: 18 -> 17, of which waited for: 12 -> 13; matrix products, arithmetic and copies ran while one was open for 0% -> 0% of each run, Pallas kernels for 0% -> 5%
where the time goes in v3:
time: 52.2 us; the launch traced here: 52 us
  waiting for transfers between devices  20.2 us (39%)
  starting transfers between devices  17.8 us (34%)
  Pallas kernels  11 us (21%)
  between operations  1.36 us (3%)
  local copies, waits for them, and re-layouts  0.89 us (2%)
  other arithmetic  0.7 us (1%)
    ppermute x12, waiting for transfers between devices, send(): lax.ppermute(blocks[k], ('wide', 'rows'), pairs(axes, k))  18.1 us
    ppermute x12, starting transfers between devices, send(): lax.ppermute(blocks[k], ('wide', 'rows'), pairs(axes, k))  17.8 us
    pallas_call x1, Pallas kernels, unit(): pl.pallas_call(functools.partial(unit_kernel, scale=scale, side=side, sha...  5.51 us
    pallas_call x1, Pallas kernels, pack(): pl.pallas_call(pack_kernel, out_shape=[jax.ShapeDtypeStruct((rows, channe...  2.61 us
    pallas_call x1, Pallas kernels, finish(): pl.pallas_call(finish_kernel, out_shape=[band] * 2, in_specs=whole(len(ke...  2.53 us
    ppermute x5, waiting for transfers between devices, exchange(): return lax.ppermute(block, 'rows', [(0, 1), (1, 0)])  2.17 us
  transfers between devices with their start and end apart: 17, of which 13 were waited for; matrix products, arithmetic and copies ran while one was open for 0% of the time, Pallas kernels for 5%

profile of v3, /device:TPU:0, one launch (start us, length us, event | category | flops | bytes accessed | tf_op | source)
XLA Modules:
  0.0 52.0 jit_solution(11468963735133308367)
XLA Ops:
  0.6 2.6 %shard_map.102 = (bf16[368,128]{1,0:T(8,128)(2,1)}, bf16[368,128]{1,0:T(8,128)(2,1)}, bf16[368,128]{1,0:T(8,128)(2,1)}, bf16[368,128]{1,0:T(8,128)(2,1)}) custom-call(s32[10]{0:T(128)} %bitcast.8, s32[10]{0:T(128)} %bitcast.9, bf16[10,32,128]{2,1,0:T(8,128)(2,1)} %bitcast.7, bf16[216,128]{1,0:T(8,128)(2,1)} %first_hbm.1, bf16[216,128]{1,0:T(8,128)(2,1)} %second_hbm.1), custom_call_target="tpu_custom_call" | custom-call | tf_op jit(solution)/shard_map/pallas_call | solution.py:229
  3.3 5.1 %collective-permute-start = (bf16[368,128]{1,0:T(8,128)(2,1)}, bf16[368,128]{1,0:T(8,128)(2,1)S(1)}, u32[]{:S(2)}, u32[]{:S(2)}) collective-permute-start(bf16[368,128]{1,0:T(8,128)(2,1)} %get-tuple-element.35), channel_id=1, source_target_pairs={{0,24},{1,7},{2,26},{3,5},{4,28},{5,3},{6,30},{7,1},{8,16},{9,15},... | collective-permute-start | bytes 282632 | tf_op jit(solution)/shard_map/ppermute | solution.py:657
  8.4 0.0 collective-permute-start.1
  8.4 0.6 %collective-permute-start.2 = (bf16[368,128]{1,0:T(8,128)(2,1)}, bf16[368,128]{1,0:T(8,128)(2,1)S(1)}, u32[]{:S(2)}, u32[]{:S(2)}) collective-permute-start(bf16[368,128]{1,0:T(8,128)(2,1)} %get-tuple-element.37), channel_id=1, source_target_pairs={{0,8},{1,3},{2,10},{3,1},{4,12},{5,7},{6,14},{7,5},{8,0},{9,11},{1... | collective-permute-start | bytes 282632 | tf_op jit(solution)/shard_map/ppermute | solution.py:657
  9.0 0.0 copy-start
  9.0 0.9 %copy-done = bf16[368,128]{1,0:T(8,128)(2,1)S(1)} copy-done((bf16[368,128]{1,0:T(8,128)(2,1)S(1)}, bf16[368,128]{1,0:T(8,128)(2,1)}, u32[]{:S(2)}) %copy-start) | copy-done | bytes 94232
  9.9 0.0 copy-start.1
  9.9 1.3 %collective-permute-done.refs_0_ = bf16[368,128]{1,0:T(8,128)(2,1)S(1)} collective-permute-done((bf16[368,128]{1,0:T(8,128)(2,1)}, bf16[368,128]{1,0:T(8,128)(2,1)S(1)}, u32[]{:S(2)}, u32[]{:S(2)}) %collective-permute-start) | collective-permute-done | bytes 94240 | tf_op jit(solution)/shard_map/ppermute | solution.py:657
  11.2 2.9 %collective-permute-done.1.refs_1_ = bf16[368,128]{1,0:T(8,128)(2,1)S(1)} collective-permute-done((bf16[368,128]{1,0:T(8,128)(2,1)}, bf16[368,128]{1,0:T(8,128)(2,1)S(1)}, u32[]{:S(2)}, u32[]{:S(2)}) %collective-permute-start.1) | collective-permute-done | bytes 94240 | tf_op jit(solution)/shard_map/ppermute | solution.py:657
  14.2 0.0 collective-permute-done.2.refs_2_
  14.2 0.0 copy-done.1
  14.2 0.1 shard_map.104
  14.3 1.6 %collective-permute-start.3 = (bf16[1040,128]{1,0:T(8,128)(2,1)S(1)}, bf16[1040,128]{1,0:T(8,128)(2,1)S(1)}, u32[]{:S(2)}, u32[]{:S(2)}) collective-permute-start(bf16[1040,128]{1,0:T(8,128)(2,1)S(1)} %get-tuple-element.40), channel_id=1, source_target_pairs={{0,2},{1,9},{2,0},{3,11},{4,6},{5,13},{6,4},{7,15},{8,10},{9,1},{1... | collective-permute-start | bytes 798728 | tf_op jit(solution)/shard_map/ppermute | solution.py:657
  15.9 2.1 %collective-permute-start.4 = (bf16[1040,128]{1,0:T(8,128)(2,1)S(1)}, bf16[1040,128]{1,0:T(8,128)(2,1)S(1)}, u32[]{:S(2)}, u32[]{:S(2)}) collective-permute-start(bf16[1040,128]{1,0:T(8,128)(2,1)S(1)} %get-tuple-element.41), channel_id=1, source_target_pairs={{0,4},{1,17},{2,6},{3,19},{4,0},{5,21},{6,2},{7,23},{8,12},{9,25},... | collective-permute-start | bytes 798728 | tf_op jit(solution)/shard_map/ppermute | solution.py:657
  18.0 0.0 collective-permute-start.5
  18.0 0.0 collective-permute-start.6
  18.0 2.8 %collective-permute-done.3.refs_1_ = bf16[1040,128]{1,0:T(8,128)(2,1)S(1)} collective-permute-done((bf16[1040,128]{1,0:T(8,128)(2,1)S(1)}, bf16[1040,128]{1,0:T(8,128)(2,1)S(1)}, u32[]{:S(2)}, u32[]{:S(2)}) %collective-permute-start.3) | collective-permute-done | bytes 266272 | tf_op jit(solution)/shard_map/ppermute | solution.py:657
  20.8 0.0 collective-permute-start.7
  20.8 4.0 %collective-permute-done.4.refs_2_ = bf16[1040,128]{1,0:T(8,128)(2,1)S(1)} collective-permute-done((bf16[1040,128]{1,0:T(8,128)(2,1)S(1)}, bf16[1040,128]{1,0:T(8,128)(2,1)S(1)}, u32[]{:S(2)}, u32[]{:S(2)}) %collective-permute-start.4) | collective-permute-done | bytes 266272 | tf_op jit(solution)/shard_map/ppermute | solution.py:657
  24.8 0.0 collective-permute-start.8
  24.8 0.5 %collective-permute-done.5.refs_3_ = bf16[1040,128]{1,0:T(8,128)(2,1)S(1)} collective-permute-done((bf16[1040,128]{1,0:T(8,128)(2,1)S(1)}, bf16[1040,128]{1,0:T(8,128)(2,1)S(1)}, u32[]{:S(2)}, u32[]{:S(2)}) %collective-permute-start.5) | collective-permute-done | bytes 266272 | tf_op jit(solution)/shard_map/ppermute | solution.py:657
  25.3 0.0 collective-permute-start.9
  26.0 0.0 collective-permute-done.6.refs_4_
  26.0 0.0 collective-permute-done.7.refs_5_
  26.0 0.3 collective-permute-done.8.refs_6_
  26.3 0.5 %collective-permute-done.9.refs_7_ = bf16[1040,128]{1,0:T(8,128)(2,1)S(1)} collective-permute-done((bf16[1040,128]{1,0:T(8,128)(2,1)S(1)}, bf16[1040,128]{1,0:T(8,128)(2,1)S(1)}, u32[]{:S(2)}, u32[]{:S(2)}) %collective-permute-start.9) | collective-permute-done | bytes 266272 | tf_op jit(solution)/shard_map/ppermute | solution.py:645
  26.9 5.5 %shard_map.105 = (f32[5,4,32,128]{3,2,1,0:T(8,128)S(1)}, bf16[5,4,32,128]{3,2,1,0:T(8,128)(2,1)S(1)}, bf16[5,4,32,128]{3,2,1,0:T(8,128)(2,1)S(1)}, bf16[5,4,32,1...) custom-call(s32[1]{0:T(128)S(6)} %copy.11.length_ref, ...), custom_call_target="tpu_custom_call" | custom-call | flops 1698693120 | bytes 4000000 | tf_op jit(solution)/shard_map/pallas_call | solution.py:494
  32.4 1.5 %collective-permute-start.10 = (bf16[4,216,128]{2,1,0:T(8,128)(2,1)S(1)}, bf16[4,216,128]{2,1,0:T(8,128)(2,1)S(1)}, u32[]{:S(2)}, u32[]{:S(2)}) collective-permute-start(bf16[4,216,128]{2,1,0:T(8,128)(2,1)S(1)} %get-tuple-element.44), channel_id=1, source_target_pairs={{0,2},{1,9},{2,0},{3,11},{4,6},{5,13},{6,4},{7,15},{8,10},{9,1},{1... | collective-permute-start | bytes 663560 | tf_op jit(solution)/shard_map/ppermute | solution.py:657
  33.8 1.0 %collective-permute-start.11 = (bf16[4,216,128]{2,1,0:T(8,128)(2,1)S(1)}, bf16[4,216,128]{2,1,0:T(8,128)(2,1)S(1)}, u32[]{:S(2)}, u32[]{:S(2)}) collective-permute-start(bf16[4,216,128]{2,1,0:T(8,128)(2,1)S(1)} %get-tuple-element.45), channel_id=1, source_target_pairs={{0,4},{1,17},{2,6},{3,19},{4,0},{5,21},{6,2},{7,23},{8,12},{9,25},... | collective-permute-start | bytes 663560 | tf_op jit(solution)/shard_map/ppermute | solution.py:657
  34.9 1.4 %collective-permute-start.12 = (bf16[4,216,128]{2,1,0:T(8,128)(2,1)S(1)}, bf16[4,216,128]{2,1,0:T(8,128)(2,1)S(1)}, u32[]{:S(2)}, u32[]{:S(2)}) collective-permute-start(bf16[4,216,128]{2,1,0:T(8,128)(2,1)S(1)} %get-tuple-element.46), channel_id=1, source_target_pairs={{0,6},{1,25},{2,4},{3,27},{4,2},{5,29},{6,0},{7,31},{8,14},{9,17},... | collective-permute-start | bytes 663560 | tf_op jit(solution)/shard_map/ppermute | solution.py:657
  36.2 2.5 %shard_map.106 = (bf16[5,2,32,128]{3,2,1,0:T(8,128)(2,1)}, bf16[5,2,32,128]{3,2,1,0:T(8,128)(2,1)}) custom-call(f32[5,4,32,128]{3,2,1,0:T(8,128)S(1)} %get-tuple-element.47.tile_ref, bf16[5,4,32,128]{3,2,1,0:T(8,128)(2,1)S(1)} %get-tuple-element.48.act_ref, bf16[5,4,32,128]{3,2,1,0:T(8,128)(2,1)S(1)} %get-tuple-element.49.out_grad_ref, ...), custom_call_target="tpu_custom_call" | custom-call | flops 566231040 | bytes 2000000 | tf_op jit(solution)/shard_map/pallas_call | solution.py:579
  38.8 0.0 collective-permute-done.10.refs_2_
  38.8 1.9 %collective-permute-done.11.refs_1_ = bf16[4,216,128]{2,1,0:T(8,128)(2,1)S(1)} collective-permute-done((bf16[4,216,128]{2,1,0:T(8,128)(2,1)S(1)}, bf16[4,216,128]{2,1,0:T(8,128)(2,1)S(1)}, u32[]{:S(2)}, u32[]{:S(2)}) %collective-permute-start.11) | collective-permute-done | bytes 221216 | tf_op jit(solution)/shard_map/ppermute | solution.py:657
  40.7 1.8 %collective-permute-done.12.refs_0_ = bf16[4,216,128]{2,1,0:T(8,128)(2,1)S(1)} collective-permute-done((bf16[4,216,128]{2,1,0:T(8,128)(2,1)S(1)}, bf16[4,216,128]{2,1,0:T(8,128)(2,1)S(1)}, u32[]{:S(2)}, u32[]{:S(2)}) %collective-permute-start.12) | collective-permute-done | bytes 221216 | tf_op jit(solution)/shard_map/ppermute | solution.py:657
  42.5 0.1 shard_map.107
  42.6 1.6 %collective-permute-start.13 = (bf16[216,128]{1,0:T(8,128)(2,1)S(1)}, bf16[216,128]{1,0:T(8,128)(2,1)S(1)}, u32[]{:S(2)}, u32[]{:S(2)}) collective-permute-start(bf16[216,128]{1,0:T(8,128)(2,1)S(1)} %get-tuple-element.62), channel_id=1, source_target_pairs={{0,24},{1,7},{2,26},{3,5},{4,28},{5,3},{6,30},{7,1},{8,16},{9,15},... | collective-permute-start | bytes 165896 | tf_op jit(solution)/shard_map/ppermute | solution.py:657
  44.2 1.4 %collective-permute-start.14 = (bf16[216,128]{1,0:T(8,128)(2,1)S(1)}, bf16[216,128]{1,0:T(8,128)(2,1)S(1)}, u32[]{:S(2)}, u32[]{:S(2)}) collective-permute-start(bf16[216,128]{1,0:T(8,128)(2,1)S(1)} %get-tuple-element.63), channel_id=1, source_target_pairs={{0,16},{1,5},{2,18},{3,7},{4,20},{5,1},{6,22},{7,3},{8,24},{9,13},... | collective-permute-start | bytes 165896 | tf_op jit(solution)/shard_map/ppermute | solution.py:657
  45.6 1.5 %collective-permute-start.15 = (bf16[216,128]{1,0:T(8,128)(2,1)S(1)}, bf16[216,128]{1,0:T(8,128)(2,1)S(1)}, u32[]{:S(2)}, u32[]{:S(2)}) collective-permute-start(bf16[216,128]{1,0:T(8,128)(2,1)S(1)} %get-tuple-element.64), channel_id=1, source_target_pairs={{0,8},{1,3},{2,10},{3,1},{4,12},{5,7},{6,14},{7,5},{8,0},{9,11},{1... | collective-permute-start | bytes 165896 | tf_op jit(solution)/shard_map/ppermute | solution.py:657
  47.1 1.6 %collective-permute-done.13.refs_0_ = bf16[216,128]{1,0:T(8,128)(2,1)S(1)} collective-permute-done((bf16[216,128]{1,0:T(8,128)(2,1)S(1)}, bf16[216,128]{1,0:T(8,128)(2,1)S(1)}, u32[]{:S(2)}, u32[]{:S(2)}) %collective-permute-start.13) | collective-permute-done | bytes 55328 | tf_op jit(solution)/shard_map/ppermute | solution.py:657
  48.6 0.6 %collective-permute-done.14.refs_1_ = bf16[216,128]{1,0:T(8,128)(2,1)S(1)} collective-permute-done((bf16[216,128]{1,0:T(8,128)(2,1)S(1)}, bf16[216,128]{1,0:T(8,128)(2,1)S(1)}, u32[]{:S(2)}, u32[]{:S(2)}) %collective-permute-start.14) | collective-permute-done | bytes 55328 | tf_op jit(solution)/shard_map/ppermute | solution.py:657
  49.3 0.6 %collective-permute-done.15.refs_2_ = bf16[216,128]{1,0:T(8,128)(2,1)S(1)} collective-permute-done((bf16[216,128]{1,0:T(8,128)(2,1)S(1)}, bf16[216,128]{1,0:T(8,128)(2,1)S(1)}, u32[]{:S(2)}, u32[]{:S(2)}) %collective-permute-start.15) | collective-permute-done | bytes 55328 | tf_op jit(solution)/shard_map/ppermute | solution.py:657
  49.9 0.1 collective-permute-start.16
  50.0 1.3 %collective-permute-done.16 = f32[216,128]{1,0:T(8,128)S(1)} collective-permute-done((f32[216,128]{1,0:T(8,128)S(1)}, f32[216,128]{1,0:T(8,128)S(1)}, u32[]{:S(2)}, u32[]{:S(2)}) %collective-permute-start.16) | collective-permute-done | bytes 110624 | tf_op jit(solution)/shard_map/ppermute | solution.py:645
  51.3 0.7 %broadcast_select_fusion = (f32[216,128]{1,0:T(8,128)}, f32[216,128]{1,0:T(8,128)}) fusion(f32[216,128]{1,0:T(8,128)S(1)} %collective-permute-done.16, f32[216,128]{1,0:T(8,128)S(1)} %shard_map.108, pred[]{:T(512)S(6)} %eq.4), kind=kLoop, calls=%fused_computation | loop fusion | flops 55296 | bytes 442369 | tf_op jit(solution)/shard_map/jit(_where)/select_n | solution.py:677
  (2 shorter events, 0.0 us)
Async XLA Ops:
  3.3 8.0 %collective-permute-start = (bf16[368,128]{1,0:T(8,128)(2,1)}, bf16[368,128]{1,0:T(8,128)(2,1)S(1)}, u32[]{:S(2)}, u32[]{:S(2)}) collective-permute-start(bf16[368,128]{1,0:T(8,128)(2,1)} %get-tuple-element.35), channel_id=1, source_target_pairs={{0,24},{1,7},{2,26},{3,5},{4,28},{5,3},{6,30},{7,1},{8,16},{9,15},... | collective-permute-start | bytes 282632 | tf_op jit(solution)/shard_map/ppermute | solution.py:657
  8.4 5.8 %collective-permute-start.1 = (bf16[368,128]{1,0:T(8,128)(2,1)}, bf16[368,128]{1,0:T(8,128)(2,1)S(1)}, u32[]{:S(2)}, u32[]{:S(2)}) collective-permute-start(bf16[368,128]{1,0:T(8,128)(2,1)} %get-tuple-element.36), channel_id=1, source_target_pairs={{0,16},{1,5},{2,18},{3,7},{4,20},{5,1},{6,22},{7,3},{8,24},{9,13},... | collective-permute-start | bytes 282632 | tf_op jit(solution)/shard_map/ppermute | solution.py:657
  8.4 5.8 %collective-permute-start.2 = (bf16[368,128]{1,0:T(8,128)(2,1)}, bf16[368,128]{1,0:T(8,128)(2,1)S(1)}, u32[]{:S(2)}, u32[]{:S(2)}) collective-permute-start(bf16[368,128]{1,0:T(8,128)(2,1)} %get-tuple-element.37), channel_id=1, source_target_pairs={{0,8},{1,3},{2,10},{3,1},{4,12},{5,7},{6,14},{7,5},{8,0},{9,11},{1... | collective-permute-start | bytes 282632 | tf_op jit(solution)/shard_map/ppermute | solution.py:657
  9.0 0.9 %copy-start = (bf16[368,128]{1,0:T(8,128)(2,1)S(1)}, bf16[368,128]{1,0:T(8,128)(2,1)}, u32[]{:S(2)}) copy-start(bf16[368,128]{1,0:T(8,128)(2,1)} %get-tuple-element.38.in_ref) | copy-start | bytes 282628
  9.9 4.3 %copy-start.1 = (bf16[1,5,2,32,128]{4,3,2,1,0:T(8,128)(2,1)S(1)}, bf16[1,5,2,32,128]{4,3,2,1,0:T(8,128)(2,1)}, u32[]{:S(2)}) copy-start(bf16[1,5,2,32,128]{4,3,2,1,0:T(8,128)(2,1)} %param.11) | copy-start | bytes 245764
  14.3 6.5 %collective-permute-start.3 = (bf16[1040,128]{1,0:T(8,128)(2,1)S(1)}, bf16[1040,128]{1,0:T(8,128)(2,1)S(1)}, u32[]{:S(2)}, u32[]{:S(2)}) collective-permute-start(bf16[1040,128]{1,0:T(8,128)(2,1)S(1)} %get-tuple-element.40), channel_id=1, source_target_pairs={{0,2},{1,9},{2,0},{3,11},{4,6},{5,13},{6,4},{7,15},{8,10},{9,1},{1... | collective-permute-start | bytes 798728 | tf_op jit(solution)/shard_map/ppermute | solution.py:657
  15.9 8.9 %collective-permute-start.4 = (bf16[1040,128]{1,0:T(8,128)(2,1)S(1)}, bf16[1040,128]{1,0:T(8,128)(2,1)S(1)}, u32[]{:S(2)}, u32[]{:S(2)}) collective-permute-start(bf16[1040,128]{1,0:T(8,128)(2,1)S(1)} %get-tuple-element.41), channel_id=1, source_target_pairs={{0,4},{1,17},{2,6},{3,19},{4,0},{5,21},{6,2},{7,23},{8,12},{9,25},... | collective-permute-start | bytes 798728 | tf_op jit(solution)/shard_map/ppermute | solution.py:657
  18.0 7.3 %collective-permute-start.5 = (bf16[1040,128]{1,0:T(8,128)(2,1)S(1)}, bf16[1040,128]{1,0:T(8,128)(2,1)S(1)}, u32[]{:S(2)}, u32[]{:S(2)}) collective-permute-start(bf16[1040,128]{1,0:T(8,128)(2,1)S(1)} %get-tuple-element.42), channel_id=1, source_target_pairs={{0,6},{1,25},{2,4},{3,27},{4,2},{5,29},{6,0},{7,31},{8,14},{9,17},... | collective-permute-start | bytes 798728 | tf_op jit(solution)/shard_map/ppermute | solution.py:657
  18.0 8.0 %collective-permute-start.6 = (bf16[1360,128]{1,0:T(8,128)(2,1)S(1)}, bf16[1360,128]{1,0:T(8,128)(2,1)S(1)}, u32[]{:S(2)}, u32[]{:S(2)}) collective-permute-start(bf16[1360,128]{1,0:T(8,128)(2,1)S(1)} %get-tuple-element.39.refs_0_), channel_id=1, source_target_pairs={{0,1},{1,0},{2,3},{3,2},{4,5},{5,4},{6,7},{7,6},{8,9},{9,8},{10,11... | collective-permute-start | bytes 1044488 | tf_op jit(solution)/shard_map/ppermute | solution.py:645
  20.8 5.2 %collective-permute-start.7 = (bf16[1040,128]{1,0:T(8,128)(2,1)S(1)}, bf16[1040,128]{1,0:T(8,128)(2,1)S(1)}, u32[]{:S(2)}, u32[]{:S(2)}) collective-permute-start(bf16[1040,128]{1,0:T(8,128)(2,1)S(1)} %collective-permute-done.3.refs_1_), channel_id=1, source_target_pairs={{0,1},{1,0},{2,3},{3,2},{4,5},{5,4},{6,7},{7,6},{8,9},{9,8},{10,11... | collective-permute-start | bytes 798728 | tf_op jit(solution)/shard_map/ppermute | solution.py:645
  24.8 1.5 %collective-permute-start.8 = (bf16[1040,128]{1,0:T(8,128)(2,1)S(1)}, bf16[1040,128]{1,0:T(8,128)(2,1)S(1)}, u32[]{:S(2)}, u32[]{:S(2)}) collective-permute-start(bf16[1040,128]{1,0:T(8,128)(2,1)S(1)} %collective-permute-done.4.refs_2_), channel_id=1, source_target_pairs={{0,1},{1,0},{2,3},{3,2},{4,5},{5,4},{6,7},{7,6},{8,9},{9,8},{10,11... | collective-permute-start | bytes 798728 | tf_op jit(solution)/shard_map/ppermute | solution.py:645
  25.3 1.5 %collective-permute-start.9 = (bf16[1040,128]{1,0:T(8,128)(2,1)S(1)}, bf16[1040,128]{1,0:T(8,128)(2,1)S(1)}, u32[]{:S(2)}, u32[]{:S(2)}) collective-permute-start(bf16[1040,128]{1,0:T(8,128)(2,1)S(1)} %collective-permute-done.5.refs_3_), channel_id=1, source_target_pairs={{0,1},{1,0},{2,3},{3,2},{4,5},{5,4},{6,7},{7,6},{8,9},{9,8},{10,11... | collective-permute-start | bytes 798728 | tf_op jit(solution)/shard_map/ppermute | solution.py:645
  32.4 6.4 %collective-permute-start.10 = (bf16[4,216,128]{2,1,0:T(8,128)(2,1)S(1)}, bf16[4,216,128]{2,1,0:T(8,128)(2,1)S(1)}, u32[]{:S(2)}, u32[]{:S(2)}) collective-permute-start(bf16[4,216,128]{2,1,0:T(8,128)(2,1)S(1)} %get-tuple-element.44), channel_id=1, source_target_pairs={{0,2},{1,9},{2,0},{3,11},{4,6},{5,13},{6,4},{7,15},{8,10},{9,1},{1... | collective-permute-start | bytes 663560 | tf_op jit(solution)/shard_map/ppermute | solution.py:657
  33.8 6.9 %collective-permute-start.11 = (bf16[4,216,128]{2,1,0:T(8,128)(2,1)S(1)}, bf16[4,216,128]{2,1,0:T(8,128)(2,1)S(1)}, u32[]{:S(2)}, u32[]{:S(2)}) collective-permute-start(bf16[4,216,128]{2,1,0:T(8,128)(2,1)S(1)} %get-tuple-element.45), channel_id=1, source_target_pairs={{0,4},{1,17},{2,6},{3,19},{4,0},{5,21},{6,2},{7,23},{8,12},{9,25},... | collective-permute-start | bytes 663560 | tf_op jit(solution)/shard_map/ppermute | solution.py:657
  34.9 7.7 %collective-permute-start.12 = (bf16[4,216,128]{2,1,0:T(8,128)(2,1)S(1)}, bf16[4,216,128]{2,1,0:T(8,128)(2,1)S(1)}, u32[]{:S(2)}, u32[]{:S(2)}) collective-permute-start(bf16[4,216,128]{2,1,0:T(8,128)(2,1)S(1)} %get-tuple-element.46), channel_id=1, source_target_pairs={{0,6},{1,25},{2,4},{3,27},{4,2},{5,29},{6,0},{7,31},{8,14},{9,17},... | collective-permute-start | bytes 663560 | tf_op jit(solution)/shard_map/ppermute | solution.py:657
  42.6 6.0 %collective-permute-start.13 = (bf16[216,128]{1,0:T(8,128)(2,1)S(1)}, bf16[216,128]{1,0:T(8,128)(2,1)S(1)}, u32[]{:S(2)}, u32[]{:S(2)}) collective-permute-start(bf16[216,128]{1,0:T(8,128)(2,1)S(1)} %get-tuple-element.62), channel_id=1, source_target_pairs={{0,24},{1,7},{2,26},{3,5},{4,28},{5,3},{6,30},{7,1},{8,16},{9,15},... | collective-permute-start | bytes 165896 | tf_op jit(solution)/shard_map/ppermute | solution.py:657
  44.2 5.1 %collective-permute-start.14 = (bf16[216,128]{1,0:T(8,128)(2,1)S(1)}, bf16[216,128]{1,0:T(8,128)(2,1)S(1)}, u32[]{:S(2)}, u32[]{:S(2)}) collective-permute-start(bf16[216,128]{1,0:T(8,128)(2,1)S(1)} %get-tuple-element.63), channel_id=1, source_target_pairs={{0,16},{1,5},{2,18},{3,7},{4,20},{5,1},{6,22},{7,3},{8,24},{9,13},... | collective-permute-start | bytes 165896 | tf_op jit(solution)/shard_map/ppermute | solution.py:657
  45.6 4.3 %collective-permute-start.15 = (bf16[216,128]{1,0:T(8,128)(2,1)S(1)}, bf16[216,128]{1,0:T(8,128)(2,1)S(1)}, u32[]{:S(2)}, u32[]{:S(2)}) collective-permute-start(bf16[216,128]{1,0:T(8,128)(2,1)S(1)} %get-tuple-element.64), channel_id=1, source_target_pairs={{0,8},{1,3},{2,10},{3,1},{4,12},{5,7},{6,14},{7,5},{8,0},{9,11},{1... | collective-permute-start | bytes 165896 | tf_op jit(solution)/shard_map/ppermute | solution.py:657
  49.9 1.4 %collective-permute-start.16 = (f32[216,128]{1,0:T(8,128)S(1)}, f32[216,128]{1,0:T(8,128)S(1)}, u32[]{:S(2)}, u32[]{:S(2)}) collective-permute-start(f32[216,128]{1,0:T(8,128)S(1)} %shard_map.108), channel_id=1, source_target_pairs={{0,1},{1,0},{2,3},{3,2},{4,5},{5,4},{6,7},{7,6},{8,9},{9,8},{10,11... | collective-permute-start | bytes 331784 | tf_op jit(solution)/shard_map/ppermute | solution.py:645

commit v4 on v3

--- a/solution.py
+++ b/solution.py
@@ -10,7 +10,6 @@
 
 BF16 = jnp.bfloat16
 F32 = jnp.float32
-LABEL_ROWS = 16
 SMALL = pltpu.CompilerParams(vmem_limit_bytes=8 * 1024 * 1024)
 
 
@@ -173,19 +172,19 @@
     return high * side + low
 
 
-def padded_rows(rows):
-    return -(-rows // 16) * 16
+def block_rows(share):
+    return -(-(share + 8) // 16) * 16
 
 
 def pack_kernel(dest_ref, pos_ref, slabs_hbm, first_hbm, second_hbm, *refs):
-    side = len(refs) - 3
+    side = len(refs) - 4
     out_refs = refs[:side]
-    slabs_ref, own_ref, sem = refs[side:]
+    slabs_ref, own_ref, block_ref, sem = refs[side:]
     core, high, low = position(side)
     p, _ = walk(core, high, low)
     count, columns, channels = slabs_ref.shape
     share = own_ref.shape[0]
-    base = padded_rows(share)
+    base = block_rows(share)
     load_slabs = pltpu.make_async_copy(slabs_hbm, slabs_ref, sem.at[0])
     load_first = pltpu.make_async_copy(first_hbm, own_ref, sem.at[1])
     load_second = pltpu.make_async_copy(second_hbm, own_ref, sem.at[1])
@@ -199,33 +198,33 @@
     def _():
         load_second.start()
 
-    row = lax.broadcasted_iota(jnp.int32, (LABEL_ROWS, channels), 0)
+    block_ref[...] = jnp.zeros(block_ref.shape, BF16)
+    row = lax.broadcasted_iota(jnp.int32, (base - share, channels), 0)
+    labels = [jnp.full((base - share, channels), -1.0, F32) for _ in range(side)]
+    steps, slots = [], []
+    for s in range(count):
+        p_to, q_to = walk(core, dest_ref[s] // side, lax.rem(dest_ref[s], side))
+        steps.append(jnp.bitwise_xor(p, p_to))
+        slots.append(q_to)
+        place = pos_ref[s].astype(F32)
+        for k in range(side):
+            hit = jnp.where(steps[s] == k, q_to, -1)
+            labels[k] = jnp.where(row == hit, place, labels[k])
     load_slabs.wait()
-    slabs = [slabs_ref[s].astype(F32) for s in range(count)]
+    for s in range(count):
+        start = pl.multiple_of(slots[s] * columns, columns)
+        block_ref[steps[s], pl.ds(start, columns), :] = slabs_ref[s]
     for k in range(side):
-        labels = jnp.full((LABEL_ROWS, channels), -1.0, F32)
-        for q in range(side):
-            target = chip_of(core, jnp.bitwise_xor(p, k), q, side)
-            total = jnp.zeros((columns, channels), F32)
-            place = jnp.int32(-1)
-            for s in range(count):
-                match = dest_ref[s] == target
-                total = jnp.where(match, slabs[s], total)
-                place = jnp.where(match, pos_ref[s], place)
-            labels = jnp.where(row == q, place.astype(F32), labels)
-            at = base + q * columns
-            out_refs[k][at : at + columns, :] = total.astype(BF16)
-        out_refs[k][base + side * columns :, :] = labels.astype(BF16)
+        out_refs[k][base:, :] = block_ref[k]
     load_first.wait()
     own = own_ref[...].astype(F32)
-    own = jnp.concatenate([own, jnp.zeros((base - share, channels), F32)], axis=0).astype(BF16)
     for k in range(side):
-        out_refs[k][:base, :] = own
+        out_refs[k][:base, :] = jnp.concatenate([own, labels[k]], axis=0).astype(BF16)
 
 
 def pack(dest, pos, slabs, first, second, side):
     count, columns, channels = slabs.shape
-    rows = padded_rows(first.shape[0]) + side * columns + LABEL_ROWS
+    rows = block_rows(first.shape[0]) + side * columns
     return pl.pallas_call(
         pack_kernel,
         out_shape=[jax.ShapeDtypeStruct((rows, channels), BF16)] * side,
@@ -234,23 +233,26 @@
         scratch_shapes=[
             pltpu.VMEM(slabs.shape, BF16),
             pltpu.VMEM(first.shape, BF16),
+            pltpu.VMEM((side, side * columns, channels), BF16),
             pltpu.SemaphoreType.DMA((2,)),
         ],
     )(dest, pos, slabs, first, second)
 
 
-def keep_kernel(in_ref, out_ref):
-    out_ref[...] = in_ref[...]
-
-
-def keep(block):
+def keep_kernel(*refs):
+    half = len(refs) // 2
+    for source, target in zip(refs[:half], refs[half:]):
+        target[...] = source[...]
+
+
+def keep(*blocks):
     return pl.pallas_call(
         keep_kernel,
-        out_shape=jax.ShapeDtypeStruct(block.shape, block.dtype),
-        in_specs=whole(1),
-        out_specs=whole(1)[0],
+        out_shape=[jax.ShapeDtypeStruct(block.shape, block.dtype) for block in blocks],
+        in_specs=whole(len(blocks)),
+        out_specs=whole(len(blocks)),
         compiler_params=SMALL,
-    )(block)
+    )(*blocks)
 
 
 def relay_kernel(cot_ref, *refs, columns, base):
@@ -258,28 +260,19 @@
     ins, outs = refs[:side][::-1], refs[side:]
     core, high, low = position(side)
     _, q = walk(core, high, low)
-    channels = ins[0].shape[1]
-    end = side * (base + columns) + LABEL_ROWS
-    row = lax.broadcasted_iota(jnp.int32, (LABEL_ROWS, channels), 0)
     for j in range(side):
-        target = jnp.bitwise_xor(q, j)
-        start = pl.multiple_of(base + target * columns, 16)
-        labels = jnp.full((LABEL_ROWS, channels), -1.0, F32)
+        start = pl.multiple_of(base + jnp.bitwise_xor(q, j) * columns, 16)
         for k in range(side):
             outs[j][k * base : (k + 1) * base, :] = ins[k][:base, :]
             at = side * base + k * columns
             outs[j][at : at + columns, :] = ins[k][pl.ds(start, columns), :]
-            theirs = ins[k][base + side * columns :, :].astype(F32)
-            label = jnp.sum(jnp.where(row == target, theirs, 0.0), axis=0, keepdims=True)
-            labels = jnp.where(row == k, label, labels)
-        outs[j][end - LABEL_ROWS : end, :] = labels.astype(BF16)
-    outs[0][end:, :] = cot_ref[...].reshape(-1, channels)
+    outs[0][side * (base + columns) :, :] = cot_ref[...].reshape(-1, cot_ref.shape[-1])
 
 
 def relay(cot, ins, columns, base):
     side = len(ins)
     channels = ins[0].shape[1]
-    rows = side * (base + columns) + LABEL_ROWS
+    rows = side * (base + columns)
     extra = cot.size // channels
     return pl.pallas_call(
         functools.partial(relay_kernel, columns=columns, base=base),
@@ -291,22 +284,24 @@
     )(cot, *ins[::-1])
 
 
-def settle(blocks, tile_ref, first_row, base):
+def settle(blocks, tile_ref, first_row, q, share):
     side = len(blocks)
+    base = block_rows(share)
     frames, _, columns, channels = tile_ref.shape
+    row = lax.broadcasted_iota(jnp.int32, (base - share, channels), 0)
     slots = []
     for block in blocks:
-        end = side * (base + columns)
-        labels = block[end : end + LABEL_ROWS, :].astype(F32)
         for k in range(side):
+            labels = block[k * base : (k + 1) * base, :].astype(F32)[share:]
+            label = jnp.sum(jnp.where(row == q, labels, 0.0), axis=0, keepdims=True)
+            label = jnp.broadcast_to(label, (columns, channels)).astype(BF16)
             at = side * base + k * columns
-            values = block[at : at + columns, :].astype(F32)
-            slots.append((labels[k : k + 1], values))
+            slots.append((label, block[at : at + columns, :]))
     for place in range(frames * 2):
-        total = jnp.zeros((columns, channels), F32)
+        total = jnp.zeros((columns, channels), BF16)
         for label, values in slots:
-            total = total + jnp.where(label == float(place), values, 0.0)
-        tile_ref[place // 2, first_row + place % 2] = total
+            total = jnp.where(label == BF16(place), values, total)
+        tile_ref[place // 2, first_row + place % 2] = total.astype(F32)
 
 
 def gather_weight(blocks, wide_ref, core, high, low, share, base):
@@ -348,41 +343,66 @@
                     store(row, row + 1, piece, jnp.zeros_like(source[:, :1]))
 
 
-def store_columns(scratch, index, frames, channels):
+def store_pieces(columns_ref):
+    channels = columns_ref.shape[-1] // 9
+
     def store(low, high, piece, values):
-        lanes = slice(piece * channels, (piece + 1) * channels)
-        scratch[index, 2:, low:high, :, lanes] = values
-        scratch[index, 0, low:high, :, lanes] = values[0]
-        scratch[index, 1, low:high, :, lanes] = values[0]
+        columns_ref[:, low:high, :, piece * channels : (piece + 1) * channels] = values
 
     return store
 
 
-def store_plain(scratch, channels):
-    def store(low, high, piece, values):
-        scratch[:, low:high, :, piece * channels : (piece + 1) * channels] = values
-
-    return store
-
-
-def data_grad(columns, wl_ref, sum_ref):
-    frames, rows, count, nine = columns.shape
-    channels = wl_ref.shape[1]
+def spread_weight(wide_ref, index, out_ref, transposed):
+    channels = wide_ref.shape[-1]
+    for a in range(3):
+        for piece in range(9):
+            at = (a * 9 + piece) * channels
+            values = wide_ref[index, at : at + channels, :].astype(BF16)
+            frame = slice(a * channels, (a + 1) * channels)
+            place = slice(piece * channels, (piece + 1) * channels)
+            if transposed:
+                out_ref[frame, place] = values
+            else:
+                out_ref[place, frame] = values
+
+
+def conv(columns, w_ref, frames):
+    channels = w_ref.shape[1] // 3
+    product = jnp.dot(columns, w_ref[...], preferred_element_type=F32)
+    product = product.reshape(frames, -1, 3 * channels)
+    parts = [product[:, :, a * channels : (a + 1) * channels] for a in range(3)]
+    out = []
+    for t in range(frames):
+        out.append(parts[0][max(t - 2, 0)] + parts[1][max(t - 1, 0)] + parts[2][t])
+    return out
+
+
+def conv_back(columns, wl_ref, frames):
+    channels = wl_ref.shape[0] // 3
     nt = (((1,), (1,)), ((), ()))
-    flat = columns.reshape(frames * rows * count, nine)
-    sum_ref[...] = jnp.zeros(sum_ref.shape, F32)
-    for a in range(3):
-        part = lax.dot_general(flat, wl_ref[a], nt, preferred_element_type=F32)
-        sum_ref[a : a + frames] += part.reshape(frames, rows, count, channels)
-    sum_ref[2] = sum_ref[0] + sum_ref[1] + sum_ref[2]
-
-
-def act_gradient(out_grad, act, wl_ref, g_ref, sum_ref):
-    spread(out_grad.astype(F32), store_plain(g_ref, out_grad.shape[-1]), True)
-    data_grad(g_ref[...], wl_ref, sum_ref)
-    act = act.astype(F32)
-    sig = 1.0 / (1.0 + jnp.exp(-act))
-    return (sum_ref[2:] * (sig * (1.0 + act * (1.0 - sig)))).astype(BF16)
+    product = lax.dot_general(columns, wl_ref[...], nt, preferred_element_type=F32)
+    product = product.reshape(frames, -1, 3 * channels)
+    parts = [product[:, :, a * channels : (a + 1) * channels] for a in range(3)]
+    out = []
+    for t in range(frames):
+        total = parts[2][t]
+        for a in range(2):
+            for source in range(frames):
+                if max(source + a - 2, 0) == t:
+                    total = total + parts[a][source]
+        out.append(total)
+    return out
+
+
+def act_gradient(out_grad, act, wl_ref, columns_ref, store):
+    spread(out_grad.astype(F32), store_pieces(columns_ref), True)
+    frames, rows, count, nine = columns_ref.shape
+    hidden = conv_back(columns_ref[...].reshape(-1, nine), wl_ref, frames)
+    for t in range(frames):
+        value = act[t].astype(F32)
+        sig = 1.0 / (1.0 + jnp.exp(-value))
+        slope = sig * (1.0 + value * (1.0 - sig))
+        store(t, (hidden[t].reshape(value.shape) * slope).astype(BF16))
 
 
 def unit_kernel(length_ref, *refs, scale, side, share):
@@ -394,17 +414,9 @@
         return taken
 
     blocks_mine, blocks_other = take(side), take(side)
-    tile_ref, act_scratch, out_grad_ref, act_grad_ref = take(4)
-    w_second_ref, wl_first_ref, wl_second_ref = take(3)
+    tile_ref, act_ref, out_grad_ref, act_grad_ref, wide_ref = take(5)
     outs = take(side)
-    (
-        wide_ref,
-        w_first_ref,
-        x_scratch,
-        g_scratch,
-        up_scratch,
-        sum_scratch,
-    ) = refs
+    w_ref, wl_ref, total_ref, x_scratch, g_scratch, left_ref = refs
     core, high, low = position(side)
     length = length_ref[0]
     frames, rows, columns, channels = tile_ref.shape
@@ -413,75 +425,66 @@
     nine = 9 * channels
     my_row = core * band_rows
     other_row = (1 - core) * band_rows
-    base = padded_rows(share)
-
-    settle(blocks_mine, tile_ref, my_row, base)
-    settle(blocks_other, tile_ref, other_row, base)
+    base = block_rows(share)
+
+    _, my_q = walk(core, high, low)
+    _, other_q = walk(1 - core, high, low)
+    settle(blocks_mine, tile_ref, my_row, my_q, share)
+    settle(blocks_other, tile_ref, other_row, other_q, share)
     gather_weight(blocks_mine, wide_ref, core, high, low, share, base)
     gather_weight(blocks_other, wide_ref, 1 - core, high, low, share, base)
-    for a in range(3):
-        for piece in range(9):
-            at = (a * 9 + piece) * channels
-            lanes = slice(piece * channels, (piece + 1) * channels)
-            values = wide_ref[0, at : at + channels, :].astype(BF16)
-            w_first_ref[a, piece] = values
-            wl_first_ref[a, :, lanes] = values
-            values = wide_ref[1, at : at + channels, :].astype(BF16)
-            w_second_ref[a, piece] = values
-            wl_second_ref[a, :, lanes] = values
+    spread_weight(wide_ref, 0, w_ref, False)
 
     tile = tile_ref[...]
     first = tile / (1.0 + jnp.exp(-tile))
-    spread(first, store_columns(x_scratch, 0, frames, channels), False)
-
-    end = side * (base + columns) + LABEL_ROWS
+    spread(first, store_pieces(x_scratch.at[0]), False)
+
+    end = side * (base + columns)
     band = (frames, band_rows, columns, channels)
     for block, row in ((blocks_mine[0], my_row), (blocks_other[0], other_row)):
         cot = block[end:, :].reshape(band)
         for t in range(frames):
-            up_scratch[1, t, pl.ds(row, band_rows)] = jnp.where(
+            out_grad_ref[t, pl.ds(row, band_rows)] = jnp.where(
                 t < length, cot[t].astype(F32), 0.0
             ).astype(BF16)
-    out_grad_ref[...] = up_scratch[1]
-
-    act = jnp.zeros((cells, channels), F32)
-    for a in range(3):
-        act = act + jnp.dot(
-            x_scratch[0, a : a + frames].reshape(cells, nine),
-            w_first_ref[a].reshape(nine, channels),
-            preferred_element_type=F32,
-        )
-    act = act.astype(BF16).reshape(frames, rows, columns, channels)
-    act_scratch[...] = act
-    act = act.astype(F32)
+    act = conv(x_scratch[0].reshape(cells, nine), w_ref, frames)
+    for t in range(frames):
+        act_ref[t] = act[t].astype(BF16).reshape(rows, columns, channels)
+    act = act_ref[...].astype(F32)
     second = act / (1.0 + jnp.exp(-act))
-    spread(second, store_columns(x_scratch, 1, frames, channels), False)
+    spread(second, store_pieces(x_scratch.at[1]), False)
 
     @pl.when(core == 0)
     def _():
-        act_grad_ref[...] = act_gradient(
-            up_scratch[1], act_scratch[...], wl_second_ref, g_scratch, sum_scratch
-        )
-        up_scratch[0] = act_grad_ref[...]
-
-    upstream = up_scratch[core].reshape(cells, channels).astype(F32).T.astype(BF16)
+        def store(t, values):
+            act_grad_ref[t] = values
+
+        spread_weight(wide_ref, 1, wl_ref, True)
+        act_gradient(out_grad_ref[...], act_ref, wl_ref, g_scratch, store)
+
+    upstream = jnp.where(core == 0, act_grad_ref[...].astype(F32), out_grad_ref[...].astype(F32))
+    upstream = upstream.reshape(frames, rows * columns, channels)
+    turned = [upstream[t].T for t in range(frames)]
     for a in range(3):
-        part = jnp.dot(
-            upstream,
-            x_scratch[core, a : a + frames].reshape(cells, nine),
-            preferred_element_type=F32,
-        )
+        for t in range(frames):
+            met = [turned[s] for s in range(frames) if max(s + a - 2, 0) == t]
+            met = sum(met[1:], met[0]) if met else jnp.zeros_like(turned[0])
+            frame = slice(a * channels, (a + 1) * channels)
+            left_ref[frame, t * rows * columns : (t + 1) * rows * columns] = met.astype(BF16)
+    product = jnp.dot(
+        left_ref[...], x_scratch[core].reshape(cells, nine), preferred_element_type=F32
+    )
+    for a in range(3):
         for piece in range(9):
             at = (a * 9 + piece) * channels
-            wide_ref[0, at : at + channels, :] = (
-                part[:, piece * channels : (piece + 1) * channels].T * scale
-            )
+            block = product[a * channels : (a + 1) * channels, piece * channels : (piece + 1) * channels]
+            total_ref[at : at + channels, :] = block.T * scale
     p, q = walk(core, high, low)
     for k in range(side):
         for j in range(side):
             owner = chip_of(core, j, jnp.bitwise_xor(q, k), side)
             start = pl.multiple_of(owner * share, 8)
-            outs[k][j] = wide_ref[0, pl.ds(start, share), :].astype(BF16)
+            outs[k][j] = total_ref[pl.ds(start, share), :].astype(BF16)
 
 
 def unit(length, blocks_mine, blocks_other, band, scale, share):
@@ -489,8 +492,9 @@
     rows = 2 * band_rows
     side = len(blocks_mine)
     field = (frames, rows, columns, channels)
+    cells = frames * rows * columns
     part = jax.ShapeDtypeStruct((side, share, channels), BF16)
-    flops = 2 * 27 * channels * channels * frames * rows * columns * 3
+    flops = 2 * 27 * channels * channels * cells * 3
     outs = pl.pallas_call(
         functools.partial(unit_kernel, scale=scale, side=side, share=share),
         out_shape=[
@@ -498,25 +502,23 @@
             jax.ShapeDtypeStruct(field, BF16),
             jax.ShapeDtypeStruct(field, BF16),
             jax.ShapeDtypeStruct(field, BF16),
-            jax.ShapeDtypeStruct((3, 9, channels, channels), BF16),
-            jax.ShapeDtypeStruct((3, channels, 9 * channels), BF16),
-            jax.ShapeDtypeStruct((3, channels, 9 * channels), BF16),
+            jax.ShapeDtypeStruct((2, 27 * channels, channels), F32),
         ]
         + [part] * side,
         in_specs=scalars(1) + whole(2 * side),
-        out_specs=whole(7 + side),
+        out_specs=whole(5 + side),
         scratch_shapes=[
-            pltpu.VMEM((2, 27 * channels, channels), F32),
-            pltpu.VMEM((3, 9, channels, channels), BF16),
-            pltpu.VMEM((2, frames + 2, rows, columns, 9 * channels), BF16),
+            pltpu.VMEM((9 * channels, 3 * channels), BF16),
+            pltpu.VMEM((3 * channels, 9 * channels), BF16),
+            pltpu.VMEM((27 * channels, channels), F32),
+            pltpu.VMEM((2, frames, rows, columns, 9 * channels), BF16),
             pltpu.VMEM((frames, rows, columns, 9 * channels), BF16),
-            pltpu.VMEM((2,) + field, BF16),
-            pltpu.VMEM((frames + 2, rows, columns, channels), F32),
+            pltpu.VMEM((3 * channels, cells), BF16),
         ],
         compiler_params=pltpu.CompilerParams(vmem_limit_bytes=36 * 1024 * 1024),
         cost_estimate=pl.CostEstimate(flops=flops, bytes_accessed=4_000_000, transcendentals=0),
     )(length, *blocks_mine, *blocks_other)
-    return outs[:7], outs[7:]
+    return outs[:5], outs[5:]
 
 
 def finish_kernel(
@@ -524,52 +526,50 @@
     act_ref,
     out_grad_ref,
     act_grad_ref,
-    w_second_ref,
-    wl_first_ref,
-    wl_second_ref,
+    wide_ref,
     block_ref,
     grad_ref,
-    x_scratch,
-    g_scratch,
-    up_scratch,
-    full_scratch,
-    sum_scratch,
+    w_ref,
+    wl_ref,
+    columns_ref,
+    up_ref,
 ):
     frames, band_rows, columns, channels = block_ref.shape
     nine = 9 * channels
-    cells = frames * band_rows * columns
     core = lax.axis_index("rows")
     my_row = core * band_rows
-    tile = tile_ref[:, pl.ds(my_row, band_rows)]
+    mine = pl.ds(my_row, band_rows)
+    shape = (band_rows, columns, channels)
 
     act = act_ref[...].astype(F32)
     second = act / (1.0 + jnp.exp(-act))
-    spread(second, store_columns(x_scratch, 0, frames, channels), False)
-    out = jnp.zeros((cells, channels), F32)
-    for a in range(3):
-        out = out + jnp.dot(
-            x_scratch[0, a : a + frames, pl.ds(my_row, band_rows)].reshape(cells, nine),
-            w_second_ref[a].reshape(nine, channels),
-            preferred_element_type=F32,
-        )
-    block_ref[...] = (tile + out.reshape(block_ref.shape)).astype(BF16)
+    spread(second, store_pieces(columns_ref), False)
+    spread_weight(wide_ref, 1, w_ref, False)
+    out = conv(columns_ref[:, mine].reshape(-1, nine), w_ref, frames)
+    for t in range(frames):
+        block_ref[t] = (tile_ref[t, mine] + out[t].reshape(shape)).astype(BF16)
 
     @pl.when(core == 0)
     def _():
-        up_scratch[...] = act_grad_ref[...]
+        up_ref[...] = act_grad_ref[...]
 
     @pl.when(core != 0)
     def _():
-        up_scratch[...] = act_gradient(
-            out_grad_ref[...], act_ref[...], wl_second_ref, g_scratch, full_scratch
-        )
-
-    spread(up_scratch[...].astype(F32), store_plain(g_scratch, channels), True)
-    data_grad(g_scratch[:, pl.ds(my_row, band_rows)], wl_first_ref, sum_scratch)
-    sig = 1.0 / (1.0 + jnp.exp(-tile))
-    slope = sig * (1.0 + tile * (1.0 - sig))
-    upstream = out_grad_ref[:, pl.ds(my_row, band_rows)].astype(F32)
-    grad_ref[...] = (upstream + sum_scratch[2:] * slope).astype(BF16)
+        def store(t, values):
+            up_ref[t] = values
+
+        spread_weight(wide_ref, 1, wl_ref, True)
+        act_gradient(out_grad_ref[...], act_ref, wl_ref, columns_ref, store)
+
+    spread(up_ref[...].astype(F32), store_pieces(columns_ref), True)
+    spread_weight(wide_ref, 0, wl_ref, True)
+    out = conv_back(columns_ref[:, mine].reshape(-1, nine), wl_ref, frames)
+    for t in range(frames):
+        tile = tile_ref[t, mine]
+        sig = 1.0 / (1.0 + jnp.exp(-tile))
+        slope = sig * (1.0 + tile * (1.0 - sig))
+        upstream = out_grad_ref[t, mine].astype(F32)
+        grad_ref[t] = (upstream + out[t].reshape(shape) * slope).astype(BF16)
 
 
 def finish(kept):
@@ -582,11 +582,10 @@
         in_specs=whole(len(kept)),
         out_specs=whole(2),
         scratch_shapes=[
-            pltpu.VMEM((1, frames + 2, rows, columns, 9 * channels), BF16),
+            pltpu.VMEM((9 * channels, 3 * channels), BF16),
+            pltpu.VMEM((3 * channels, 9 * channels), BF16),
             pltpu.VMEM((frames, rows, columns, 9 * channels), BF16),
             pltpu.VMEM((frames, rows, columns, channels), BF16),
-            pltpu.VMEM((frames + 2, rows, columns, channels), F32),
-            pltpu.VMEM((frames + 2, rows // 2, columns, channels), F32),
         ],
         compiler_params=pltpu.CompilerParams(vmem_limit_bytes=20 * 1024 * 1024),
         cost_estimate=pl.CostEstimate(flops=flops, bytes_accessed=2_000_000, transcendentals=0),
@@ -639,7 +638,7 @@
     core = lax.axis_index("rows")
     frames, band_rows, columns, channels = cot.shape[1:]
     share = w_first.shape[0]
-    base = padded_rows(share)
+    base = block_rows(share)
 
     def exchange(block):
         return lax.ppermute(block, "rows", [(0, 1), (1, 0)])
@@ -661,7 +660,8 @@
 
     packed = pack(dest[0, 0], pos[0, 0], slabs[0, 0], w_first, w_second, side)
     _, *arrived = send(packed, (0, 1))
-    relayed = relay(cot[0], [keep(packed[0]), *arrived], columns, base)
+    kept_block, kept_cot = keep(packed[0], cot[0])
+    relayed = relay(kept_cot, [kept_block, *arrived], columns, base)
     blocks_mine = send(relayed, (1, 0))
     blocks_other = [exchange(block) for block in blocks_mine]
 

time: 52.2 us -> 50.4 us (0.966)
  Pallas kernels: 11 us -> 9.16 us
  local copies, waits for them, and re-layouts: 0.89 us -> 1.78 us
  waiting for transfers between devices: 20.2 us -> 19.5 us
    pallas_call x1, Pallas kernels: 5.51 us -> 4.21 us  [unit(): pl.pallas_call(functools.partial(unit_kernel, scale=scale, side=side, sha...]
    unnamed x4, local copies, waits for them, and re-layouts: 0.89 us -> 1.78 us
    ppermute x12, waiting for transfers between devices: 18.1 us -> 17.3 us  [send(): lax.ppermute(blocks[k], ('wide', 'rows'), pairs(axes, k))]
where the time goes in v4:
time: 50.4 us; the launch traced here: 50.2 us
  waiting for transfers between devices  19.5 us (39%)
  starting transfers between devices  17.7 us (35%)
  Pallas kernels  9.16 us (18%)
  local copies, waits for them, and re-layouts  1.78 us (4%)
  between operations  1.36 us (3%)
  other arithmetic  0.7 us (1%)
    ppermute x12, starting transfers between devices, send(): lax.ppermute(blocks[k], ('wide', 'rows'), pairs(axes, k))  17.7 us
    ppermute x12, waiting for transfers between devices, send(): lax.ppermute(blocks[k], ('wide', 'rows'), pairs(axes, k))  17.3 us
    pallas_call x1, Pallas kernels, unit(): pl.pallas_call(functools.partial(unit_kernel, scale=scale, side=side, sha...  4.21 us
    pallas_call x1, Pallas kernels, pack(): pl.pallas_call(pack_kernel, out_shape=[jax.ShapeDtypeStruct((rows, channe...  2.36 us
    pallas_call x1, Pallas kernels, finish(): pl.pallas_call(finish_kernel, out_shape=[band] * 2, in_specs=whole(len(ke...  2.3 us
    ppermute x5, waiting for transfers between devices, exchange(): return lax.ppermute(block, 'rows', [(0, 1), (1, 0)])  2.16 us
    unnamed x4, local copies, waits for them, and re-layouts  1.78 us
  transfers between devices with their start and end apart: 17, of which 13 were waited for; matrix products, arithmetic and copies ran while one was open for 0% of the time, Pallas kernels for 5%

profile of v4, /device:TPU:0, one launch (start us, length us, event | category | flops | bytes accessed | tf_op | source)
XLA Modules:
  0.0 50.2 jit_solution(1018284004934709467)
XLA Ops:
  0.6 2.4 %shard_map.102 = (bf16[352,128]{1,0:T(8,128)(2,1)}, bf16[352,128]{1,0:T(8,128)(2,1)}, bf16[352,128]{1,0:T(8,128)(2,1)}, bf16[352,128]{1,0:T(8,128)(2,1)}) custom-call(s32[10]{0:T(128)} %bitcast.8, s32[10]{0:T(128)} %bitcast.9, bf16[10,32,128]{2,1,0:T(8,128)(2,1)} %bitcast.7, bf16[216,128]{1,0:T(8,128)(2,1)} %first_hbm.1, bf16[216,128]{1,0:T(8,128)(2,1)} %second_hbm.1), custom_call_target="tpu_custom_call" | custom-call | tf_op jit(solution)/shard_map/pallas_call | solution.py:228
  3.0 5.1 %collective-permute-start = (bf16[352,128]{1,0:T(8,128)(2,1)}, bf16[352,128]{1,0:T(8,128)(2,1)S(1)}, u32[]{:S(2)}, u32[]{:S(2)}) collective-permute-start(bf16[352,128]{1,0:T(8,128)(2,1)} %get-tuple-element.37), channel_id=1, source_target_pairs={{0,24},{1,7},{2,26},{3,5},{4,28},{5,3},{6,30},{7,1},{8,16},{9,15},... | collective-permute-start | bytes 270344 | tf_op jit(solution)/shard_map/ppermute | solution.py:656
  8.1 0.0 collective-permute-start.1
  8.1 0.6 %collective-permute-start.2 = (bf16[352,128]{1,0:T(8,128)(2,1)}, bf16[352,128]{1,0:T(8,128)(2,1)S(1)}, u32[]{:S(2)}, u32[]{:S(2)}) collective-permute-start(bf16[352,128]{1,0:T(8,128)(2,1)} %get-tuple-element.39), channel_id=1, source_target_pairs={{0,8},{1,3},{2,10},{3,1},{4,12},{5,7},{6,14},{7,5},{8,0},{9,11},{1... | collective-permute-start | bytes 270344 | tf_op jit(solution)/shard_map/ppermute | solution.py:656
  8.8 0.0 copy-start
  8.8 0.9 %copy-done = bf16[352,128]{1,0:T(8,128)(2,1)S(1)} copy-done((bf16[352,128]{1,0:T(8,128)(2,1)S(1)}, bf16[352,128]{1,0:T(8,128)(2,1)}, u32[]{:S(2)}) %copy-start) | copy-done | bytes 90136
  9.6 0.0 copy-start.1
  9.6 0.9 %copy-done.1 = bf16[1,5,2,32,128]{4,3,2,1,0:T(8,128)(2,1)S(1)} copy-done((bf16[1,5,2,32,128]{4,3,2,1,0:T(8,128)(2,1)S(1)}, bf16[1,5,2,32,128]{4,3,2,1,0:T(8,128)(2,1)}, u32[]{:S(2)}) %copy-start.1) | copy-done | bytes 81944
  10.6 0.4 collective-permute-done.refs_0_
  10.9 2.9 %collective-permute-done.1.refs_1_ = bf16[352,128]{1,0:T(8,128)(2,1)S(1)} collective-permute-done((bf16[352,128]{1,0:T(8,128)(2,1)}, bf16[352,128]{1,0:T(8,128)(2,1)S(1)}, u32[]{:S(2)}, u32[]{:S(2)}) %collective-permute-start.1) | collective-permute-done | bytes 90144 | tf_op jit(solution)/shard_map/ppermute | solution.py:656
  13.9 0.0 collective-permute-done.2.refs_2_
  13.9 0.1 shard_map.104
  14.0 1.6 %collective-permute-start.3 = (bf16[1024,128]{1,0:T(8,128)(2,1)S(1)}, bf16[1024,128]{1,0:T(8,128)(2,1)S(1)}, u32[]{:S(2)}, u32[]{:S(2)}) collective-permute-start(bf16[1024,128]{1,0:T(8,128)(2,1)S(1)} %get-tuple-element.42), channel_id=1, source_target_pairs={{0,2},{1,9},{2,0},{3,11},{4,6},{5,13},{6,4},{7,15},{8,10},{9,1},{1... | collective-permute-start | bytes 786440 | tf_op jit(solution)/shard_map/ppermute | solution.py:656
  15.6 2.1 %collective-permute-start.4 = (bf16[1024,128]{1,0:T(8,128)(2,1)S(1)}, bf16[1024,128]{1,0:T(8,128)(2,1)S(1)}, u32[]{:S(2)}, u32[]{:S(2)}) collective-permute-start(bf16[1024,128]{1,0:T(8,128)(2,1)S(1)} %get-tuple-element.43), channel_id=1, source_target_pairs={{0,4},{1,17},{2,6},{3,19},{4,0},{5,21},{6,2},{7,23},{8,12},{9,25},... | collective-permute-start | bytes 786440 | tf_op jit(solution)/shard_map/ppermute | solution.py:656
  17.6 0.0 collective-permute-start.5
  17.6 0.0 collective-permute-start.6
  17.6 2.8 %collective-permute-done.3.refs_1_ = bf16[1024,128]{1,0:T(8,128)(2,1)S(1)} collective-permute-done((bf16[1024,128]{1,0:T(8,128)(2,1)S(1)}, bf16[1024,128]{1,0:T(8,128)(2,1)S(1)}, u32[]{:S(2)}, u32[]{:S(2)}) %collective-permute-start.3) | collective-permute-done | bytes 262176 | tf_op jit(solution)/shard_map/ppermute | solution.py:656
  20.4 0.0 collective-permute-start.7
  20.4 3.9 %collective-permute-done.4.refs_2_ = bf16[1024,128]{1,0:T(8,128)(2,1)S(1)} collective-permute-done((bf16[1024,128]{1,0:T(8,128)(2,1)S(1)}, bf16[1024,128]{1,0:T(8,128)(2,1)S(1)}, u32[]{:S(2)}, u32[]{:S(2)}) %collective-permute-start.4) | collective-permute-done | bytes 262176 | tf_op jit(solution)/shard_map/ppermute | solution.py:656
  24.3 0.0 collective-permute-start.8
  24.3 0.6 %collective-permute-done.5.refs_3_ = bf16[1024,128]{1,0:T(8,128)(2,1)S(1)} collective-permute-done((bf16[1024,128]{1,0:T(8,128)(2,1)S(1)}, bf16[1024,128]{1,0:T(8,128)(2,1)S(1)}, u32[]{:S(2)}, u32[]{:S(2)}) %collective-permute-start.5) | collective-permute-done | bytes 262176 | tf_op jit(solution)/shard_map/ppermute | solution.py:656
  24.9 0.0 collective-permute-start.9
  25.6 0.0 collective-permute-done.6.refs_4_
  25.6 0.0 collective-permute-done.7.refs_5_
  25.6 0.3 collective-permute-done.8.refs_6_
  25.9 0.6 %collective-permute-done.9.refs_7_ = bf16[1024,128]{1,0:T(8,128)(2,1)S(1)} collective-permute-done((bf16[1024,128]{1,0:T(8,128)(2,1)S(1)}, bf16[1024,128]{1,0:T(8,128)(2,1)S(1)}, u32[]{:S(2)}, u32[]{:S(2)}) %collective-permute-start.9) | collective-permute-done | bytes 262176 | tf_op jit(solution)/shard_map/ppermute | solution.py:644
  26.4 4.2 %shard_map.105 = (f32[5,4,32,128]{3,2,1,0:T(8,128)S(1)}, bf16[5,4,32,128]{3,2,1,0:T(8,128)(2,1)S(1)}, bf16[5,4,32,128]{3,2,1,0:T(8,128)(2,1)S(1)}, bf16[5,4,32,1...) custom-call(s32[1]{0:T(128)S(6)} %copy.11.length_ref, ...), custom_call_target="tpu_custom_call" | custom-call | flops 1698693120 | bytes 4000000 | tf_op jit(solution)/shard_map/pallas_call | solution.py:498
  30.7 1.4 %collective-permute-start.10 = (bf16[4,216,128]{2,1,0:T(8,128)(2,1)S(1)}, bf16[4,216,128]{2,1,0:T(8,128)(2,1)S(1)}, u32[]{:S(2)}, u32[]{:S(2)}) collective-permute-start(bf16[4,216,128]{2,1,0:T(8,128)(2,1)S(1)} %get-tuple-element.46), channel_id=1, source_target_pairs={{0,2},{1,9},{2,0},{3,11},{4,6},{5,13},{6,4},{7,15},{8,10},{9,1},{1... | collective-permute-start | bytes 663560 | tf_op jit(solution)/shard_map/ppermute | solution.py:656
  32.1 1.0 %collective-permute-start.11 = (bf16[4,216,128]{2,1,0:T(8,128)(2,1)S(1)}, bf16[4,216,128]{2,1,0:T(8,128)(2,1)S(1)}, u32[]{:S(2)}, u32[]{:S(2)}) collective-permute-start(bf16[4,216,128]{2,1,0:T(8,128)(2,1)S(1)} %get-tuple-element.47), channel_id=1, source_target_pairs={{0,4},{1,17},{2,6},{3,19},{4,0},{5,21},{6,2},{7,23},{8,12},{9,25},... | collective-permute-start | bytes 663560 | tf_op jit(solution)/shard_map/ppermute | solution.py:656
  33.1 1.4 %collective-permute-start.12 = (bf16[4,216,128]{2,1,0:T(8,128)(2,1)S(1)}, bf16[4,216,128]{2,1,0:T(8,128)(2,1)S(1)}, u32[]{:S(2)}, u32[]{:S(2)}) collective-permute-start(bf16[4,216,128]{2,1,0:T(8,128)(2,1)S(1)} %get-tuple-element.48), channel_id=1, source_target_pairs={{0,6},{1,25},{2,4},{3,27},{4,2},{5,29},{6,0},{7,31},{8,14},{9,17},... | collective-permute-start | bytes 663560 | tf_op jit(solution)/shard_map/ppermute | solution.py:656
  34.5 2.3 %shard_map.106 = (bf16[5,2,32,128]{3,2,1,0:T(8,128)(2,1)}, bf16[5,2,32,128]{3,2,1,0:T(8,128)(2,1)}) custom-call(f32[5,4,32,128]{3,2,1,0:T(8,128)S(1)} %get-tuple-element.49.tile_ref, bf16[5,4,32,128]{3,2,1,0:T(8,128)(2,1)S(1)} %get-tuple-element.50.act_ref, bf16[5,4,32,128]{3,2,1,0:T(8,128)(2,1)S(1)} %get-tuple-element.51.out_grad_ref, ...), custom_call_target="tpu_custom_call" | custom-call | flops 566231040 | bytes 2000000 | tf_op jit(solution)/shard_map/pallas_call | solution.py:579
  36.8 0.0 collective-permute-done.10.refs_2_
  36.8 2.2 %collective-permute-done.11.refs_1_ = bf16[4,216,128]{2,1,0:T(8,128)(2,1)S(1)} collective-permute-done((bf16[4,216,128]{2,1,0:T(8,128)(2,1)S(1)}, bf16[4,216,128]{2,1,0:T(8,128)(2,1)S(1)}, u32[]{:S(2)}, u32[]{:S(2)}) %collective-permute-start.11) | collective-permute-done | bytes 221216 | tf_op jit(solution)/shard_map/ppermute | solution.py:656
  39.0 1.8 %collective-permute-done.12.refs_0_ = bf16[4,216,128]{2,1,0:T(8,128)(2,1)S(1)} collective-permute-done((bf16[4,216,128]{2,1,0:T(8,128)(2,1)S(1)}, bf16[4,216,128]{2,1,0:T(8,128)(2,1)S(1)}, u32[]{:S(2)}, u32[]{:S(2)}) %collective-permute-start.12) | collective-permute-done | bytes 221216 | tf_op jit(solution)/shard_map/ppermute | solution.py:656
  40.8 0.1 shard_map.107
  40.9 1.6 %collective-permute-start.13 = (bf16[216,128]{1,0:T(8,128)(2,1)S(1)}, bf16[216,128]{1,0:T(8,128)(2,1)S(1)}, u32[]{:S(2)}, u32[]{:S(2)}) collective-permute-start(bf16[216,128]{1,0:T(8,128)(2,1)S(1)} %get-tuple-element.62), channel_id=1, source_target_pairs={{0,24},{1,7},{2,26},{3,5},{4,28},{5,3},{6,30},{7,1},{8,16},{9,15},... | collective-permute-start | bytes 165896 | tf_op jit(solution)/shard_map/ppermute | solution.py:656
  42.4 1.3 %collective-permute-start.14 = (bf16[216,128]{1,0:T(8,128)(2,1)S(1)}, bf16[216,128]{1,0:T(8,128)(2,1)S(1)}, u32[]{:S(2)}, u32[]{:S(2)}) collective-permute-start(bf16[216,128]{1,0:T(8,128)(2,1)S(1)} %get-tuple-element.63), channel_id=1, source_target_pairs={{0,16},{1,5},{2,18},{3,7},{4,20},{5,1},{6,22},{7,3},{8,24},{9,13},... | collective-permute-start | bytes 165896 | tf_op jit(solution)/shard_map/ppermute | solution.py:656
  43.7 1.6 %collective-permute-start.15 = (bf16[216,128]{1,0:T(8,128)(2,1)S(1)}, bf16[216,128]{1,0:T(8,128)(2,1)S(1)}, u32[]{:S(2)}, u32[]{:S(2)}) collective-permute-start(bf16[216,128]{1,0:T(8,128)(2,1)S(1)} %get-tuple-element.64), channel_id=1, source_target_pairs={{0,8},{1,3},{2,10},{3,1},{4,12},{5,7},{6,14},{7,5},{8,0},{9,11},{1... | collective-permute-start | bytes 165896 | tf_op jit(solution)/shard_map/ppermute | solution.py:656
  45.3 1.6 %collective-permute-done.13.refs_0_ = bf16[216,128]{1,0:T(8,128)(2,1)S(1)} collective-permute-done((bf16[216,128]{1,0:T(8,128)(2,1)S(1)}, bf16[216,128]{1,0:T(8,128)(2,1)S(1)}, u32[]{:S(2)}, u32[]{:S(2)}) %collective-permute-start.13) | collective-permute-done | bytes 55328 | tf_op jit(solution)/shard_map/ppermute | solution.py:656
  46.9 0.6 %collective-permute-done.14.refs_1_ = bf16[216,128]{1,0:T(8,128)(2,1)S(1)} collective-permute-done((bf16[216,128]{1,0:T(8,128)(2,1)S(1)}, bf16[216,128]{1,0:T(8,128)(2,1)S(1)}, u32[]{:S(2)}, u32[]{:S(2)}) %collective-permute-start.14) | collective-permute-done | bytes 55328 | tf_op jit(solution)/shard_map/ppermute | solution.py:656
  47.5 0.6 %collective-permute-done.15.refs_2_ = bf16[216,128]{1,0:T(8,128)(2,1)S(1)} collective-permute-done((bf16[216,128]{1,0:T(8,128)(2,1)S(1)}, bf16[216,128]{1,0:T(8,128)(2,1)S(1)}, u32[]{:S(2)}, u32[]{:S(2)}) %collective-permute-start.15) | collective-permute-done | bytes 55328 | tf_op jit(solution)/shard_map/ppermute | solution.py:656
  48.1 0.1 collective-permute-start.16
  48.2 1.3 %collective-permute-done.16 = f32[216,128]{1,0:T(8,128)S(1)} collective-permute-done((f32[216,128]{1,0:T(8,128)S(1)}, f32[216,128]{1,0:T(8,128)S(1)}, u32[]{:S(2)}, u32[]{:S(2)}) %collective-permute-start.16) | collective-permute-done | bytes 110624 | tf_op jit(solution)/shard_map/ppermute | solution.py:644
  49.5 0.7 %broadcast_select_fusion = (f32[216,128]{1,0:T(8,128)}, f32[216,128]{1,0:T(8,128)}) fusion(f32[216,128]{1,0:T(8,128)S(1)} %collective-permute-done.16, f32[216,128]{1,0:T(8,128)S(1)} %shard_map.108, pred[]{:T(512)S(6)} %eq.4), kind=kLoop, calls=%fused_computation | loop fusion | flops 55296 | bytes 442369 | tf_op jit(solution)/shard_map/jit(_where)/select_n | solution.py:677
  (2 shorter events, 0.0 us)
Async XLA Ops:
  3.0 7.9 %collective-permute-start = (bf16[352,128]{1,0:T(8,128)(2,1)}, bf16[352,128]{1,0:T(8,128)(2,1)S(1)}, u32[]{:S(2)}, u32[]{:S(2)}) collective-permute-start(bf16[352,128]{1,0:T(8,128)(2,1)} %get-tuple-element.37), channel_id=1, source_target_pairs={{0,24},{1,7},{2,26},{3,5},{4,28},{5,3},{6,30},{7,1},{8,16},{9,15},... | collective-permute-start | bytes 270344 | tf_op jit(solution)/shard_map/ppermute | solution.py:656
  8.1 5.7 %collective-permute-start.1 = (bf16[352,128]{1,0:T(8,128)(2,1)}, bf16[352,128]{1,0:T(8,128)(2,1)S(1)}, u32[]{:S(2)}, u32[]{:S(2)}) collective-permute-start(bf16[352,128]{1,0:T(8,128)(2,1)} %get-tuple-element.38), channel_id=1, source_target_pairs={{0,16},{1,5},{2,18},{3,7},{4,20},{5,1},{6,22},{7,3},{8,24},{9,13},... | collective-permute-start | bytes 270344 | tf_op jit(solution)/shard_map/ppermute | solution.py:656
  8.1 5.7 %collective-permute-start.2 = (bf16[352,128]{1,0:T(8,128)(2,1)}, bf16[352,128]{1,0:T(8,128)(2,1)S(1)}, u32[]{:S(2)}, u32[]{:S(2)}) collective-permute-start(bf16[352,128]{1,0:T(8,128)(2,1)} %get-tuple-element.39), channel_id=1, source_target_pairs={{0,8},{1,3},{2,10},{3,1},{4,12},{5,7},{6,14},{7,5},{8,0},{9,11},{1... | collective-permute-start | bytes 270344 | tf_op jit(solution)/shard_map/ppermute | solution.py:656
  8.8 0.9 %copy-start = (bf16[352,128]{1,0:T(8,128)(2,1)S(1)}, bf16[352,128]{1,0:T(8,128)(2,1)}, u32[]{:S(2)}) copy-start(bf16[352,128]{1,0:T(8,128)(2,1)} %get-tuple-element.35.refs_0_) | copy-start | bytes 270340
  9.6 0.9 %copy-start.1 = (bf16[1,5,2,32,128]{4,3,2,1,0:T(8,128)(2,1)S(1)}, bf16[1,5,2,32,128]{4,3,2,1,0:T(8,128)(2,1)}, u32[]{:S(2)}) copy-start(bf16[1,5,2,32,128]{4,3,2,1,0:T(8,128)(2,1)} %param.11) | copy-start | bytes 245764
  14.0 6.4 %collective-permute-start.3 = (bf16[1024,128]{1,0:T(8,128)(2,1)S(1)}, bf16[1024,128]{1,0:T(8,128)(2,1)S(1)}, u32[]{:S(2)}, u32[]{:S(2)}) collective-permute-start(bf16[1024,128]{1,0:T(8,128)(2,1)S(1)} %get-tuple-element.42), channel_id=1, source_target_pairs={{0,2},{1,9},{2,0},{3,11},{4,6},{5,13},{6,4},{7,15},{8,10},{9,1},{1... | collective-permute-start | bytes 786440 | tf_op jit(solution)/shard_map/ppermute | solution.py:656
  15.6 8.8 %collective-permute-start.4 = (bf16[1024,128]{1,0:T(8,128)(2,1)S(1)}, bf16[1024,128]{1,0:T(8,128)(2,1)S(1)}, u32[]{:S(2)}, u32[]{:S(2)}) collective-permute-start(bf16[1024,128]{1,0:T(8,128)(2,1)S(1)} %get-tuple-element.43), channel_id=1, source_target_pairs={{0,4},{1,17},{2,6},{3,19},{4,0},{5,21},{6,2},{7,23},{8,12},{9,25},... | collective-permute-start | bytes 786440 | tf_op jit(solution)/shard_map/ppermute | solution.py:656
  17.6 7.3 %collective-permute-start.5 = (bf16[1024,128]{1,0:T(8,128)(2,1)S(1)}, bf16[1024,128]{1,0:T(8,128)(2,1)S(1)}, u32[]{:S(2)}, u32[]{:S(2)}) collective-permute-start(bf16[1024,128]{1,0:T(8,128)(2,1)S(1)} %get-tuple-element.44), channel_id=1, source_target_pairs={{0,6},{1,25},{2,4},{3,27},{4,2},{5,29},{6,0},{7,31},{8,14},{9,17},... | collective-permute-start | bytes 786440 | tf_op jit(solution)/shard_map/ppermute | solution.py:656
  17.6 7.9 %collective-permute-start.6 = (bf16[1344,128]{1,0:T(8,128)(2,1)S(1)}, bf16[1344,128]{1,0:T(8,128)(2,1)S(1)}, u32[]{:S(2)}, u32[]{:S(2)}) collective-permute-start(bf16[1344,128]{1,0:T(8,128)(2,1)S(1)} %get-tuple-element.41.refs_0_), channel_id=1, source_target_pairs={{0,1},{1,0},{2,3},{3,2},{4,5},{5,4},{6,7},{7,6},{8,9},{9,8},{10,11... | collective-permute-start | bytes 1032200 | tf_op jit(solution)/shard_map/ppermute | solution.py:644
  20.4 5.1 %collective-permute-start.7 = (bf16[1024,128]{1,0:T(8,128)(2,1)S(1)}, bf16[1024,128]{1,0:T(8,128)(2,1)S(1)}, u32[]{:S(2)}, u32[]{:S(2)}) collective-permute-start(bf16[1024,128]{1,0:T(8,128)(2,1)S(1)} %collective-permute-done.3.refs_1_), channel_id=1, source_target_pairs={{0,1},{1,0},{2,3},{3,2},{4,5},{5,4},{6,7},{7,6},{8,9},{9,8},{10,11... | collective-permute-start | bytes 786440 | tf_op jit(solution)/shard_map/ppermute | solution.py:644
  24.3 1.5 %collective-permute-start.8 = (bf16[1024,128]{1,0:T(8,128)(2,1)S(1)}, bf16[1024,128]{1,0:T(8,128)(2,1)S(1)}, u32[]{:S(2)}, u32[]{:S(2)}) collective-permute-start(bf16[1024,128]{1,0:T(8,128)(2,1)S(1)} %collective-permute-done.4.refs_2_), channel_id=1, source_target_pairs={{0,1},{1,0},{2,3},{3,2},{4,5},{5,4},{6,7},{7,6},{8,9},{9,8},{10,11... | collective-permute-start | bytes 786440 | tf_op jit(solution)/shard_map/ppermute | solution.py:644
  24.9 1.5 %collective-permute-start.9 = (bf16[1024,128]{1,0:T(8,128)(2,1)S(1)}, bf16[1024,128]{1,0:T(8,128)(2,1)S(1)}, u32[]{:S(2)}, u32[]{:S(2)}) collective-permute-start(bf16[1024,128]{1,0:T(8,128)(2,1)S(1)} %collective-permute-done.5.refs_3_), channel_id=1, source_target_pairs={{0,1},{1,0},{2,3},{3,2},{4,5},{5,4},{6,7},{7,6},{8,9},{9,8},{10,11... | collective-permute-start | bytes 786440 | tf_op jit(solution)/shard_map/ppermute | solution.py:644
  30.7 6.1 %collective-permute-start.10 = (bf16[4,216,128]{2,1,0:T(8,128)(2,1)S(1)}, bf16[4,216,128]{2,1,0:T(8,128)(2,1)S(1)}, u32[]{:S(2)}, u32[]{:S(2)}) collective-permute-start(bf16[4,216,128]{2,1,0:T(8,128)(2,1)S(1)} %get-tuple-element.46), channel_id=1, source_target_pairs={{0,2},{1,9},{2,0},{3,11},{4,6},{5,13},{6,4},{7,15},{8,10},{9,1},{1... | collective-permute-start | bytes 663560 | tf_op jit(solution)/shard_map/ppermute | solution.py:656
  32.1 6.9 %collective-permute-start.11 = (bf16[4,216,128]{2,1,0:T(8,128)(2,1)S(1)}, bf16[4,216,128]{2,1,0:T(8,128)(2,1)S(1)}, u32[]{:S(2)}, u32[]{:S(2)}) collective-permute-start(bf16[4,216,128]{2,1,0:T(8,128)(2,1)S(1)} %get-tuple-element.47), channel_id=1, source_target_pairs={{0,4},{1,17},{2,6},{3,19},{4,0},{5,21},{6,2},{7,23},{8,12},{9,25},... | collective-permute-start | bytes 663560 | tf_op jit(solution)/shard_map/ppermute | solution.py:656
  33.1 7.7 %collective-permute-start.12 = (bf16[4,216,128]{2,1,0:T(8,128)(2,1)S(1)}, bf16[4,216,128]{2,1,0:T(8,128)(2,1)S(1)}, u32[]{:S(2)}, u32[]{:S(2)}) collective-permute-start(bf16[4,216,128]{2,1,0:T(8,128)(2,1)S(1)} %get-tuple-element.48), channel_id=1, source_target_pairs={{0,6},{1,25},{2,4},{3,27},{4,2},{5,29},{6,0},{7,31},{8,14},{9,17},... | collective-permute-start | bytes 663560 | tf_op jit(solution)/shard_map/ppermute | solution.py:656
  40.9 6.0 %collective-permute-start.13 = (bf16[216,128]{1,0:T(8,128)(2,1)S(1)}, bf16[216,128]{1,0:T(8,128)(2,1)S(1)}, u32[]{:S(2)}, u32[]{:S(2)}) collective-permute-start(bf16[216,128]{1,0:T(8,128)(2,1)S(1)} %get-tuple-element.62), channel_id=1, source_target_pairs={{0,24},{1,7},{2,26},{3,5},{4,28},{5,3},{6,30},{7,1},{8,16},{9,15},... | collective-permute-start | bytes 165896 | tf_op jit(solution)/shard_map/ppermute | solution.py:656
  42.4 5.1 %collective-permute-start.14 = (bf16[216,128]{1,0:T(8,128)(2,1)S(1)}, bf16[216,128]{1,0:T(8,128)(2,1)S(1)}, u32[]{:S(2)}, u32[]{:S(2)}) collective-permute-start(bf16[216,128]{1,0:T(8,128)(2,1)S(1)} %get-tuple-element.63), channel_id=1, source_target_pairs={{0,16},{1,5},{2,18},{3,7},{4,20},{5,1},{6,22},{7,3},{8,24},{9,13},... | collective-permute-start | bytes 165896 | tf_op jit(solution)/shard_map/ppermute | solution.py:656
  43.7 4.3 %collective-permute-start.15 = (bf16[216,128]{1,0:T(8,128)(2,1)S(1)}, bf16[216,128]{1,0:T(8,128)(2,1)S(1)}, u32[]{:S(2)}, u32[]{:S(2)}) collective-permute-start(bf16[216,128]{1,0:T(8,128)(2,1)S(1)} %get-tuple-element.64), channel_id=1, source_target_pairs={{0,8},{1,3},{2,10},{3,1},{4,12},{5,7},{6,14},{7,5},{8,0},{9,11},{1... | collective-permute-start | bytes 165896 | tf_op jit(solution)/shard_map/ppermute | solution.py:656
  48.1 1.4 %collective-permute-start.16 = (f32[216,128]{1,0:T(8,128)S(1)}, f32[216,128]{1,0:T(8,128)S(1)}, u32[]{:S(2)}, u32[]{:S(2)}) collective-permute-start(f32[216,128]{1,0:T(8,128)S(1)} %shard_map.108), channel_id=1, source_target_pairs={{0,1},{1,0},{2,3},{3,2},{4,5},{5,4},{6,7},{7,6},{8,9},{9,8},{10,11... | collective-permute-start | bytes 331784 | tf_op jit(solution)/shard_map/ppermute | solution.py:644

commit v5 on v4

--- a/solution.py
+++ b/solution.py
@@ -312,7 +312,7 @@
             owner = chip_of(core, jnp.bitwise_xor(p, k), jnp.bitwise_xor(q, j), side)
             start = pl.multiple_of(owner * share, 8)
             values = blocks[j][k * base : (k + 1) * base, :].astype(F32)
-            wide_ref[core, pl.ds(start, share), :] = values[:share]
+            wide_ref[pl.ds(start, share), :] = values[:share]
 
 
 def shifted(field):
@@ -352,12 +352,12 @@
     return store
 
 
-def spread_weight(wide_ref, index, out_ref, transposed):
+def spread_weight(wide_ref, out_ref, transposed):
     channels = wide_ref.shape[-1]
     for a in range(3):
         for piece in range(9):
             at = (a * 9 + piece) * channels
-            values = wide_ref[index, at : at + channels, :].astype(BF16)
+            values = wide_ref[at : at + channels, :].astype(BF16)
             frame = slice(a * channels, (a + 1) * channels)
             place = slice(piece * channels, (piece + 1) * channels)
             if transposed:
@@ -394,8 +394,7 @@
     return out
 
 
-def act_gradient(out_grad, act, wl_ref, columns_ref, store):
-    spread(out_grad.astype(F32), store_pieces(columns_ref), True)
+def act_gradient(act, wl_ref, columns_ref, store):
     frames, rows, count, nine = columns_ref.shape
     hidden = conv_back(columns_ref[...].reshape(-1, nine), wl_ref, frames)
     for t in range(frames):
@@ -405,48 +404,80 @@
         store(t, (hidden[t].reshape(value.shape) * slope).astype(BF16))
 
 
-def unit_kernel(length_ref, *refs, scale, side, share):
-    refs = list(refs)
-
-    def take(count):
-        taken = refs[:count]
-        del refs[:count]
-        return taken
-
-    blocks_mine, blocks_other = take(side), take(side)
-    tile_ref, act_ref, out_grad_ref, act_grad_ref, wide_ref = take(5)
-    outs = take(side)
-    w_ref, wl_ref, total_ref, x_scratch, g_scratch, left_ref = refs
+def spread_chosen(of_core_zero, mine_ref, other_ref, out_ref, transposed):
+    core = lax.axis_index("rows")
+    own = (core == 0) if of_core_zero else (core != 0)
+
+    @pl.when(own)
+    def _():
+        spread_weight(mine_ref, out_ref, transposed)
+
+    @pl.when(jnp.logical_not(own))
+    def _():
+        spread_weight(other_ref, out_ref, transposed)
+
+
+def prepare_kernel(length_ref, *refs, share):
+    side = len(refs) - 5
+    blocks, first_other = refs[:side], refs[side]
+    tile_ref, wide_ref, out_grad_ref, columns_ref = refs[side + 1 :]
     core, high, low = position(side)
-    length = length_ref[0]
+    frames, rows, columns, channels = out_grad_ref.shape
+    band_rows = rows // 2
+    _, q = walk(core, high, low)
+    settle(blocks, tile_ref, 0, q, share)
+    gather_weight(blocks, wide_ref, core, high, low, share, block_rows(share))
+    end = side * (block_rows(share) + columns)
+    band = (frames, band_rows, columns, channels)
+    for block, owner in ((blocks[0], core), (first_other, 1 - core)):
+        cot = block[end:, :].reshape(band)
+        for t in range(frames):
+            out_grad_ref[t, pl.ds(owner * band_rows, band_rows)] = jnp.where(
+                t < length_ref[0], cot[t].astype(F32), 0.0
+            ).astype(BF16)
+
+    @pl.when(core == 0)
+    def _():
+        spread(out_grad_ref[...].astype(F32), store_pieces(columns_ref), True)
+
+
+def prepare(length, blocks_mine, first_other, band, share):
+    frames, band_rows, columns, channels = band
+    field = (frames, 2 * band_rows, columns, channels)
+    return pl.pallas_call(
+        functools.partial(prepare_kernel, share=share),
+        out_shape=[
+            jax.ShapeDtypeStruct(band, F32),
+            jax.ShapeDtypeStruct((27 * channels, channels), F32),
+            jax.ShapeDtypeStruct(field, BF16),
+            jax.ShapeDtypeStruct(field[:-1] + (9 * channels,), BF16),
+        ],
+        in_specs=scalars(1) + whole(len(blocks_mine) + 1),
+        out_specs=whole(4),
+        compiler_params=SMALL,
+    )(length, *blocks_mine, first_other)
+
+
+def unit_kernel(tile_mine, wide_mine, out_grad_ref, columns_ref, *refs, scale, side, share):
+    blocks_other, refs = refs[:side], refs[side:]
+    tile_ref, act_ref, act_grad_ref, wide_other = refs[:4]
+    outs, refs = refs[4 : 4 + side], refs[4 + side :]
+    w_ref, wl_ref, total_ref, x_scratch, left_ref = refs
+    core, high, low = position(side)
     frames, rows, columns, channels = tile_ref.shape
     band_rows = rows // 2
     cells = frames * rows * columns
     nine = 9 * channels
-    my_row = core * band_rows
-    other_row = (1 - core) * band_rows
-    base = block_rows(share)
-
-    _, my_q = walk(core, high, low)
+
     _, other_q = walk(1 - core, high, low)
-    settle(blocks_mine, tile_ref, my_row, my_q, share)
-    settle(blocks_other, tile_ref, other_row, other_q, share)
-    gather_weight(blocks_mine, wide_ref, core, high, low, share, base)
-    gather_weight(blocks_other, wide_ref, 1 - core, high, low, share, base)
-    spread_weight(wide_ref, 0, w_ref, False)
+    settle(blocks_other, tile_ref, (1 - core) * band_rows, other_q, share)
+    tile_ref[:, pl.ds(core * band_rows, band_rows)] = tile_mine[...]
+    gather_weight(blocks_other, wide_other, 1 - core, high, low, share, block_rows(share))
+    spread_chosen(True, wide_mine, wide_other, w_ref, False)
 
     tile = tile_ref[...]
     first = tile / (1.0 + jnp.exp(-tile))
     spread(first, store_pieces(x_scratch.at[0]), False)
-
-    end = side * (base + columns)
-    band = (frames, band_rows, columns, channels)
-    for block, row in ((blocks_mine[0], my_row), (blocks_other[0], other_row)):
-        cot = block[end:, :].reshape(band)
-        for t in range(frames):
-            out_grad_ref[t, pl.ds(row, band_rows)] = jnp.where(
-                t < length, cot[t].astype(F32), 0.0
-            ).astype(BF16)
     act = conv(x_scratch[0].reshape(cells, nine), w_ref, frames)
     for t in range(frames):
         act_ref[t] = act[t].astype(BF16).reshape(rows, columns, channels)
@@ -459,8 +490,8 @@
         def store(t, values):
             act_grad_ref[t] = values
 
-        spread_weight(wide_ref, 1, wl_ref, True)
-        act_gradient(out_grad_ref[...], act_ref, wl_ref, g_scratch, store)
+        spread_weight(wide_other, wl_ref, True)
+        act_gradient(act_ref, wl_ref, columns_ref, store)
 
     upstream = jnp.where(core == 0, act_grad_ref[...].astype(F32), out_grad_ref[...].astype(F32))
     upstream = upstream.reshape(frames, rows * columns, channels)
@@ -477,7 +508,8 @@
     for a in range(3):
         for piece in range(9):
             at = (a * 9 + piece) * channels
-            block = product[a * channels : (a + 1) * channels, piece * channels : (piece + 1) * channels]
+            lanes = slice(piece * channels, (piece + 1) * channels)
+            block = product[a * channels : (a + 1) * channels, lanes]
             total_ref[at : at + channels, :] = block.T * scale
     p, q = walk(core, high, low)
     for k in range(side):
@@ -487,10 +519,9 @@
             outs[k][j] = total_ref[pl.ds(start, share), :].astype(BF16)
 
 
-def unit(length, blocks_mine, blocks_other, band, scale, share):
-    frames, band_rows, columns, channels = band
-    rows = 2 * band_rows
-    side = len(blocks_mine)
+def unit(prepared, blocks_other, scale, share):
+    frames, rows, columns, channels = prepared[2].shape
+    side = len(blocks_other)
     field = (frames, rows, columns, channels)
     cells = frames * rows * columns
     part = jax.ShapeDtypeStruct((side, share, channels), BF16)
@@ -501,24 +532,23 @@
             jax.ShapeDtypeStruct(field, F32),
             jax.ShapeDtypeStruct(field, BF16),
             jax.ShapeDtypeStruct(field, BF16),
-            jax.ShapeDtypeStruct(field, BF16),
-            jax.ShapeDtypeStruct((2, 27 * channels, channels), F32),
+            jax.ShapeDtypeStruct((27 * channels, channels), F32),
         ]
         + [part] * side,
-        in_specs=scalars(1) + whole(2 * side),
-        out_specs=whole(5 + side),
+        in_specs=whole(len(prepared) + side),
+        out_specs=whole(4 + side),
         scratch_shapes=[
             pltpu.VMEM((9 * channels, 3 * channels), BF16),
             pltpu.VMEM((3 * channels, 9 * channels), BF16),
             pltpu.VMEM((27 * channels, channels), F32),
             pltpu.VMEM((2, frames, rows, columns, 9 * channels), BF16),
-            pltpu.VMEM((frames, rows, columns, 9 * channels), BF16),
             pltpu.VMEM((3 * channels, cells), BF16),
         ],
-        compiler_params=pltpu.CompilerParams(vmem_limit_bytes=36 * 1024 * 1024),
+        compiler_params=pltpu.CompilerParams(vmem_limit_bytes=32 * 1024 * 1024),
         cost_estimate=pl.CostEstimate(flops=flops, bytes_accessed=4_000_000, transcendentals=0),
-    )(length, *blocks_mine, *blocks_other)
-    return outs[:5], outs[5:]
+    )(*prepared, *blocks_other)
+    tile, act, act_grad, wide_other = outs[:4]
+    return (tile, act, prepared[2], act_grad, prepared[1], wide_other), outs[4:]
 
 
 def finish_kernel(
@@ -526,7 +556,8 @@
     act_ref,
     out_grad_ref,
     act_grad_ref,
-    wide_ref,
+    wide_mine,
+    wide_other,
     block_ref,
     grad_ref,
     w_ref,
@@ -537,14 +568,13 @@
     frames, band_rows, columns, channels = block_ref.shape
     nine = 9 * channels
     core = lax.axis_index("rows")
-    my_row = core * band_rows
-    mine = pl.ds(my_row, band_rows)
+    mine = pl.ds(core * band_rows, band_rows)
     shape = (band_rows, columns, channels)
 
     act = act_ref[...].astype(F32)
     second = act / (1.0 + jnp.exp(-act))
     spread(second, store_pieces(columns_ref), False)
-    spread_weight(wide_ref, 1, w_ref, False)
+    spread_chosen(False, wide_mine, wide_other, w_ref, False)
     out = conv(columns_ref[:, mine].reshape(-1, nine), w_ref, frames)
     for t in range(frames):
         block_ref[t] = (tile_ref[t, mine] + out[t].reshape(shape)).astype(BF16)
@@ -558,11 +588,12 @@
         def store(t, values):
             up_ref[t] = values
 
-        spread_weight(wide_ref, 1, wl_ref, True)
-        act_gradient(out_grad_ref[...], act_ref, wl_ref, columns_ref, store)
+        spread_weight(wide_mine, wl_ref, True)
+        spread(out_grad_ref[...].astype(F32), store_pieces(columns_ref), True)
+        act_gradient(act_ref, wl_ref, columns_ref, store)
 
     spread(up_ref[...].astype(F32), store_pieces(columns_ref), True)
-    spread_weight(wide_ref, 0, wl_ref, True)
+    spread_chosen(True, wide_mine, wide_other, wl_ref, True)
     out = conv_back(columns_ref[:, mine].reshape(-1, nine), wl_ref, frames)
     for t in range(frames):
         tile = tile_ref[t, mine]
@@ -666,7 +697,8 @@
     blocks_other = [exchange(block) for block in blocks_mine]
 
     scale = 1.0 / math.sqrt(frames * band_rows * columns * 2 * wide_size)
-    kept, parts = unit(lengths, blocks_mine, blocks_other, cot.shape[1:], scale, share)
+    prepared = prepare(lengths, blocks_mine, blocks_other[0], cot.shape[1:], share)
+    kept, parts = unit(prepared, blocks_other, scale, share)
     block_out, grad_input = finish(kept)
 
     arrived = send(parts, (1, 0))

time: 50.4 us -> 50 us (level)
  waiting for transfers between devices: 19.5 us -> 18.8 us
  transfers between devices with their start and end apart: 17 -> 17, of which waited for: 13 -> 12; matrix products, arithmetic and copies ran while one was open for 0% -> 0% of each run, Pallas kernels for 5% -> 6%
where the time goes in v5:
time: 50 us; the launch traced here: 49.8 us
  waiting for transfers between devices  18.8 us (38%)
  starting transfers between devices  17.7 us (35%)
  Pallas kernels  9.37 us (19%)
  local copies, waits for them, and re-layouts  1.78 us (4%)
  between operations  1.37 us (3%)
  other arithmetic  0.7 us (1%)
    ppermute x12, starting transfers between devices, send(): lax.ppermute(blocks[k], ('wide', 'rows'), pairs(axes, k))  17.7 us
    ppermute x12, waiting for transfers between devices, send(): lax.ppermute(blocks[k], ('wide', 'rows'), pairs(axes, k))  17.1 us
    pallas_call x1, Pallas kernels, unit(): pl.pallas_call(functools.partial(unit_kernel, scale=scale, side=side, sha...  3.79 us
    pallas_call x1, Pallas kernels, finish(): pl.pallas_call(finish_kernel, out_shape=[band] * 2, in_specs=whole(len(ke...  2.48 us
    pallas_call x1, Pallas kernels, pack(): pl.pallas_call(pack_kernel, out_shape=[jax.ShapeDtypeStruct((rows, channe...  2.36 us
    unnamed x4, local copies, waits for them, and re-layouts  1.78 us
    ppermute x5, waiting for transfers between devices, exchange(): return lax.ppermute(block, 'rows', [(0, 1), (1, 0)])  1.7 us
  transfers between devices with their start and end apart: 17, of which 12 were waited for; matrix products, arithmetic and copies ran while one was open for 0% of the time, Pallas kernels for 6%

profile of v5, /device:TPU:0, one launch (start us, length us, event | category | flops | bytes accessed | tf_op | source)
XLA Modules:
  0.0 49.8 jit_solution(15949468590989062731)
XLA Ops:
  0.6 2.4 %shard_map.102 = (bf16[352,128]{1,0:T(8,128)(2,1)}, bf16[352,128]{1,0:T(8,128)(2,1)}, bf16[352,128]{1,0:T(8,128)(2,1)}, bf16[352,128]{1,0:T(8,128)(2,1)}) custom-call(s32[10]{0:T(128)} %bitcast.8, s32[10]{0:T(128)} %bitcast.9, bf16[10,32,128]{2,1,0:T(8,128)(2,1)} %bitcast.7, bf16[216,128]{1,0:T(8,128)(2,1)} %first_hbm.1, bf16[216,128]{1,0:T(8,128)(2,1)} %second_hbm.1), custom_call_target="tpu_custom_call" | custom-call | tf_op jit(solution)/shard_map/pallas_call | solution.py:228
  3.0 5.1 %collective-permute-start = (bf16[352,128]{1,0:T(8,128)(2,1)}, bf16[352,128]{1,0:T(8,128)(2,1)S(1)}, u32[]{:S(2)}, u32[]{:S(2)}) collective-permute-start(bf16[352,128]{1,0:T(8,128)(2,1)} %get-tuple-element.40), channel_id=1, source_target_pairs={{0,24},{1,7},{2,26},{3,5},{4,28},{5,3},{6,30},{7,1},{8,16},{9,15},... | collective-permute-start | bytes 270344 | tf_op jit(solution)/shard_map/ppermute | solution.py:687
  8.1 0.0 collective-permute-start.1
  8.1 0.6 %collective-permute-start.2 = (bf16[352,128]{1,0:T(8,128)(2,1)}, bf16[352,128]{1,0:T(8,128)(2,1)S(1)}, u32[]{:S(2)}, u32[]{:S(2)}) collective-permute-start(bf16[352,128]{1,0:T(8,128)(2,1)} %get-tuple-element.42), channel_id=1, source_target_pairs={{0,8},{1,3},{2,10},{3,1},{4,12},{5,7},{6,14},{7,5},{8,0},{9,11},{1... | collective-permute-start | bytes 270344 | tf_op jit(solution)/shard_map/ppermute | solution.py:687
  8.8 0.0 copy-start
  8.8 0.9 %copy-done = bf16[352,128]{1,0:T(8,128)(2,1)S(1)} copy-done((bf16[352,128]{1,0:T(8,128)(2,1)S(1)}, bf16[352,128]{1,0:T(8,128)(2,1)}, u32[]{:S(2)}) %copy-start) | copy-done | bytes 90136
  9.6 0.0 copy-start.1
  9.6 0.9 %copy-done.1 = bf16[1,5,2,32,128]{4,3,2,1,0:T(8,128)(2,1)S(1)} copy-done((bf16[1,5,2,32,128]{4,3,2,1,0:T(8,128)(2,1)S(1)}, bf16[1,5,2,32,128]{4,3,2,1,0:T(8,128)(2,1)}, u32[]{:S(2)}) %copy-start.1) | copy-done | bytes 81944
  10.5 0.4 collective-permute-done.refs_0_
  10.9 2.9 %collective-permute-done.1.refs_1_ = bf16[352,128]{1,0:T(8,128)(2,1)S(1)} collective-permute-done((bf16[352,128]{1,0:T(8,128)(2,1)}, bf16[352,128]{1,0:T(8,128)(2,1)S(1)}, u32[]{:S(2)}, u32[]{:S(2)}) %collective-permute-start.1) | collective-permute-done | bytes 90144 | tf_op jit(solution)/shard_map/ppermute | solution.py:687
  13.9 0.0 collective-permute-done.2.refs_2_
  13.9 0.1 shard_map.104
  14.0 1.6 %collective-permute-start.3 = (bf16[1024,128]{1,0:T(8,128)(2,1)S(1)}, bf16[1024,128]{1,0:T(8,128)(2,1)S(1)}, u32[]{:S(2)}, u32[]{:S(2)}) collective-permute-start(bf16[1024,128]{1,0:T(8,128)(2,1)S(1)} %get-tuple-element.45), channel_id=1, source_target_pairs={{0,2},{1,9},{2,0},{3,11},{4,6},{5,13},{6,4},{7,15},{8,10},{9,1},{1... | collective-permute-start | bytes 786440 | tf_op jit(solution)/shard_map/ppermute | solution.py:687
  15.6 2.1 %collective-permute-start.4 = (bf16[1024,128]{1,0:T(8,128)(2,1)S(1)}, bf16[1024,128]{1,0:T(8,128)(2,1)S(1)}, u32[]{:S(2)}, u32[]{:S(2)}) collective-permute-start(bf16[1024,128]{1,0:T(8,128)(2,1)S(1)} %get-tuple-element.46), channel_id=1, source_target_pairs={{0,4},{1,17},{2,6},{3,19},{4,0},{5,21},{6,2},{7,23},{8,12},{9,25},... | collective-permute-start | bytes 786440 | tf_op jit(solution)/shard_map/ppermute | solution.py:687
  17.6 0.0 collective-permute-start.5
  17.6 0.0 collective-permute-start.6
  17.6 2.8 %collective-permute-done.3.refs_1_ = bf16[1024,128]{1,0:T(8,128)(2,1)S(1)} collective-permute-done((bf16[1024,128]{1,0:T(8,128)(2,1)S(1)}, bf16[1024,128]{1,0:T(8,128)(2,1)S(1)}, u32[]{:S(2)}, u32[]{:S(2)}) %collective-permute-start.3) | collective-permute-done | bytes 262176 | tf_op jit(solution)/shard_map/ppermute | solution.py:687
  20.4 0.0 collective-permute-start.7
  20.4 3.9 %collective-permute-done.4.refs_2_ = bf16[1024,128]{1,0:T(8,128)(2,1)S(1)} collective-permute-done((bf16[1024,128]{1,0:T(8,128)(2,1)S(1)}, bf16[1024,128]{1,0:T(8,128)(2,1)S(1)}, u32[]{:S(2)}, u32[]{:S(2)}) %collective-permute-start.4) | collective-permute-done | bytes 262176 | tf_op jit(solution)/shard_map/ppermute | solution.py:687
  24.3 0.0 collective-permute-start.8
  24.3 0.6 %collective-permute-done.5.refs_3_ = bf16[1024,128]{1,0:T(8,128)(2,1)S(1)} collective-permute-done((bf16[1024,128]{1,0:T(8,128)(2,1)S(1)}, bf16[1024,128]{1,0:T(8,128)(2,1)S(1)}, u32[]{:S(2)}, u32[]{:S(2)}) %collective-permute-start.5) | collective-permute-done | bytes 262176 | tf_op jit(solution)/shard_map/ppermute | solution.py:687
  24.9 0.0 collective-permute-start.9
  25.6 0.0 collective-permute-done.6.refs_4_.refs_0_
  25.6 0.5 shard_map.105
  26.0 0.0 collective-permute-done.7.refs_1_
  26.0 0.0 collective-permute-done.8.refs_2_
  26.1 0.4 collective-permute-done.9.refs_3_
  26.4 3.8 %shard_map.106 = (f32[5,4,32,128]{3,2,1,0:T(8,128)S(1)}, bf16[5,4,32,128]{3,2,1,0:T(8,128)(2,1)S(1)}, bf16[5,4,32,128]{3,2,1,0:T(8,128)(2,1)S(1)}, f32[3456,128]...) custom-call(f32[5,2,32,128]{3,2,1,0:T(8,128)S(1)} %get-tuple-element, ...), custom_call_target="tpu_custom_call" | custom-call | flops 1698693120 | bytes 4000000 | tf_op jit(solution)/shard_map/pallas_call | solution.py:529
  30.2 1.4 %collective-permute-start.10 = (bf16[4,216,128]{2,1,0:T(8,128)(2,1)S(1)}, bf16[4,216,128]{2,1,0:T(8,128)(2,1)S(1)}, u32[]{:S(2)}, u32[]{:S(2)}) collective-permute-start(bf16[4,216,128]{2,1,0:T(8,128)(2,1)S(1)} %get-tuple-element.53), channel_id=1, source_target_pairs={{0,2},{1,9},{2,0},{3,11},{4,6},{5,13},{6,4},{7,15},{8,10},{9,1},{1... | collective-permute-start | bytes 663560 | tf_op jit(solution)/shard_map/ppermute | solution.py:687
  31.7 1.0 %collective-permute-start.11 = (bf16[4,216,128]{2,1,0:T(8,128)(2,1)S(1)}, bf16[4,216,128]{2,1,0:T(8,128)(2,1)S(1)}, u32[]{:S(2)}, u32[]{:S(2)}) collective-permute-start(bf16[4,216,128]{2,1,0:T(8,128)(2,1)S(1)} %get-tuple-element.54), channel_id=1, source_target_pairs={{0,4},{1,17},{2,6},{3,19},{4,0},{5,21},{6,2},{7,23},{8,12},{9,25},... | collective-permute-start | bytes 663560 | tf_op jit(solution)/shard_map/ppermute | solution.py:687
  32.7 1.4 %collective-permute-start.12 = (bf16[4,216,128]{2,1,0:T(8,128)(2,1)S(1)}, bf16[4,216,128]{2,1,0:T(8,128)(2,1)S(1)}, u32[]{:S(2)}, u32[]{:S(2)}) collective-permute-start(bf16[4,216,128]{2,1,0:T(8,128)(2,1)S(1)} %get-tuple-element.55), channel_id=1, source_target_pairs={{0,6},{1,25},{2,4},{3,27},{4,2},{5,29},{6,0},{7,31},{8,14},{9,17},... | collective-permute-start | bytes 663560 | tf_op jit(solution)/shard_map/ppermute | solution.py:687
  34.1 2.5 %shard_map.107 = (bf16[5,2,32,128]{3,2,1,0:T(8,128)(2,1)}, bf16[5,2,32,128]{3,2,1,0:T(8,128)(2,1)}) custom-call(f32[5,4,32,128]{3,2,1,0:T(8,128)S(1)} %get-tuple-element.56.tile_ref, bf16[5,4,32,128]{3,2,1,0:T(8,128)(2,1)S(1)} %get-tuple-element.57.act_ref, bf16[5,4,32,128]{3,2,1,0:T(8,128)(2,1)S(1)} %get-tuple-element.50.out_grad_ref, ...), custom_call_target="tpu_custom_call" | custom-call | flops 566231040 | bytes 2000000 | tf_op jit(solution)/shard_map/pallas_call | solution.py:610
  36.5 0.0 collective-permute-done.10.refs_2_
  36.6 2.0 %collective-permute-done.11.refs_1_ = bf16[4,216,128]{2,1,0:T(8,128)(2,1)S(1)} collective-permute-done((bf16[4,216,128]{2,1,0:T(8,128)(2,1)S(1)}, bf16[4,216,128]{2,1,0:T(8,128)(2,1)S(1)}, u32[]{:S(2)}, u32[]{:S(2)}) %collective-permute-start.11) | collective-permute-done | bytes 221216 | tf_op jit(solution)/shard_map/ppermute | solution.py:687
  38.5 1.8 %collective-permute-done.12.refs_0_ = bf16[4,216,128]{2,1,0:T(8,128)(2,1)S(1)} collective-permute-done((bf16[4,216,128]{2,1,0:T(8,128)(2,1)S(1)}, bf16[4,216,128]{2,1,0:T(8,128)(2,1)S(1)}, u32[]{:S(2)}, u32[]{:S(2)}) %collective-permute-start.12) | collective-permute-done | bytes 221216 | tf_op jit(solution)/shard_map/ppermute | solution.py:687
  40.3 0.1 shard_map.108
  40.5 1.6 %collective-permute-start.13 = (bf16[216,128]{1,0:T(8,128)(2,1)S(1)}, bf16[216,128]{1,0:T(8,128)(2,1)S(1)}, u32[]{:S(2)}, u32[]{:S(2)}) collective-permute-start(bf16[216,128]{1,0:T(8,128)(2,1)S(1)} %get-tuple-element.68), channel_id=1, source_target_pairs={{0,24},{1,7},{2,26},{3,5},{4,28},{5,3},{6,30},{7,1},{8,16},{9,15},... | collective-permute-start | bytes 165896 | tf_op jit(solution)/shard_map/ppermute | solution.py:687
  42.0 1.3 %collective-permute-start.14 = (bf16[216,128]{1,0:T(8,128)(2,1)S(1)}, bf16[216,128]{1,0:T(8,128)(2,1)S(1)}, u32[]{:S(2)}, u32[]{:S(2)}) collective-permute-start(bf16[216,128]{1,0:T(8,128)(2,1)S(1)} %get-tuple-element.69), channel_id=1, source_target_pairs={{0,16},{1,5},{2,18},{3,7},{4,20},{5,1},{6,22},{7,3},{8,24},{9,13},... | collective-permute-start | bytes 165896 | tf_op jit(solution)/shard_map/ppermute | solution.py:687
  43.3 1.6 %collective-permute-start.15 = (bf16[216,128]{1,0:T(8,128)(2,1)S(1)}, bf16[216,128]{1,0:T(8,128)(2,1)S(1)}, u32[]{:S(2)}, u32[]{:S(2)}) collective-permute-start(bf16[216,128]{1,0:T(8,128)(2,1)S(1)} %get-tuple-element.70), channel_id=1, source_target_pairs={{0,8},{1,3},{2,10},{3,1},{4,12},{5,7},{6,14},{7,5},{8,0},{9,11},{1... | collective-permute-start | bytes 165896 | tf_op jit(solution)/shard_map/ppermute | solution.py:687
  44.9 1.6 %collective-permute-done.13.refs_0_ = bf16[216,128]{1,0:T(8,128)(2,1)S(1)} collective-permute-done((bf16[216,128]{1,0:T(8,128)(2,1)S(1)}, bf16[216,128]{1,0:T(8,128)(2,1)S(1)}, u32[]{:S(2)}, u32[]{:S(2)}) %collective-permute-start.13) | collective-permute-done | bytes 55328 | tf_op jit(solution)/shard_map/ppermute | solution.py:687
  46.5 0.6 %collective-permute-done.14.refs_1_ = bf16[216,128]{1,0:T(8,128)(2,1)S(1)} collective-permute-done((bf16[216,128]{1,0:T(8,128)(2,1)S(1)}, bf16[216,128]{1,0:T(8,128)(2,1)S(1)}, u32[]{:S(2)}, u32[]{:S(2)}) %collective-permute-start.14) | collective-permute-done | bytes 55328 | tf_op jit(solution)/shard_map/ppermute | solution.py:687
  47.1 0.6 %collective-permute-done.15.refs_2_ = bf16[216,128]{1,0:T(8,128)(2,1)S(1)} collective-permute-done((bf16[216,128]{1,0:T(8,128)(2,1)S(1)}, bf16[216,128]{1,0:T(8,128)(2,1)S(1)}, u32[]{:S(2)}, u32[]{:S(2)}) %collective-permute-start.15) | collective-permute-done | bytes 55328 | tf_op jit(solution)/shard_map/ppermute | solution.py:687
  47.7 0.1 collective-permute-start.16
  47.8 1.3 %collective-permute-done.16 = f32[216,128]{1,0:T(8,128)S(1)} collective-permute-done((f32[216,128]{1,0:T(8,128)S(1)}, f32[216,128]{1,0:T(8,128)S(1)}, u32[]{:S(2)}, u32[]{:S(2)}) %collective-permute-start.16) | collective-permute-done | bytes 110624 | tf_op jit(solution)/shard_map/ppermute | solution.py:675
  49.1 0.7 %broadcast_select_fusion = (f32[216,128]{1,0:T(8,128)}, f32[216,128]{1,0:T(8,128)}) fusion(f32[216,128]{1,0:T(8,128)S(1)} %collective-permute-done.16, f32[216,128]{1,0:T(8,128)S(1)} %shard_map.109, pred[]{:T(512)S(6)} %eq.4), kind=kLoop, calls=%fused_computation | loop fusion | flops 55296 | bytes 442369 | tf_op jit(solution)/shard_map/jit(_where)/select_n | solution.py:709
  (2 shorter events, 0.0 us)
Async XLA Ops:
  3.0 7.9 %collective-permute-start = (bf16[352,128]{1,0:T(8,128)(2,1)}, bf16[352,128]{1,0:T(8,128)(2,1)S(1)}, u32[]{:S(2)}, u32[]{:S(2)}) collective-permute-start(bf16[352,128]{1,0:T(8,128)(2,1)} %get-tuple-element.40), channel_id=1, source_target_pairs={{0,24},{1,7},{2,26},{3,5},{4,28},{5,3},{6,30},{7,1},{8,16},{9,15},... | collective-permute-start | bytes 270344 | tf_op jit(solution)/shard_map/ppermute | solution.py:687
  8.1 5.7 %collective-permute-start.1 = (bf16[352,128]{1,0:T(8,128)(2,1)}, bf16[352,128]{1,0:T(8,128)(2,1)S(1)}, u32[]{:S(2)}, u32[]{:S(2)}) collective-permute-start(bf16[352,128]{1,0:T(8,128)(2,1)} %get-tuple-element.41), channel_id=1, source_target_pairs={{0,16},{1,5},{2,18},{3,7},{4,20},{5,1},{6,22},{7,3},{8,24},{9,13},... | collective-permute-start | bytes 270344 | tf_op jit(solution)/shard_map/ppermute | solution.py:687
  8.1 5.7 %collective-permute-start.2 = (bf16[352,128]{1,0:T(8,128)(2,1)}, bf16[352,128]{1,0:T(8,128)(2,1)S(1)}, u32[]{:S(2)}, u32[]{:S(2)}) collective-permute-start(bf16[352,128]{1,0:T(8,128)(2,1)} %get-tuple-element.42), channel_id=1, source_target_pairs={{0,8},{1,3},{2,10},{3,1},{4,12},{5,7},{6,14},{7,5},{8,0},{9,11},{1... | collective-permute-start | bytes 270344 | tf_op jit(solution)/shard_map/ppermute | solution.py:687
  8.8 0.9 %copy-start = (bf16[352,128]{1,0:T(8,128)(2,1)S(1)}, bf16[352,128]{1,0:T(8,128)(2,1)}, u32[]{:S(2)}) copy-start(bf16[352,128]{1,0:T(8,128)(2,1)} %get-tuple-element.38.refs_0_) | copy-start | bytes 270340
  9.6 0.9 %copy-start.1 = (bf16[1,5,2,32,128]{4,3,2,1,0:T(8,128)(2,1)S(1)}, bf16[1,5,2,32,128]{4,3,2,1,0:T(8,128)(2,1)}, u32[]{:S(2)}) copy-start(bf16[1,5,2,32,128]{4,3,2,1,0:T(8,128)(2,1)} %param.11) | copy-start | bytes 245764
  14.0 6.4 %collective-permute-start.3 = (bf16[1024,128]{1,0:T(8,128)(2,1)S(1)}, bf16[1024,128]{1,0:T(8,128)(2,1)S(1)}, u32[]{:S(2)}, u32[]{:S(2)}) collective-permute-start(bf16[1024,128]{1,0:T(8,128)(2,1)S(1)} %get-tuple-element.45), channel_id=1, source_target_pairs={{0,2},{1,9},{2,0},{3,11},{4,6},{5,13},{6,4},{7,15},{8,10},{9,1},{1... | collective-permute-start | bytes 786440 | tf_op jit(solution)/shard_map/ppermute | solution.py:687
  15.6 8.8 %collective-permute-start.4 = (bf16[1024,128]{1,0:T(8,128)(2,1)S(1)}, bf16[1024,128]{1,0:T(8,128)(2,1)S(1)}, u32[]{:S(2)}, u32[]{:S(2)}) collective-permute-start(bf16[1024,128]{1,0:T(8,128)(2,1)S(1)} %get-tuple-element.46), channel_id=1, source_target_pairs={{0,4},{1,17},{2,6},{3,19},{4,0},{5,21},{6,2},{7,23},{8,12},{9,25},... | collective-permute-start | bytes 786440 | tf_op jit(solution)/shard_map/ppermute | solution.py:687
  17.6 7.3 %collective-permute-start.5 = (bf16[1024,128]{1,0:T(8,128)(2,1)S(1)}, bf16[1024,128]{1,0:T(8,128)(2,1)S(1)}, u32[]{:S(2)}, u32[]{:S(2)}) collective-permute-start(bf16[1024,128]{1,0:T(8,128)(2,1)S(1)} %get-tuple-element.47), channel_id=1, source_target_pairs={{0,6},{1,25},{2,4},{3,27},{4,2},{5,29},{6,0},{7,31},{8,14},{9,17},... | collective-permute-start | bytes 786440 | tf_op jit(solution)/shard_map/ppermute | solution.py:687
  17.6 7.9 %collective-permute-start.6 = (bf16[1344,128]{1,0:T(8,128)(2,1)S(1)}, bf16[1344,128]{1,0:T(8,128)(2,1)S(1)}, u32[]{:S(2)}, u32[]{:S(2)}) collective-permute-start(bf16[1344,128]{1,0:T(8,128)(2,1)S(1)} %get-tuple-element.44.refs_0_), channel_id=1, source_target_pairs={{0,1},{1,0},{2,3},{3,2},{4,5},{5,4},{6,7},{7,6},{8,9},{9,8},{10,11... | collective-permute-start | bytes 1032200 | tf_op jit(solution)/shard_map/ppermute | solution.py:675
  20.4 5.6 %collective-permute-start.7 = (bf16[1024,128]{1,0:T(8,128)(2,1)S(1)}, bf16[1024,128]{1,0:T(8,128)(2,1)S(1)}, u32[]{:S(2)}, u32[]{:S(2)}) collective-permute-start(bf16[1024,128]{1,0:T(8,128)(2,1)S(1)} %collective-permute-done.3.refs_1_), channel_id=1, source_target_pairs={{0,1},{1,0},{2,3},{3,2},{4,5},{5,4},{6,7},{7,6},{8,9},{9,8},{10,11... | collective-permute-start | bytes 786440 | tf_op jit(solution)/shard_map/ppermute | solution.py:675
  24.3 1.7 %collective-permute-start.8 = (bf16[1024,128]{1,0:T(8,128)(2,1)S(1)}, bf16[1024,128]{1,0:T(8,128)(2,1)S(1)}, u32[]{:S(2)}, u32[]{:S(2)}) collective-permute-start(bf16[1024,128]{1,0:T(8,128)(2,1)S(1)} %collective-permute-done.4.refs_2_), channel_id=1, source_target_pairs={{0,1},{1,0},{2,3},{3,2},{4,5},{5,4},{6,7},{7,6},{8,9},{9,8},{10,11... | collective-permute-start | bytes 786440 | tf_op jit(solution)/shard_map/ppermute | solution.py:675
  24.9 1.5 %collective-permute-start.9 = (bf16[1024,128]{1,0:T(8,128)(2,1)S(1)}, bf16[1024,128]{1,0:T(8,128)(2,1)S(1)}, u32[]{:S(2)}, u32[]{:S(2)}) collective-permute-start(bf16[1024,128]{1,0:T(8,128)(2,1)S(1)} %collective-permute-done.5.refs_3_), channel_id=1, source_target_pairs={{0,1},{1,0},{2,3},{3,2},{4,5},{5,4},{6,7},{7,6},{8,9},{9,8},{10,11... | collective-permute-start | bytes 786440 | tf_op jit(solution)/shard_map/ppermute | solution.py:675
  30.2 6.3 %collective-permute-start.10 = (bf16[4,216,128]{2,1,0:T(8,128)(2,1)S(1)}, bf16[4,216,128]{2,1,0:T(8,128)(2,1)S(1)}, u32[]{:S(2)}, u32[]{:S(2)}) collective-permute-start(bf16[4,216,128]{2,1,0:T(8,128)(2,1)S(1)} %get-tuple-element.53), channel_id=1, source_target_pairs={{0,2},{1,9},{2,0},{3,11},{4,6},{5,13},{6,4},{7,15},{8,10},{9,1},{1... | collective-permute-start | bytes 663560 | tf_op jit(solution)/shard_map/ppermute | solution.py:687
  31.7 6.9 %collective-permute-start.11 = (bf16[4,216,128]{2,1,0:T(8,128)(2,1)S(1)}, bf16[4,216,128]{2,1,0:T(8,128)(2,1)S(1)}, u32[]{:S(2)}, u32[]{:S(2)}) collective-permute-start(bf16[4,216,128]{2,1,0:T(8,128)(2,1)S(1)} %get-tuple-element.54), channel_id=1, source_target_pairs={{0,4},{1,17},{2,6},{3,19},{4,0},{5,21},{6,2},{7,23},{8,12},{9,25},... | collective-permute-start | bytes 663560 | tf_op jit(solution)/shard_map/ppermute | solution.py:687
  32.7 7.7 %collective-permute-start.12 = (bf16[4,216,128]{2,1,0:T(8,128)(2,1)S(1)}, bf16[4,216,128]{2,1,0:T(8,128)(2,1)S(1)}, u32[]{:S(2)}, u32[]{:S(2)}) collective-permute-start(bf16[4,216,128]{2,1,0:T(8,128)(2,1)S(1)} %get-tuple-element.55), channel_id=1, source_target_pairs={{0,6},{1,25},{2,4},{3,27},{4,2},{5,29},{6,0},{7,31},{8,14},{9,17},... | collective-permute-start | bytes 663560 | tf_op jit(solution)/shard_map/ppermute | solution.py:687
  40.5 6.0 %collective-permute-start.13 = (bf16[216,128]{1,0:T(8,128)(2,1)S(1)}, bf16[216,128]{1,0:T(8,128)(2,1)S(1)}, u32[]{:S(2)}, u32[]{:S(2)}) collective-permute-start(bf16[216,128]{1,0:T(8,128)(2,1)S(1)} %get-tuple-element.68), channel_id=1, source_target_pairs={{0,24},{1,7},{2,26},{3,5},{4,28},{5,3},{6,30},{7,1},{8,16},{9,15},... | collective-permute-start | bytes 165896 | tf_op jit(solution)/shard_map/ppermute | solution.py:687
  42.0 5.1 %collective-permute-start.14 = (bf16[216,128]{1,0:T(8,128)(2,1)S(1)}, bf16[216,128]{1,0:T(8,128)(2,1)S(1)}, u32[]{:S(2)}, u32[]{:S(2)}) collective-permute-start(bf16[216,128]{1,0:T(8,128)(2,1)S(1)} %get-tuple-element.69), channel_id=1, source_target_pairs={{0,16},{1,5},{2,18},{3,7},{4,20},{5,1},{6,22},{7,3},{8,24},{9,13},... | collective-permute-start | bytes 165896 | tf_op jit(solution)/shard_map/ppermute | solution.py:687
  43.3 4.3 %collective-permute-start.15 = (bf16[216,128]{1,0:T(8,128)(2,1)S(1)}, bf16[216,128]{1,0:T(8,128)(2,1)S(1)}, u32[]{:S(2)}, u32[]{:S(2)}) collective-permute-start(bf16[216,128]{1,0:T(8,128)(2,1)S(1)} %get-tuple-element.70), channel_id=1, source_target_pairs={{0,8},{1,3},{2,10},{3,1},{4,12},{5,7},{6,14},{7,5},{8,0},{9,11},{1... | collective-permute-start | bytes 165896 | tf_op jit(solution)/shard_map/ppermute | solution.py:687
  47.7 1.4 %collective-permute-start.16 = (f32[216,128]{1,0:T(8,128)S(1)}, f32[216,128]{1,0:T(8,128)S(1)}, u32[]{:S(2)}, u32[]{:S(2)}) collective-permute-start(f32[216,128]{1,0:T(8,128)S(1)} %shard_map.109), channel_id=1, source_target_pairs={{0,1},{1,0},{2,3},{3,2},{4,5},{5,4},{6,7},{7,6},{8,9},{9,8},{10,11... | collective-permute-start | bytes 331784 | tf_op jit(solution)/shard_map/ppermute | solution.py:675

commit v6 on v5

--- a/solution.py
+++ b/solution.py
@@ -462,7 +462,7 @@
     blocks_other, refs = refs[:side], refs[side:]
     tile_ref, act_ref, act_grad_ref, wide_other = refs[:4]
     outs, refs = refs[4 : 4 + side], refs[4 + side :]
-    w_ref, wl_ref, total_ref, x_scratch, left_ref = refs
+    w_ref, wl_ref, total_ref, x_scratch, right_ref = refs
     core, high, low = position(side)
     frames, rows, columns, channels = tile_ref.shape
     band_rows = rows // 2
@@ -495,22 +495,24 @@
 
     upstream = jnp.where(core == 0, act_grad_ref[...].astype(F32), out_grad_ref[...].astype(F32))
     upstream = upstream.reshape(frames, rows * columns, channels)
-    turned = [upstream[t].T for t in range(frames)]
     for a in range(3):
         for t in range(frames):
-            met = [turned[s] for s in range(frames) if max(s + a - 2, 0) == t]
-            met = sum(met[1:], met[0]) if met else jnp.zeros_like(turned[0])
+            met = [upstream[s] for s in range(frames) if max(s + a - 2, 0) == t]
+            met = sum(met[1:], met[0]) if met else jnp.zeros_like(upstream[0])
             frame = slice(a * channels, (a + 1) * channels)
-            left_ref[frame, t * rows * columns : (t + 1) * rows * columns] = met.astype(BF16)
-    product = jnp.dot(
-        left_ref[...], x_scratch[core].reshape(cells, nine), preferred_element_type=F32
+            right_ref[t * rows * columns : (t + 1) * rows * columns, frame] = met.astype(BF16)
+    product = lax.dot_general(
+        x_scratch[core].reshape(cells, nine),
+        right_ref[...],
+        (((0,), (0,)), ((), ())),
+        preferred_element_type=F32,
     )
     for a in range(3):
         for piece in range(9):
             at = (a * 9 + piece) * channels
-            lanes = slice(piece * channels, (piece + 1) * channels)
-            block = product[a * channels : (a + 1) * channels, lanes]
-            total_ref[at : at + channels, :] = block.T * scale
+            place = slice(piece * channels, (piece + 1) * channels)
+            block = product[place, a * channels : (a + 1) * channels]
+            total_ref[at : at + channels, :] = block * scale
     p, q = walk(core, high, low)
     for k in range(side):
         for j in range(side):
@@ -542,7 +544,7 @@
             pltpu.VMEM((3 * channels, 9 * channels), BF16),
             pltpu.VMEM((27 * channels, channels), F32),
             pltpu.VMEM((2, frames, rows, columns, 9 * channels), BF16),
-            pltpu.VMEM((3 * channels, cells), BF16),
+            pltpu.VMEM((cells, 3 * channels), BF16),
         ],
         compiler_params=pltpu.CompilerParams(vmem_limit_bytes=32 * 1024 * 1024),
         cost_estimate=pl.CostEstimate(flops=flops, bytes_accessed=4_000_000, transcendentals=0),
@@ -694,7 +696,8 @@
     kept_block, kept_cot = keep(packed[0], cot[0])
     relayed = relay(kept_cot, [kept_block, *arrived], columns, base)
     blocks_mine = send(relayed, (1, 0))
-    blocks_other = [exchange(block) for block in blocks_mine]
+    own_block, _ = lax.optimization_barrier((blocks_mine[0], blocks_mine[1]))
+    blocks_other = [exchange(block) for block in (own_block, *blocks_mine[1:])]
 
     scale = 1.0 / math.sqrt(frames * band_rows * columns * 2 * wide_size)
     prepared = prepare(lengths, blocks_mine, blocks_other[0], cot.shape[1:], share)

time: 50 us -> 50 us (level)
  starting transfers between devices: 17.7 us -> 18.2 us
  waiting for transfers between devices: 18.8 us -> 18.3 us
    ppermute x12, waiting for transfers between devices: 17.1 us -> 16.6 us  [send(): lax.ppermute(blocks[k], ('wide', 'rows'), pairs(axes, k))]
    ppermute x5, starting transfers between devices: 0.08 us -> 0.59 us  [exchange(): return lax.ppermute(block, 'rows', [(0, 1), (1, 0)])]
where the time goes in v6:
time: 50 us; the launch traced here: 49.8 us
  waiting for transfers between devices  18.3 us (37%)
  starting transfers between devices  18.2 us (36%)
  Pallas kernels  9.35 us (19%)
  local copies, waits for them, and re-layouts  1.78 us (4%)
  between operations  1.37 us (3%)
  other arithmetic  0.7 us (1%)
    ppermute x12, starting transfers between devices, send(): lax.ppermute(blocks[k], ('wide', 'rows'), pairs(axes, k))  17.7 us
    ppermute x12, waiting for transfers between devices, send(): lax.ppermute(blocks[k], ('wide', 'rows'), pairs(axes, k))  16.6 us
    pallas_call x1, Pallas kernels, unit(): pl.pallas_call(functools.partial(unit_kernel, scale=scale, side=side, sha...  3.77 us
    pallas_call x1, Pallas kernels, finish(): pl.pallas_call(finish_kernel, out_shape=[band] * 2, in_specs=whole(len(ke...  2.48 us
    pallas_call x1, Pallas kernels, pack(): pl.pallas_call(pack_kernel, out_shape=[jax.ShapeDtypeStruct((rows, channe...  2.36 us
    unnamed x4, local copies, waits for them, and re-layouts  1.78 us
    ppermute x5, waiting for transfers between devices, exchange(): return lax.ppermute(block, 'rows', [(0, 1), (1, 0)])  1.7 us
  transfers between devices with their start and end apart: 17, of which 12 were waited for; matrix products, arithmetic and copies ran while one was open for 0% of the time, Pallas kernels for 6%

profile of v6, /device:TPU:0, one launch (start us, length us, event | category | flops | bytes accessed | tf_op | source)
XLA Modules:
  0.0 49.8 jit_solution(322889739773735652)
XLA Ops:
  0.6 2.4 %shard_map.102 = (bf16[352,128]{1,0:T(8,128)(2,1)}, bf16[352,128]{1,0:T(8,128)(2,1)}, bf16[352,128]{1,0:T(8,128)(2,1)}, bf16[352,128]{1,0:T(8,128)(2,1)}) custom-call(s32[10]{0:T(128)} %bitcast.8, s32[10]{0:T(128)} %bitcast.9, bf16[10,32,128]{2,1,0:T(8,128)(2,1)} %bitcast.7, bf16[216,128]{1,0:T(8,128)(2,1)} %first_hbm.1, bf16[216,128]{1,0:T(8,128)(2,1)} %second_hbm.1), custom_call_target="tpu_custom_call" | custom-call | tf_op jit(solution)/shard_map/pallas_call | solution.py:228
  3.0 5.1 %collective-permute-start = (bf16[352,128]{1,0:T(8,128)(2,1)}, bf16[352,128]{1,0:T(8,128)(2,1)S(1)}, u32[]{:S(2)}, u32[]{:S(2)}) collective-permute-start(bf16[352,128]{1,0:T(8,128)(2,1)} %get-tuple-element.41), channel_id=1, source_target_pairs={{0,24},{1,7},{2,26},{3,5},{4,28},{5,3},{6,30},{7,1},{8,16},{9,15},... | collective-permute-start | bytes 270344 | tf_op jit(solution)/shard_map/ppermute | solution.py:689
  8.1 0.0 collective-permute-start.1
  8.1 0.6 %collective-permute-start.2 = (bf16[352,128]{1,0:T(8,128)(2,1)}, bf16[352,128]{1,0:T(8,128)(2,1)S(1)}, u32[]{:S(2)}, u32[]{:S(2)}) collective-permute-start(bf16[352,128]{1,0:T(8,128)(2,1)} %get-tuple-element.43), channel_id=1, source_target_pairs={{0,8},{1,3},{2,10},{3,1},{4,12},{5,7},{6,14},{7,5},{8,0},{9,11},{1... | collective-permute-start | bytes 270344 | tf_op jit(solution)/shard_map/ppermute | solution.py:689
  8.8 0.0 copy-start
  8.8 0.9 %copy-done = bf16[352,128]{1,0:T(8,128)(2,1)S(1)} copy-done((bf16[352,128]{1,0:T(8,128)(2,1)S(1)}, bf16[352,128]{1,0:T(8,128)(2,1)}, u32[]{:S(2)}) %copy-start) | copy-done | bytes 90136
  9.6 0.0 copy-start.1
  9.6 0.9 %copy-done.1 = bf16[1,5,2,32,128]{4,3,2,1,0:T(8,128)(2,1)S(1)} copy-done((bf16[1,5,2,32,128]{4,3,2,1,0:T(8,128)(2,1)S(1)}, bf16[1,5,2,32,128]{4,3,2,1,0:T(8,128)(2,1)}, u32[]{:S(2)}) %copy-start.1) | copy-done | bytes 81944
  10.5 0.4 collective-permute-done.refs_0_
  10.9 2.9 %collective-permute-done.1.refs_1_ = bf16[352,128]{1,0:T(8,128)(2,1)S(1)} collective-permute-done((bf16[352,128]{1,0:T(8,128)(2,1)}, bf16[352,128]{1,0:T(8,128)(2,1)S(1)}, u32[]{:S(2)}, u32[]{:S(2)}) %collective-permute-start.1) | collective-permute-done | bytes 90144 | tf_op jit(solution)/shard_map/ppermute | solution.py:689
  13.9 0.0 collective-permute-done.2.refs_2_
  13.9 0.1 shard_map.104
  14.0 1.6 %collective-permute-start.3 = (bf16[1024,128]{1,0:T(8,128)(2,1)S(1)}, bf16[1024,128]{1,0:T(8,128)(2,1)S(1)}, u32[]{:S(2)}, u32[]{:S(2)}) collective-permute-start(bf16[1024,128]{1,0:T(8,128)(2,1)S(1)} %get-tuple-element.46), channel_id=1, source_target_pairs={{0,2},{1,9},{2,0},{3,11},{4,6},{5,13},{6,4},{7,15},{8,10},{9,1},{1... | collective-permute-start | bytes 786440 | tf_op jit(solution)/shard_map/ppermute | solution.py:689
  15.6 2.1 %collective-permute-start.4 = (bf16[1024,128]{1,0:T(8,128)(2,1)S(1)}, bf16[1024,128]{1,0:T(8,128)(2,1)S(1)}, u32[]{:S(2)}, u32[]{:S(2)}) collective-permute-start(bf16[1024,128]{1,0:T(8,128)(2,1)S(1)} %get-tuple-element.47), channel_id=1, source_target_pairs={{0,4},{1,17},{2,6},{3,19},{4,0},{5,21},{6,2},{7,23},{8,12},{9,25},... | collective-permute-start | bytes 786440 | tf_op jit(solution)/shard_map/ppermute | solution.py:689
  17.6 0.0 collective-permute-start.5
  17.6 2.8 %collective-permute-done.3.refs_1_ = bf16[1024,128]{1,0:T(8,128)(2,1)S(1)} collective-permute-done((bf16[1024,128]{1,0:T(8,128)(2,1)S(1)}, bf16[1024,128]{1,0:T(8,128)(2,1)S(1)}, u32[]{:S(2)}, u32[]{:S(2)}) %collective-permute-start.3) | collective-permute-done | bytes 262176 | tf_op jit(solution)/shard_map/ppermute | solution.py:689
  20.4 0.0 collective-permute-start.6
  20.4 0.5 %collective-permute-start.7 = (bf16[1024,128]{1,0:T(8,128)(2,1)S(1)}, bf16[1024,128]{1,0:T(8,128)(2,1)S(1)}, u32[]{:S(2)}, u32[]{:S(2)}) collective-permute-start(bf16[1024,128]{1,0:T(8,128)(2,1)S(1)} %collective-permute-done.3.refs_1_), channel_id=1, source_target_pairs={{0,1},{1,0},{2,3},{3,2},{4,5},{5,4},{6,7},{7,6},{8,9},{9,8},{10,11... | collective-permute-start | bytes 786440 | tf_op jit(solution)/shard_map/ppermute | solution.py:677
  20.9 3.4 %collective-permute-done.4.refs_2_ = bf16[1024,128]{1,0:T(8,128)(2,1)S(1)} collective-permute-done((bf16[1024,128]{1,0:T(8,128)(2,1)S(1)}, bf16[1024,128]{1,0:T(8,128)(2,1)S(1)}, u32[]{:S(2)}, u32[]{:S(2)}) %collective-permute-start.4) | collective-permute-done | bytes 262176 | tf_op jit(solution)/shard_map/ppermute | solution.py:689
  24.3 0.0 collective-permute-start.8
  24.3 0.6 %collective-permute-done.5.refs_3_ = bf16[1024,128]{1,0:T(8,128)(2,1)S(1)} collective-permute-done((bf16[1024,128]{1,0:T(8,128)(2,1)S(1)}, bf16[1024,128]{1,0:T(8,128)(2,1)S(1)}, u32[]{:S(2)}, u32[]{:S(2)}) %collective-permute-start.5) | collective-permute-done | bytes 262176 | tf_op jit(solution)/shard_map/ppermute | solution.py:689
  24.9 0.0 collective-permute-start.9
  25.6 0.0 collective-permute-done.6.refs_4_.refs_0_
  25.6 0.5 shard_map.105
  26.0 0.0 collective-permute-done.7.refs_1_
  26.0 0.0 collective-permute-done.8.refs_2_
  26.1 0.4 collective-permute-done.9.refs_3_
  26.4 3.8 %shard_map.106 = (f32[5,4,32,128]{3,2,1,0:T(8,128)S(1)}, bf16[5,4,32,128]{3,2,1,0:T(8,128)(2,1)S(1)}, bf16[5,4,32,128]{3,2,1,0:T(8,128)(2,1)S(1)}, f32[3456,128]...) custom-call(f32[5,2,32,128]{3,2,1,0:T(8,128)S(1)} %get-tuple-element, ...), custom_call_target="tpu_custom_call" | custom-call | flops 1698693120 | bytes 4000000 | tf_op jit(solution)/shard_map/pallas_call | solution.py:531
  30.2 1.4 %collective-permute-start.10 = (bf16[4,216,128]{2,1,0:T(8,128)(2,1)S(1)}, bf16[4,216,128]{2,1,0:T(8,128)(2,1)S(1)}, u32[]{:S(2)}, u32[]{:S(2)}) collective-permute-start(bf16[4,216,128]{2,1,0:T(8,128)(2,1)S(1)} %get-tuple-element.55), channel_id=1, source_target_pairs={{0,2},{1,9},{2,0},{3,11},{4,6},{5,13},{6,4},{7,15},{8,10},{9,1},{1... | collective-permute-start | bytes 663560 | tf_op jit(solution)/shard_map/ppermute | solution.py:689
  31.6 1.0 %collective-permute-start.11 = (bf16[4,216,128]{2,1,0:T(8,128)(2,1)S(1)}, bf16[4,216,128]{2,1,0:T(8,128)(2,1)S(1)}, u32[]{:S(2)}, u32[]{:S(2)}) collective-permute-start(bf16[4,216,128]{2,1,0:T(8,128)(2,1)S(1)} %get-tuple-element.56), channel_id=1, source_target_pairs={{0,4},{1,17},{2,6},{3,19},{4,0},{5,21},{6,2},{7,23},{8,12},{9,25},... | collective-permute-start | bytes 663560 | tf_op jit(solution)/shard_map/ppermute | solution.py:689
  32.7 1.4 %collective-permute-start.12 = (bf16[4,216,128]{2,1,0:T(8,128)(2,1)S(1)}, bf16[4,216,128]{2,1,0:T(8,128)(2,1)S(1)}, u32[]{:S(2)}, u32[]{:S(2)}) collective-permute-start(bf16[4,216,128]{2,1,0:T(8,128)(2,1)S(1)} %get-tuple-element.57), channel_id=1, source_target_pairs={{0,6},{1,25},{2,4},{3,27},{4,2},{5,29},{6,0},{7,31},{8,14},{9,17},... | collective-permute-start | bytes 663560 | tf_op jit(solution)/shard_map/ppermute | solution.py:689
  34.0 2.5 %shard_map.107 = (bf16[5,2,32,128]{3,2,1,0:T(8,128)(2,1)}, bf16[5,2,32,128]{3,2,1,0:T(8,128)(2,1)}) custom-call(f32[5,4,32,128]{3,2,1,0:T(8,128)S(1)} %get-tuple-element.58.tile_ref, bf16[5,4,32,128]{3,2,1,0:T(8,128)(2,1)S(1)} %get-tuple-element.59.act_ref, bf16[5,4,32,128]{3,2,1,0:T(8,128)(2,1)S(1)} %get-tuple-element.52.out_grad_ref, ...), custom_call_target="tpu_custom_call" | custom-call | flops 566231040 | bytes 2000000 | tf_op jit(solution)/shard_map/pallas_call | solution.py:612
  36.5 0.0 collective-permute-done.10.refs_2_
  36.5 2.0 %collective-permute-done.11.refs_1_ = bf16[4,216,128]{2,1,0:T(8,128)(2,1)S(1)} collective-permute-done((bf16[4,216,128]{2,1,0:T(8,128)(2,1)S(1)}, bf16[4,216,128]{2,1,0:T(8,128)(2,1)S(1)}, u32[]{:S(2)}, u32[]{:S(2)}) %collective-permute-start.11) | collective-permute-done | bytes 221216 | tf_op jit(solution)/shard_map/ppermute | solution.py:689
  38.5 1.8 %collective-permute-done.12.refs_0_ = bf16[4,216,128]{2,1,0:T(8,128)(2,1)S(1)} collective-permute-done((bf16[4,216,128]{2,1,0:T(8,128)(2,1)S(1)}, bf16[4,216,128]{2,1,0:T(8,128)(2,1)S(1)}, u32[]{:S(2)}, u32[]{:S(2)}) %collective-permute-start.12) | collective-permute-done | bytes 221216 | tf_op jit(solution)/shard_map/ppermute | solution.py:689
  40.3 0.1 shard_map.108
  40.4 1.5 %collective-permute-start.13 = (bf16[216,128]{1,0:T(8,128)(2,1)S(1)}, bf16[216,128]{1,0:T(8,128)(2,1)S(1)}, u32[]{:S(2)}, u32[]{:S(2)}) collective-permute-start(bf16[216,128]{1,0:T(8,128)(2,1)S(1)} %get-tuple-element.70), channel_id=1, source_target_pairs={{0,24},{1,7},{2,26},{3,5},{4,28},{5,3},{6,30},{7,1},{8,16},{9,15},... | collective-permute-start | bytes 165896 | tf_op jit(solution)/shard_map/ppermute | solution.py:689
  42.0 1.3 %collective-permute-start.14 = (bf16[216,128]{1,0:T(8,128)(2,1)S(1)}, bf16[216,128]{1,0:T(8,128)(2,1)S(1)}, u32[]{:S(2)}, u32[]{:S(2)}) collective-permute-start(bf16[216,128]{1,0:T(8,128)(2,1)S(1)} %get-tuple-element.71), channel_id=1, source_target_pairs={{0,16},{1,5},{2,18},{3,7},{4,20},{5,1},{6,22},{7,3},{8,24},{9,13},... | collective-permute-start | bytes 165896 | tf_op jit(solution)/shard_map/ppermute | solution.py:689
  43.3 1.6 %collective-permute-start.15 = (bf16[216,128]{1,0:T(8,128)(2,1)S(1)}, bf16[216,128]{1,0:T(8,128)(2,1)S(1)}, u32[]{:S(2)}, u32[]{:S(2)}) collective-permute-start(bf16[216,128]{1,0:T(8,128)(2,1)S(1)} %get-tuple-element.72), channel_id=1, source_target_pairs={{0,8},{1,3},{2,10},{3,1},{4,12},{5,7},{6,14},{7,5},{8,0},{9,11},{1... | collective-permute-start | bytes 165896 | tf_op jit(solution)/shard_map/ppermute | solution.py:689
  44.9 1.6 %collective-permute-done.13.refs_0_ = bf16[216,128]{1,0:T(8,128)(2,1)S(1)} collective-permute-done((bf16[216,128]{1,0:T(8,128)(2,1)S(1)}, bf16[216,128]{1,0:T(8,128)(2,1)S(1)}, u32[]{:S(2)}, u32[]{:S(2)}) %collective-permute-start.13) | collective-permute-done | bytes 55328 | tf_op jit(solution)/shard_map/ppermute | solution.py:689
  46.5 0.6 %collective-permute-done.14.refs_1_ = bf16[216,128]{1,0:T(8,128)(2,1)S(1)} collective-permute-done((bf16[216,128]{1,0:T(8,128)(2,1)S(1)}, bf16[216,128]{1,0:T(8,128)(2,1)S(1)}, u32[]{:S(2)}, u32[]{:S(2)}) %collective-permute-start.14) | collective-permute-done | bytes 55328 | tf_op jit(solution)/shard_map/ppermute | solution.py:689
  47.1 0.6 %collective-permute-done.15.refs_2_ = bf16[216,128]{1,0:T(8,128)(2,1)S(1)} collective-permute-done((bf16[216,128]{1,0:T(8,128)(2,1)S(1)}, bf16[216,128]{1,0:T(8,128)(2,1)S(1)}, u32[]{:S(2)}, u32[]{:S(2)}) %collective-permute-start.15) | collective-permute-done | bytes 55328 | tf_op jit(solution)/shard_map/ppermute | solution.py:689
  47.7 0.1 collective-permute-start.16
  47.8 1.3 %collective-permute-done.16 = f32[216,128]{1,0:T(8,128)S(1)} collective-permute-done((f32[216,128]{1,0:T(8,128)S(1)}, f32[216,128]{1,0:T(8,128)S(1)}, u32[]{:S(2)}, u32[]{:S(2)}) %collective-permute-start.16) | collective-permute-done | bytes 110624 | tf_op jit(solution)/shard_map/ppermute | solution.py:677
  49.1 0.7 %broadcast_select_fusion = (f32[216,128]{1,0:T(8,128)}, f32[216,128]{1,0:T(8,128)}) fusion(f32[216,128]{1,0:T(8,128)S(1)} %collective-permute-done.16, f32[216,128]{1,0:T(8,128)S(1)} %shard_map.109, pred[]{:T(512)S(6)} %eq.4), kind=kLoop, calls=%fused_computation | loop fusion | flops 55296 | bytes 442369 | tf_op jit(solution)/shard_map/jit(_where)/select_n | solution.py:712
  (2 shorter events, 0.0 us)
Async XLA Ops:
  3.0 7.9 %collective-permute-start = (bf16[352,128]{1,0:T(8,128)(2,1)}, bf16[352,128]{1,0:T(8,128)(2,1)S(1)}, u32[]{:S(2)}, u32[]{:S(2)}) collective-permute-start(bf16[352,128]{1,0:T(8,128)(2,1)} %get-tuple-element.41), channel_id=1, source_target_pairs={{0,24},{1,7},{2,26},{3,5},{4,28},{5,3},{6,30},{7,1},{8,16},{9,15},... | collective-permute-start | bytes 270344 | tf_op jit(solution)/shard_map/ppermute | solution.py:689
  8.1 5.7 %collective-permute-start.1 = (bf16[352,128]{1,0:T(8,128)(2,1)}, bf16[352,128]{1,0:T(8,128)(2,1)S(1)}, u32[]{:S(2)}, u32[]{:S(2)}) collective-permute-start(bf16[352,128]{1,0:T(8,128)(2,1)} %get-tuple-element.42), channel_id=1, source_target_pairs={{0,16},{1,5},{2,18},{3,7},{4,20},{5,1},{6,22},{7,3},{8,24},{9,13},... | collective-permute-start | bytes 270344 | tf_op jit(solution)/shard_map/ppermute | solution.py:689
  8.1 5.7 %collective-permute-start.2 = (bf16[352,128]{1,0:T(8,128)(2,1)}, bf16[352,128]{1,0:T(8,128)(2,1)S(1)}, u32[]{:S(2)}, u32[]{:S(2)}) collective-permute-start(bf16[352,128]{1,0:T(8,128)(2,1)} %get-tuple-element.43), channel_id=1, source_target_pairs={{0,8},{1,3},{2,10},{3,1},{4,12},{5,7},{6,14},{7,5},{8,0},{9,11},{1... | collective-permute-start | bytes 270344 | tf_op jit(solution)/shard_map/ppermute | solution.py:689
  8.8 0.9 %copy-start = (bf16[352,128]{1,0:T(8,128)(2,1)S(1)}, bf16[352,128]{1,0:T(8,128)(2,1)}, u32[]{:S(2)}) copy-start(bf16[352,128]{1,0:T(8,128)(2,1)} %get-tuple-element.39.refs_0_) | copy-start | bytes 270340
  9.6 0.9 %copy-start.1 = (bf16[1,5,2,32,128]{4,3,2,1,0:T(8,128)(2,1)S(1)}, bf16[1,5,2,32,128]{4,3,2,1,0:T(8,128)(2,1)}, u32[]{:S(2)}) copy-start(bf16[1,5,2,32,128]{4,3,2,1,0:T(8,128)(2,1)} %param.11) | copy-start | bytes 245764
  14.0 6.4 %collective-permute-start.3 = (bf16[1024,128]{1,0:T(8,128)(2,1)S(1)}, bf16[1024,128]{1,0:T(8,128)(2,1)S(1)}, u32[]{:S(2)}, u32[]{:S(2)}) collective-permute-start(bf16[1024,128]{1,0:T(8,128)(2,1)S(1)} %get-tuple-element.46), channel_id=1, source_target_pairs={{0,2},{1,9},{2,0},{3,11},{4,6},{5,13},{6,4},{7,15},{8,10},{9,1},{1... | collective-permute-start | bytes 786440 | tf_op jit(solution)/shard_map/ppermute | solution.py:689
  15.6 8.8 %collective-permute-start.4 = (bf16[1024,128]{1,0:T(8,128)(2,1)S(1)}, bf16[1024,128]{1,0:T(8,128)(2,1)S(1)}, u32[]{:S(2)}, u32[]{:S(2)}) collective-permute-start(bf16[1024,128]{1,0:T(8,128)(2,1)S(1)} %get-tuple-element.47), channel_id=1, source_target_pairs={{0,4},{1,17},{2,6},{3,19},{4,0},{5,21},{6,2},{7,23},{8,12},{9,25},... | collective-permute-start | bytes 786440 | tf_op jit(solution)/shard_map/ppermute | solution.py:689
  17.6 7.3 %collective-permute-start.5 = (bf16[1024,128]{1,0:T(8,128)(2,1)S(1)}, bf16[1024,128]{1,0:T(8,128)(2,1)S(1)}, u32[]{:S(2)}, u32[]{:S(2)}) collective-permute-start(bf16[1024,128]{1,0:T(8,128)(2,1)S(1)} %get-tuple-element.48), channel_id=1, source_target_pairs={{0,6},{1,25},{2,4},{3,27},{4,2},{5,29},{6,0},{7,31},{8,14},{9,17},... | collective-permute-start | bytes 786440 | tf_op jit(solution)/shard_map/ppermute | solution.py:689
  20.4 5.1 %collective-permute-start.6 = (bf16[1344,128]{1,0:T(8,128)(2,1)S(1)}, bf16[1344,128]{1,0:T(8,128)(2,1)S(1)}, u32[]{:S(2)}, u32[]{:S(2)}) collective-permute-start(bf16[1344,128]{1,0:T(8,128)(2,1)S(1)} %get-tuple-element.49.refs_0_), channel_id=1, source_target_pairs={{0,1},{1,0},{2,3},{3,2},{4,5},{5,4},{6,7},{7,6},{8,9},{9,8},{10,11... | collective-permute-start | bytes 1032200 | tf_op jit(solution)/shard_map/ppermute | solution.py:677
  20.4 5.6 %collective-permute-start.7 = (bf16[1024,128]{1,0:T(8,128)(2,1)S(1)}, bf16[1024,128]{1,0:T(8,128)(2,1)S(1)}, u32[]{:S(2)}, u32[]{:S(2)}) collective-permute-start(bf16[1024,128]{1,0:T(8,128)(2,1)S(1)} %collective-permute-done.3.refs_1_), channel_id=1, source_target_pairs={{0,1},{1,0},{2,3},{3,2},{4,5},{5,4},{6,7},{7,6},{8,9},{9,8},{10,11... | collective-permute-start | bytes 786440 | tf_op jit(solution)/shard_map/ppermute | solution.py:677
  24.3 1.7 %collective-permute-start.8 = (bf16[1024,128]{1,0:T(8,128)(2,1)S(1)}, bf16[1024,128]{1,0:T(8,128)(2,1)S(1)}, u32[]{:S(2)}, u32[]{:S(2)}) collective-permute-start(bf16[1024,128]{1,0:T(8,128)(2,1)S(1)} %collective-permute-done.4.refs_2_), channel_id=1, source_target_pairs={{0,1},{1,0},{2,3},{3,2},{4,5},{5,4},{6,7},{7,6},{8,9},{9,8},{10,11... | collective-permute-start | bytes 786440 | tf_op jit(solution)/shard_map/ppermute | solution.py:677
  24.9 1.5 %collective-permute-start.9 = (bf16[1024,128]{1,0:T(8,128)(2,1)S(1)}, bf16[1024,128]{1,0:T(8,128)(2,1)S(1)}, u32[]{:S(2)}, u32[]{:S(2)}) collective-permute-start(bf16[1024,128]{1,0:T(8,128)(2,1)S(1)} %collective-permute-done.5.refs_3_), channel_id=1, source_target_pairs={{0,1},{1,0},{2,3},{3,2},{4,5},{5,4},{6,7},{7,6},{8,9},{9,8},{10,11... | collective-permute-start | bytes 786440 | tf_op jit(solution)/shard_map/ppermute | solution.py:677
  30.2 6.3 %collective-permute-start.10 = (bf16[4,216,128]{2,1,0:T(8,128)(2,1)S(1)}, bf16[4,216,128]{2,1,0:T(8,128)(2,1)S(1)}, u32[]{:S(2)}, u32[]{:S(2)}) collective-permute-start(bf16[4,216,128]{2,1,0:T(8,128)(2,1)S(1)} %get-tuple-element.55), channel_id=1, source_target_pairs={{0,2},{1,9},{2,0},{3,11},{4,6},{5,13},{6,4},{7,15},{8,10},{9,1},{1... | collective-permute-start | bytes 663560 | tf_op jit(solution)/shard_map/ppermute | solution.py:689
  31.6 6.9 %collective-permute-start.11 = (bf16[4,216,128]{2,1,0:T(8,128)(2,1)S(1)}, bf16[4,216,128]{2,1,0:T(8,128)(2,1)S(1)}, u32[]{:S(2)}, u32[]{:S(2)}) collective-permute-start(bf16[4,216,128]{2,1,0:T(8,128)(2,1)S(1)} %get-tuple-element.56), channel_id=1, source_target_pairs={{0,4},{1,17},{2,6},{3,19},{4,0},{5,21},{6,2},{7,23},{8,12},{9,25},... | collective-permute-start | bytes 663560 | tf_op jit(solution)/shard_map/ppermute | solution.py:689
  32.7 7.7 %collective-permute-start.12 = (bf16[4,216,128]{2,1,0:T(8,128)(2,1)S(1)}, bf16[4,216,128]{2,1,0:T(8,128)(2,1)S(1)}, u32[]{:S(2)}, u32[]{:S(2)}) collective-permute-start(bf16[4,216,128]{2,1,0:T(8,128)(2,1)S(1)} %get-tuple-element.57), channel_id=1, source_target_pairs={{0,6},{1,25},{2,4},{3,27},{4,2},{5,29},{6,0},{7,31},{8,14},{9,17},... | collective-permute-start | bytes 663560 | tf_op jit(solution)/shard_map/ppermute | solution.py:689
  40.4 6.0 %collective-permute-start.13 = (bf16[216,128]{1,0:T(8,128)(2,1)S(1)}, bf16[216,128]{1,0:T(8,128)(2,1)S(1)}, u32[]{:S(2)}, u32[]{:S(2)}) collective-permute-start(bf16[216,128]{1,0:T(8,128)(2,1)S(1)} %get-tuple-element.70), channel_id=1, source_target_pairs={{0,24},{1,7},{2,26},{3,5},{4,28},{5,3},{6,30},{7,1},{8,16},{9,15},... | collective-permute-start | bytes 165896 | tf_op jit(solution)/shard_map/ppermute | solution.py:689
  42.0 5.1 %collective-permute-start.14 = (bf16[216,128]{1,0:T(8,128)(2,1)S(1)}, bf16[216,128]{1,0:T(8,128)(2,1)S(1)}, u32[]{:S(2)}, u32[]{:S(2)}) collective-permute-start(bf16[216,128]{1,0:T(8,128)(2,1)S(1)} %get-tuple-element.71), channel_id=1, source_target_pairs={{0,16},{1,5},{2,18},{3,7},{4,20},{5,1},{6,22},{7,3},{8,24},{9,13},... | collective-permute-start | bytes 165896 | tf_op jit(solution)/shard_map/ppermute | solution.py:689
  43.3 4.3 %collective-permute-start.15 = (bf16[216,128]{1,0:T(8,128)(2,1)S(1)}, bf16[216,128]{1,0:T(8,128)(2,1)S(1)}, u32[]{:S(2)}, u32[]{:S(2)}) collective-permute-start(bf16[216,128]{1,0:T(8,128)(2,1)S(1)} %get-tuple-element.72), channel_id=1, source_target_pairs={{0,8},{1,3},{2,10},{3,1},{4,12},{5,7},{6,14},{7,5},{8,0},{9,11},{1... | collective-permute-start | bytes 165896 | tf_op jit(solution)/shard_map/ppermute | solution.py:689
  47.7 1.4 %collective-permute-start.16 = (f32[216,128]{1,0:T(8,128)S(1)}, f32[216,128]{1,0:T(8,128)S(1)}, u32[]{:S(2)}, u32[]{:S(2)}) collective-permute-start(f32[216,128]{1,0:T(8,128)S(1)} %shard_map.109), channel_id=1, source_target_pairs={{0,1},{1,0},{2,3},{3,2},{4,5},{5,4},{6,7},{7,6},{8,9},{9,8},{10,11... | collective-permute-start | bytes 331784 | tf_op jit(solution)/shard_map/ppermute | solution.py:677

commit v7 on v6

--- a/solution.py
+++ b/solution.py
@@ -696,7 +696,7 @@
     kept_block, kept_cot = keep(packed[0], cot[0])
     relayed = relay(kept_cot, [kept_block, *arrived], columns, base)
     blocks_mine = send(relayed, (1, 0))
-    own_block, _ = lax.optimization_barrier((blocks_mine[0], blocks_mine[1]))
+    own_block, _ = lax.optimization_barrier((blocks_mine[0], blocks_mine[2]))
     blocks_other = [exchange(block) for block in (own_block, *blocks_mine[1:])]
 
     scale = 1.0 / math.sqrt(frames * band_rows * columns * 2 * wide_size)

time: 50 us -> 50.2 us (level)
  no operation moved by 1% of the time
where the time goes in v7:
time: 50.2 us; the launch traced here: 50 us
  waiting for transfers between devices  18.7 us (37%)
  starting transfers between devices  18.1 us (36%)
  Pallas kernels  9.36 us (19%)
  local copies, waits for them, and re-layouts  1.78 us (4%)
  between operations  1.37 us (3%)
  other arithmetic  0.7 us (1%)
    ppermute x12, starting transfers between devices, send(): lax.ppermute(blocks[k], ('wide', 'rows'), pairs(axes, k))  17.5 us
    ppermute x12, waiting for transfers between devices, send(): lax.ppermute(blocks[k], ('wide', 'rows'), pairs(axes, k))  17 us
    pallas_call x1, Pallas kernels, unit(): pl.pallas_call(functools.partial(unit_kernel, scale=scale, side=side, sha...  3.78 us
    pallas_call x1, Pallas kernels, finish(): pl.pallas_call(finish_kernel, out_shape=[band] * 2, in_specs=whole(len(ke...  2.48 us
    pallas_call x1, Pallas kernels, pack(): pl.pallas_call(pack_kernel, out_shape=[jax.ShapeDtypeStruct((rows, channe...  2.36 us
    unnamed x4, local copies, waits for them, and re-layouts  1.78 us
    ppermute x5, waiting for transfers between devices, exchange(): return lax.ppermute(block, 'rows', [(0, 1), (1, 0)])  1.7 us
  transfers between devices with their start and end apart: 17, of which 12 were waited for; matrix products, arithmetic and copies ran while one was open for 0% of the time, Pallas kernels for 6%

profile of v7, /device:TPU:0, one launch (start us, length us, event | category | flops | bytes accessed | tf_op | source)
XLA Modules:
  0.0 50.0 jit_solution(4792475250175856089)
XLA Ops:
  0.6 2.4 %shard_map.102 = (bf16[352,128]{1,0:T(8,128)(2,1)}, bf16[352,128]{1,0:T(8,128)(2,1)}, bf16[352,128]{1,0:T(8,128)(2,1)}, bf16[352,128]{1,0:T(8,128)(2,1)}) custom-call(s32[10]{0:T(128)} %bitcast.8, s32[10]{0:T(128)} %bitcast.9, bf16[10,32,128]{2,1,0:T(8,128)(2,1)} %bitcast.7, bf16[216,128]{1,0:T(8,128)(2,1)} %first_hbm.1, bf16[216,128]{1,0:T(8,128)(2,1)} %second_hbm.1), custom_call_target="tpu_custom_call" | custom-call | tf_op jit(solution)/shard_map/pallas_call | solution.py:228
  3.0 5.1 %collective-permute-start = (bf16[352,128]{1,0:T(8,128)(2,1)}, bf16[352,128]{1,0:T(8,128)(2,1)S(1)}, u32[]{:S(2)}, u32[]{:S(2)}) collective-permute-start(bf16[352,128]{1,0:T(8,128)(2,1)} %get-tuple-element.41), channel_id=1, source_target_pairs={{0,24},{1,7},{2,26},{3,5},{4,28},{5,3},{6,30},{7,1},{8,16},{9,15},... | collective-permute-start | bytes 270344 | tf_op jit(solution)/shard_map/ppermute | solution.py:689
  8.1 0.0 collective-permute-start.1
  8.1 0.6 %collective-permute-start.2 = (bf16[352,128]{1,0:T(8,128)(2,1)}, bf16[352,128]{1,0:T(8,128)(2,1)S(1)}, u32[]{:S(2)}, u32[]{:S(2)}) collective-permute-start(bf16[352,128]{1,0:T(8,128)(2,1)} %get-tuple-element.43), channel_id=1, source_target_pairs={{0,8},{1,3},{2,10},{3,1},{4,12},{5,7},{6,14},{7,5},{8,0},{9,11},{1... | collective-permute-start | bytes 270344 | tf_op jit(solution)/shard_map/ppermute | solution.py:689
  8.8 0.0 copy-start
  8.8 0.9 %copy-done = bf16[352,128]{1,0:T(8,128)(2,1)S(1)} copy-done((bf16[352,128]{1,0:T(8,128)(2,1)S(1)}, bf16[352,128]{1,0:T(8,128)(2,1)}, u32[]{:S(2)}) %copy-start) | copy-done | bytes 90136
  9.6 0.0 copy-start.1
  9.6 0.9 %copy-done.1 = bf16[1,5,2,32,128]{4,3,2,1,0:T(8,128)(2,1)S(1)} copy-done((bf16[1,5,2,32,128]{4,3,2,1,0:T(8,128)(2,1)S(1)}, bf16[1,5,2,32,128]{4,3,2,1,0:T(8,128)(2,1)}, u32[]{:S(2)}) %copy-start.1) | copy-done | bytes 81944
  10.5 0.4 collective-permute-done.refs_0_
  10.9 2.9 %collective-permute-done.1.refs_1_ = bf16[352,128]{1,0:T(8,128)(2,1)S(1)} collective-permute-done((bf16[352,128]{1,0:T(8,128)(2,1)}, bf16[352,128]{1,0:T(8,128)(2,1)S(1)}, u32[]{:S(2)}, u32[]{:S(2)}) %collective-permute-start.1) | collective-permute-done | bytes 90144 | tf_op jit(solution)/shard_map/ppermute | solution.py:689
  13.8 0.0 collective-permute-done.2.refs_2_
  13.8 0.1 shard_map.104
  14.0 1.6 %collective-permute-start.4 = (bf16[1024,128]{1,0:T(8,128)(2,1)S(1)}, bf16[1024,128]{1,0:T(8,128)(2,1)S(1)}, u32[]{:S(2)}, u32[]{:S(2)}) collective-permute-start(bf16[1024,128]{1,0:T(8,128)(2,1)S(1)} %get-tuple-element.47), channel_id=1, source_target_pairs={{0,4},{1,17},{2,6},{3,19},{4,0},{5,21},{6,2},{7,23},{8,12},{9,25},... | collective-permute-start | bytes 786440 | tf_op jit(solution)/shard_map/ppermute | solution.py:689
  15.6 2.1 %collective-permute-start.3 = (bf16[1024,128]{1,0:T(8,128)(2,1)S(1)}, bf16[1024,128]{1,0:T(8,128)(2,1)S(1)}, u32[]{:S(2)}, u32[]{:S(2)}) collective-permute-start(bf16[1024,128]{1,0:T(8,128)(2,1)S(1)} %get-tuple-element.46), channel_id=1, source_target_pairs={{0,2},{1,9},{2,0},{3,11},{4,6},{5,13},{6,4},{7,15},{8,10},{9,1},{1... | collective-permute-start | bytes 786440 | tf_op jit(solution)/shard_map/ppermute | solution.py:689
  17.7 0.0 collective-permute-start.5
  17.7 2.7 %collective-permute-done.4.refs_2_ = bf16[1024,128]{1,0:T(8,128)(2,1)S(1)} collective-permute-done((bf16[1024,128]{1,0:T(8,128)(2,1)S(1)}, bf16[1024,128]{1,0:T(8,128)(2,1)S(1)}, u32[]{:S(2)}, u32[]{:S(2)}) %collective-permute-start.4) | collective-permute-done | bytes 262176 | tf_op jit(solution)/shard_map/ppermute | solution.py:689
  20.4 0.0 collective-permute-start.6
  20.4 0.5 %collective-permute-start.8 = (bf16[1024,128]{1,0:T(8,128)(2,1)S(1)}, bf16[1024,128]{1,0:T(8,128)(2,1)S(1)}, u32[]{:S(2)}, u32[]{:S(2)}) collective-permute-start(bf16[1024,128]{1,0:T(8,128)(2,1)S(1)} %collective-permute-done.4.refs_2_), channel_id=1, source_target_pairs={{0,1},{1,0},{2,3},{3,2},{4,5},{5,4},{6,7},{7,6},{8,9},{9,8},{10,11... | collective-permute-start | bytes 786440 | tf_op jit(solution)/shard_map/ppermute | solution.py:677
  20.9 1.1 %collective-permute-done.3.refs_1_ = bf16[1024,128]{1,0:T(8,128)(2,1)S(1)} collective-permute-done((bf16[1024,128]{1,0:T(8,128)(2,1)S(1)}, bf16[1024,128]{1,0:T(8,128)(2,1)S(1)}, u32[]{:S(2)}, u32[]{:S(2)}) %collective-permute-start.3) | collective-permute-done | bytes 262176 | tf_op jit(solution)/shard_map/ppermute | solution.py:689
  22.0 0.0 collective-permute-start.7
  22.0 2.9 %collective-permute-done.5.refs_3_ = bf16[1024,128]{1,0:T(8,128)(2,1)S(1)} collective-permute-done((bf16[1024,128]{1,0:T(8,128)(2,1)S(1)}, bf16[1024,128]{1,0:T(8,128)(2,1)S(1)}, u32[]{:S(2)}, u32[]{:S(2)}) %collective-permute-start.5) | collective-permute-done | bytes 262176 | tf_op jit(solution)/shard_map/ppermute | solution.py:689
  25.0 0.0 collective-permute-start.9
  25.6 0.0 collective-permute-done.6.refs_4_.refs_0_
  25.6 0.4 shard_map.105
  26.1 0.0 collective-permute-done.8.refs_2_
  26.1 0.0 collective-permute-done.7.refs_1_
  26.1 0.4 collective-permute-done.9.refs_3_
  26.5 3.8 %shard_map.106 = (f32[5,4,32,128]{3,2,1,0:T(8,128)S(1)}, bf16[5,4,32,128]{3,2,1,0:T(8,128)(2,1)S(1)}, bf16[5,4,32,128]{3,2,1,0:T(8,128)(2,1)S(1)}, f32[3456,128]...) custom-call(f32[5,2,32,128]{3,2,1,0:T(8,128)S(1)} %get-tuple-element, ...), custom_call_target="tpu_custom_call" | custom-call | flops 1698693120 | bytes 4000000 | tf_op jit(solution)/shard_map/pallas_call | solution.py:531
  30.3 1.5 %collective-permute-start.10 = (bf16[4,216,128]{2,1,0:T(8,128)(2,1)S(1)}, bf16[4,216,128]{2,1,0:T(8,128)(2,1)S(1)}, u32[]{:S(2)}, u32[]{:S(2)}) collective-permute-start(bf16[4,216,128]{2,1,0:T(8,128)(2,1)S(1)} %get-tuple-element.55), channel_id=1, source_target_pairs={{0,2},{1,9},{2,0},{3,11},{4,6},{5,13},{6,4},{7,15},{8,10},{9,1},{1... | collective-permute-start | bytes 663560 | tf_op jit(solution)/shard_map/ppermute | solution.py:689
  31.8 1.9 %collective-permute-start.11 = (bf16[4,216,128]{2,1,0:T(8,128)(2,1)S(1)}, bf16[4,216,128]{2,1,0:T(8,128)(2,1)S(1)}, u32[]{:S(2)}, u32[]{:S(2)}) collective-permute-start(bf16[4,216,128]{2,1,0:T(8,128)(2,1)S(1)} %get-tuple-element.56), channel_id=1, source_target_pairs={{0,4},{1,17},{2,6},{3,19},{4,0},{5,21},{6,2},{7,23},{8,12},{9,25},... | collective-permute-start | bytes 663560 | tf_op jit(solution)/shard_map/ppermute | solution.py:689
  33.7 0.1 collective-permute-start.12
  33.8 2.5 %shard_map.107 = (bf16[5,2,32,128]{3,2,1,0:T(8,128)(2,1)}, bf16[5,2,32,128]{3,2,1,0:T(8,128)(2,1)}) custom-call(f32[5,4,32,128]{3,2,1,0:T(8,128)S(1)} %get-tuple-element.58.tile_ref, bf16[5,4,32,128]{3,2,1,0:T(8,128)(2,1)S(1)} %get-tuple-element.59.act_ref, bf16[5,4,32,128]{3,2,1,0:T(8,128)(2,1)S(1)} %get-tuple-element.52.out_grad_ref, ...), custom_call_target="tpu_custom_call" | custom-call | flops 566231040 | bytes 2000000 | tf_op jit(solution)/shard_map/pallas_call | solution.py:612
  36.3 0.0 collective-permute-done.10.refs_2_
  36.3 3.2 %collective-permute-done.11.refs_1_ = bf16[4,216,128]{2,1,0:T(8,128)(2,1)S(1)} collective-permute-done((bf16[4,216,128]{2,1,0:T(8,128)(2,1)S(1)}, bf16[4,216,128]{2,1,0:T(8,128)(2,1)S(1)}, u32[]{:S(2)}, u32[]{:S(2)}) %collective-permute-start.11) | collective-permute-done | bytes 221216 | tf_op jit(solution)/shard_map/ppermute | solution.py:689
  39.5 1.0 %collective-permute-done.12.refs_0_ = bf16[4,216,128]{2,1,0:T(8,128)(2,1)S(1)} collective-permute-done((bf16[4,216,128]{2,1,0:T(8,128)(2,1)S(1)}, bf16[4,216,128]{2,1,0:T(8,128)(2,1)S(1)}, u32[]{:S(2)}, u32[]{:S(2)}) %collective-permute-start.12) | collective-permute-done | bytes 221216 | tf_op jit(solution)/shard_map/ppermute | solution.py:689
  40.5 0.1 shard_map.108
  40.7 1.5 %collective-permute-start.13 = (bf16[216,128]{1,0:T(8,128)(2,1)S(1)}, bf16[216,128]{1,0:T(8,128)(2,1)S(1)}, u32[]{:S(2)}, u32[]{:S(2)}) collective-permute-start(bf16[216,128]{1,0:T(8,128)(2,1)S(1)} %get-tuple-element.70), channel_id=1, source_target_pairs={{0,24},{1,7},{2,26},{3,5},{4,28},{5,3},{6,30},{7,1},{8,16},{9,15},... | collective-permute-start | bytes 165896 | tf_op jit(solution)/shard_map/ppermute | solution.py:689
  42.2 0.8 %collective-permute-start.14 = (bf16[216,128]{1,0:T(8,128)(2,1)S(1)}, bf16[216,128]{1,0:T(8,128)(2,1)S(1)}, u32[]{:S(2)}, u32[]{:S(2)}) collective-permute-start(bf16[216,128]{1,0:T(8,128)(2,1)S(1)} %get-tuple-element.71), channel_id=1, source_target_pairs={{0,16},{1,5},{2,18},{3,7},{4,20},{5,1},{6,22},{7,3},{8,24},{9,13},... | collective-permute-start | bytes 165896 | tf_op jit(solution)/shard_map/ppermute | solution.py:689
  42.9 2.2 %collective-permute-start.15 = (bf16[216,128]{1,0:T(8,128)(2,1)S(1)}, bf16[216,128]{1,0:T(8,128)(2,1)S(1)}, u32[]{:S(2)}, u32[]{:S(2)}) collective-permute-start(bf16[216,128]{1,0:T(8,128)(2,1)S(1)} %get-tuple-element.72), channel_id=1, source_target_pairs={{0,8},{1,3},{2,10},{3,1},{4,12},{5,7},{6,14},{7,5},{8,0},{9,11},{1... | collective-permute-start | bytes 165896 | tf_op jit(solution)/shard_map/ppermute | solution.py:689
  45.1 1.6 %collective-permute-done.13.refs_0_ = bf16[216,128]{1,0:T(8,128)(2,1)S(1)} collective-permute-done((bf16[216,128]{1,0:T(8,128)(2,1)S(1)}, bf16[216,128]{1,0:T(8,128)(2,1)S(1)}, u32[]{:S(2)}, u32[]{:S(2)}) %collective-permute-start.13) | collective-permute-done | bytes 55328 | tf_op jit(solution)/shard_map/ppermute | solution.py:689
  46.7 0.7 %collective-permute-done.14.refs_1_ = bf16[216,128]{1,0:T(8,128)(2,1)S(1)} collective-permute-done((bf16[216,128]{1,0:T(8,128)(2,1)S(1)}, bf16[216,128]{1,0:T(8,128)(2,1)S(1)}, u32[]{:S(2)}, u32[]{:S(2)}) %collective-permute-start.14) | collective-permute-done | bytes 55328 | tf_op jit(solution)/shard_map/ppermute | solution.py:689
  47.3 0.5 %collective-permute-done.15.refs_2_ = bf16[216,128]{1,0:T(8,128)(2,1)S(1)} collective-permute-done((bf16[216,128]{1,0:T(8,128)(2,1)S(1)}, bf16[216,128]{1,0:T(8,128)(2,1)S(1)}, u32[]{:S(2)}, u32[]{:S(2)}) %collective-permute-start.15) | collective-permute-done | bytes 55328 | tf_op jit(solution)/shard_map/ppermute | solution.py:689
  47.9 0.1 collective-permute-start.16
  48.0 1.3 %collective-permute-done.16 = f32[216,128]{1,0:T(8,128)S(1)} collective-permute-done((f32[216,128]{1,0:T(8,128)S(1)}, f32[216,128]{1,0:T(8,128)S(1)}, u32[]{:S(2)}, u32[]{:S(2)}) %collective-permute-start.16) | collective-permute-done | bytes 110624 | tf_op jit(solution)/shard_map/ppermute | solution.py:677
  49.3 0.7 %broadcast_select_fusion = (f32[216,128]{1,0:T(8,128)}, f32[216,128]{1,0:T(8,128)}) fusion(f32[216,128]{1,0:T(8,128)S(1)} %collective-permute-done.16, f32[216,128]{1,0:T(8,128)S(1)} %shard_map.109, pred[]{:T(512)S(6)} %eq.4), kind=kLoop, calls=%fused_computation | loop fusion | flops 55296 | bytes 442369 | tf_op jit(solution)/shard_map/jit(_where)/select_n | solution.py:712
  (2 shorter events, 0.0 us)
Async XLA Ops:
  3.0 7.9 %collective-permute-start = (bf16[352,128]{1,0:T(8,128)(2,1)}, bf16[352,128]{1,0:T(8,128)(2,1)S(1)}, u32[]{:S(2)}, u32[]{:S(2)}) collective-permute-start(bf16[352,128]{1,0:T(8,128)(2,1)} %get-tuple-element.41), channel_id=1, source_target_pairs={{0,24},{1,7},{2,26},{3,5},{4,28},{5,3},{6,30},{7,1},{8,16},{9,15},... | collective-permute-start | bytes 270344 | tf_op jit(solution)/shard_map/ppermute | solution.py:689
  8.1 5.7 %collective-permute-start.1 = (bf16[352,128]{1,0:T(8,128)(2,1)}, bf16[352,128]{1,0:T(8,128)(2,1)S(1)}, u32[]{:S(2)}, u32[]{:S(2)}) collective-permute-start(bf16[352,128]{1,0:T(8,128)(2,1)} %get-tuple-element.42), channel_id=1, source_target_pairs={{0,16},{1,5},{2,18},{3,7},{4,20},{5,1},{6,22},{7,3},{8,24},{9,13},... | collective-permute-start | bytes 270344 | tf_op jit(solution)/shard_map/ppermute | solution.py:689
  8.1 5.7 %collective-permute-start.2 = (bf16[352,128]{1,0:T(8,128)(2,1)}, bf16[352,128]{1,0:T(8,128)(2,1)S(1)}, u32[]{:S(2)}, u32[]{:S(2)}) collective-permute-start(bf16[352,128]{1,0:T(8,128)(2,1)} %get-tuple-element.43), channel_id=1, source_target_pairs={{0,8},{1,3},{2,10},{3,1},{4,12},{5,7},{6,14},{7,5},{8,0},{9,11},{1... | collective-permute-start | bytes 270344 | tf_op jit(solution)/shard_map/ppermute | solution.py:689
  8.8 0.9 %copy-start = (bf16[352,128]{1,0:T(8,128)(2,1)S(1)}, bf16[352,128]{1,0:T(8,128)(2,1)}, u32[]{:S(2)}) copy-start(bf16[352,128]{1,0:T(8,128)(2,1)} %get-tuple-element.39.refs_0_) | copy-start | bytes 270340
  9.6 0.9 %copy-start.1 = (bf16[1,5,2,32,128]{4,3,2,1,0:T(8,128)(2,1)S(1)}, bf16[1,5,2,32,128]{4,3,2,1,0:T(8,128)(2,1)}, u32[]{:S(2)}) copy-start(bf16[1,5,2,32,128]{4,3,2,1,0:T(8,128)(2,1)} %param.11) | copy-start | bytes 245764
  14.0 6.4 %collective-permute-start.4 = (bf16[1024,128]{1,0:T(8,128)(2,1)S(1)}, bf16[1024,128]{1,0:T(8,128)(2,1)S(1)}, u32[]{:S(2)}, u32[]{:S(2)}) collective-permute-start(bf16[1024,128]{1,0:T(8,128)(2,1)S(1)} %get-tuple-element.47), channel_id=1, source_target_pairs={{0,4},{1,17},{2,6},{3,19},{4,0},{5,21},{6,2},{7,23},{8,12},{9,25},... | collective-permute-start | bytes 786440 | tf_op jit(solution)/shard_map/ppermute | solution.py:689
  15.6 6.5 %collective-permute-start.3 = (bf16[1024,128]{1,0:T(8,128)(2,1)S(1)}, bf16[1024,128]{1,0:T(8,128)(2,1)S(1)}, u32[]{:S(2)}, u32[]{:S(2)}) collective-permute-start(bf16[1024,128]{1,0:T(8,128)(2,1)S(1)} %get-tuple-element.46), channel_id=1, source_target_pairs={{0,2},{1,9},{2,0},{3,11},{4,6},{5,13},{6,4},{7,15},{8,10},{9,1},{1... | collective-permute-start | bytes 786440 | tf_op jit(solution)/shard_map/ppermute | solution.py:689
  17.7 7.3 %collective-permute-start.5 = (bf16[1024,128]{1,0:T(8,128)(2,1)S(1)}, bf16[1024,128]{1,0:T(8,128)(2,1)S(1)}, u32[]{:S(2)}, u32[]{:S(2)}) collective-permute-start(bf16[1024,128]{1,0:T(8,128)(2,1)S(1)} %get-tuple-element.48), channel_id=1, source_target_pairs={{0,6},{1,25},{2,4},{3,27},{4,2},{5,29},{6,0},{7,31},{8,14},{9,17},... | collective-permute-start | bytes 786440 | tf_op jit(solution)/shard_map/ppermute | solution.py:689
  20.4 5.2 %collective-permute-start.6 = (bf16[1344,128]{1,0:T(8,128)(2,1)S(1)}, bf16[1344,128]{1,0:T(8,128)(2,1)S(1)}, u32[]{:S(2)}, u32[]{:S(2)}) collective-permute-start(bf16[1344,128]{1,0:T(8,128)(2,1)S(1)} %get-tuple-element.49.refs_0_), channel_id=1, source_target_pairs={{0,1},{1,0},{2,3},{3,2},{4,5},{5,4},{6,7},{7,6},{8,9},{9,8},{10,11... | collective-permute-start | bytes 1032200 | tf_op jit(solution)/shard_map/ppermute | solution.py:677
  20.4 5.7 %collective-permute-start.8 = (bf16[1024,128]{1,0:T(8,128)(2,1)S(1)}, bf16[1024,128]{1,0:T(8,128)(2,1)S(1)}, u32[]{:S(2)}, u32[]{:S(2)}) collective-permute-start(bf16[1024,128]{1,0:T(8,128)(2,1)S(1)} %collective-permute-done.4.refs_2_), channel_id=1, source_target_pairs={{0,1},{1,0},{2,3},{3,2},{4,5},{5,4},{6,7},{7,6},{8,9},{9,8},{10,11... | collective-permute-start | bytes 786440 | tf_op jit(solution)/shard_map/ppermute | solution.py:677
  22.0 4.1 %collective-permute-start.7 = (bf16[1024,128]{1,0:T(8,128)(2,1)S(1)}, bf16[1024,128]{1,0:T(8,128)(2,1)S(1)}, u32[]{:S(2)}, u32[]{:S(2)}) collective-permute-start(bf16[1024,128]{1,0:T(8,128)(2,1)S(1)} %collective-permute-done.3.refs_1_), channel_id=1, source_target_pairs={{0,1},{1,0},{2,3},{3,2},{4,5},{5,4},{6,7},{7,6},{8,9},{9,8},{10,11... | collective-permute-start | bytes 786440 | tf_op jit(solution)/shard_map/ppermute | solution.py:677
  25.0 1.5 %collective-permute-start.9 = (bf16[1024,128]{1,0:T(8,128)(2,1)S(1)}, bf16[1024,128]{1,0:T(8,128)(2,1)S(1)}, u32[]{:S(2)}, u32[]{:S(2)}) collective-permute-start(bf16[1024,128]{1,0:T(8,128)(2,1)S(1)} %collective-permute-done.5.refs_3_), channel_id=1, source_target_pairs={{0,1},{1,0},{2,3},{3,2},{4,5},{5,4},{6,7},{7,6},{8,9},{9,8},{10,11... | collective-permute-start | bytes 786440 | tf_op jit(solution)/shard_map/ppermute | solution.py:677
  30.3 6.0 %collective-permute-start.10 = (bf16[4,216,128]{2,1,0:T(8,128)(2,1)S(1)}, bf16[4,216,128]{2,1,0:T(8,128)(2,1)S(1)}, u32[]{:S(2)}, u32[]{:S(2)}) collective-permute-start(bf16[4,216,128]{2,1,0:T(8,128)(2,1)S(1)} %get-tuple-element.55), channel_id=1, source_target_pairs={{0,2},{1,9},{2,0},{3,11},{4,6},{5,13},{6,4},{7,15},{8,10},{9,1},{1... | collective-permute-start | bytes 663560 | tf_op jit(solution)/shard_map/ppermute | solution.py:689
  31.8 7.8 %collective-permute-start.11 = (bf16[4,216,128]{2,1,0:T(8,128)(2,1)S(1)}, bf16[4,216,128]{2,1,0:T(8,128)(2,1)S(1)}, u32[]{:S(2)}, u32[]{:S(2)}) collective-permute-start(bf16[4,216,128]{2,1,0:T(8,128)(2,1)S(1)} %get-tuple-element.56), channel_id=1, source_target_pairs={{0,4},{1,17},{2,6},{3,19},{4,0},{5,21},{6,2},{7,23},{8,12},{9,25},... | collective-permute-start | bytes 663560 | tf_op jit(solution)/shard_map/ppermute | solution.py:689
  33.7 6.8 %collective-permute-start.12 = (bf16[4,216,128]{2,1,0:T(8,128)(2,1)S(1)}, bf16[4,216,128]{2,1,0:T(8,128)(2,1)S(1)}, u32[]{:S(2)}, u32[]{:S(2)}) collective-permute-start(bf16[4,216,128]{2,1,0:T(8,128)(2,1)S(1)} %get-tuple-element.57), channel_id=1, source_target_pairs={{0,6},{1,25},{2,4},{3,27},{4,2},{5,29},{6,0},{7,31},{8,14},{9,17},... | collective-permute-start | bytes 663560 | tf_op jit(solution)/shard_map/ppermute | solution.py:689
  40.7 6.0 %collective-permute-start.13 = (bf16[216,128]{1,0:T(8,128)(2,1)S(1)}, bf16[216,128]{1,0:T(8,128)(2,1)S(1)}, u32[]{:S(2)}, u32[]{:S(2)}) collective-permute-start(bf16[216,128]{1,0:T(8,128)(2,1)S(1)} %get-tuple-element.70), channel_id=1, source_target_pairs={{0,24},{1,7},{2,26},{3,5},{4,28},{5,3},{6,30},{7,1},{8,16},{9,15},... | collective-permute-start | bytes 165896 | tf_op jit(solution)/shard_map/ppermute | solution.py:689
  42.2 5.2 %collective-permute-start.14 = (bf16[216,128]{1,0:T(8,128)(2,1)S(1)}, bf16[216,128]{1,0:T(8,128)(2,1)S(1)}, u32[]{:S(2)}, u32[]{:S(2)}) collective-permute-start(bf16[216,128]{1,0:T(8,128)(2,1)S(1)} %get-tuple-element.71), channel_id=1, source_target_pairs={{0,16},{1,5},{2,18},{3,7},{4,20},{5,1},{6,22},{7,3},{8,24},{9,13},... | collective-permute-start | bytes 165896 | tf_op jit(solution)/shard_map/ppermute | solution.py:689
  42.9 4.9 %collective-permute-start.15 = (bf16[216,128]{1,0:T(8,128)(2,1)S(1)}, bf16[216,128]{1,0:T(8,128)(2,1)S(1)}, u32[]{:S(2)}, u32[]{:S(2)}) collective-permute-start(bf16[216,128]{1,0:T(8,128)(2,1)S(1)} %get-tuple-element.72), channel_id=1, source_target_pairs={{0,8},{1,3},{2,10},{3,1},{4,12},{5,7},{6,14},{7,5},{8,0},{9,11},{1... | collective-permute-start | bytes 165896 | tf_op jit(solution)/shard_map/ppermute | solution.py:689
  47.9 1.4 %collective-permute-start.16 = (f32[216,128]{1,0:T(8,128)S(1)}, f32[216,128]{1,0:T(8,128)S(1)}, u32[]{:S(2)}, u32[]{:S(2)}) collective-permute-start(f32[216,128]{1,0:T(8,128)S(1)} %shard_map.109), channel_id=1, source_target_pairs={{0,1},{1,0},{2,3},{3,2},{4,5},{5,4},{6,7},{7,6},{8,9},{9,8},{10,11... | collective-permute-start | bytes 331784 | tf_op jit(solution)/shard_map/ppermute | solution.py:677
